TPU v7x, 32 devices: a whole 2x2x4 slice. The times are simulated.
32 devices in a mesh: dom: 32 (over z, y, x, core).
Axes of the slice: x: 2, y: 2, z: 4, core: 2. Of those that a mesh axis runs over, the one named last changes fastest.
Arguments:
- features: bfloat16 [65536, 512], P('dom'), may hold values from -6 to 6
- weight: bfloat16 [512, 512], replicated, may hold values from -0.25 to 0.25
- cotangent: bfloat16 [65536, 512], P('dom'), may hold values from -6 to 6
- tile_values: bfloat16 [3072, 128, 128], P('dom'), may hold values from -0.21875 to 0.21875
- tile_rows: int32 [3072], P('dom'), may hold values from 0 to 15
- tile_cols: int32 [3072], P('dom'), may hold values from 0 to 18, as said below
- hub_rows: int32 [128], P('dom'), may hold values from 0 to 2047
- send_rows: int32 [32, 32, 8], P('dom'), may hold values from 0 to 2047
- send_count: int32 [32, 32], P('dom'), may hold values from 1 to 8, as said below
Outputs:
- output: bfloat16 [65536, 512], P('dom')
- grad_features: bfloat16 [65536, 512], P('dom')
- grad_weight: float32 [512, 512], replicated
Inputs may be any that keep to these rules, and one draw needn't show every extreme that they name: `tile_cols`: on every device the first 64 tiles name column blocks below 17 and the other 32 name blocks from 17 on. `send_count`: every source sends 8 rows to at least one device.
All inputs are finite; a program needn't handle non-finite values.
Results may differ from a plain program's by a relative error of at most 0.019.
Values may be sent and summed in bfloat16 or wider, within the bound.
No kernel may reach another device: no remote copies, remote signals or barrier semaphores. Data moves between devices by JAX's collectives and lax.ppermute only.
A program may use at most 128 MiB of HBM per device.

v0:
```python
import functools

import jax
import jax.numpy as jnp
from jax import lax
from jax.experimental import pallas as pl
from jax.experimental.pallas import tpu as pltpu
from jax.sharding import PartitionSpec as P

LOC_TILES = 64
LANES = 128
VMEM = pl.BlockSpec(memory_space=pltpu.VMEM)
SMEM = pl.BlockSpec(memory_space=pltpu.SMEM)


def rows_at(block, size):
    return pl.ds(pl.multiple_of(block * size, size), size)


def params(limit):
    return pltpu.CompilerParams(vmem_limit_bytes=limit)


def pack_kernel(n, slots, hubs, send_rows, send_count, hub_rows, feats, out, select):
    rows, width = feats.shape
    chunks = width // LANES
    sub = lax.broadcasted_iota(jnp.int32, (2 * slots, LANES), 0)
    lane = lax.broadcasted_iota(jnp.int32, (2 * slots, LANES), 1)

    def put(at, column):
        for part in range(rows // LANES):
            hit = jnp.where(column == lane + part * LANES, 1.0, 0.0)
            select[rows_at(at, 2 * slots), part * LANES : (part + 1) * LANES] = hit.astype(jnp.bfloat16)

    column = jnp.zeros((2 * slots, LANES), jnp.int32)
    for row in range(hubs * chunks):
        column = jnp.where(sub == row, hub_rows[row % hubs], column)
    put(0, column)

    def pair(q, _):
        column = jnp.full((2 * slots, LANES), -1, jnp.int32)
        for half in range(2):
            dest = 2 * q + half
            count = send_count[0, dest]
            for k in range(slots):
                row = jnp.where(k < count, send_rows[0, dest, k], -1)
                column = jnp.where(sub == half * slots + k, row, column)
        put(q + 1, column)
        return 0

    lax.fori_loop(0, n // 2, pair, 0)
    group = sub // hubs
    found = jnp.dot(select[0 : 2 * slots, :], feats[...], preferred_element_type=jnp.float32)
    hub = jnp.zeros((hubs * chunks, LANES), jnp.float32)
    for c in range(chunks):
        hub = jnp.where(group == c, found[:, c * LANES : (c + 1) * LANES], hub)
    hub = hub.astype(jnp.bfloat16)
    per = 128 // slots

    def many(b, _):
        got = jnp.dot(
            select[pl.ds(pl.multiple_of(b * 128 + 2 * slots, 16), 128), :],
            feats[...],
            preferred_element_type=jnp.float32,
        )
        for s in range(per):
            dest = b * per + s
            out[dest, 0:16, :] = hub
            mine = got[s * slots : (s + 1) * slots, :]
            for c in range(0, chunks, 2):
                both = jnp.concatenate(
                    [mine[:, c * LANES : (c + 1) * LANES], mine[:, (c + 1) * LANES : (c + 2) * LANES]], axis=0
                )
                out[dest, 16 + c * slots : 16 + (c + 2) * slots, :] = both.astype(jnp.bfloat16)
        return 0

    lax.fori_loop(0, n // per, many, 0)


def pack_rows(n, send_rows, send_count, hub_rows, features):
    slots, hubs = send_rows.shape[2], hub_rows.shape[0]
    rows, width = features.shape
    packed = (slots + hubs) * width // LANES
    return pl.pallas_call(
        functools.partial(pack_kernel, n, slots, hubs),
        out_shape=jax.ShapeDtypeStruct((n, packed, LANES), jnp.bfloat16),
        in_specs=[SMEM, SMEM, SMEM, VMEM],
        out_specs=VMEM,
        scratch_shapes=[pltpu.VMEM((n * slots + 2 * slots, rows), jnp.bfloat16)],
        compiler_params=params(16 << 20),
        name="pack_rows",
    )(send_rows, send_count, hub_rows, features)


def near_forward_kernel(count, tile_rows, tile_cols, tiles, feats, total):
    size = tiles.shape[1]
    blocks = feats.shape[0] // size
    total[...] = jnp.zeros_like(total)

    def one(t, _):
        row, col = tile_rows[t], tile_cols[t]

        @pl.when(col < blocks)
        def _():
            total[rows_at(row, size), :] += jnp.dot(
                tiles[t], feats[rows_at(col, size), :], preferred_element_type=jnp.float32
            )

        return 0

    lax.fori_loop(0, count, one, 0)


def near_forward(tile_rows, tile_cols, tiles, features):
    return pl.pallas_call(
        functools.partial(near_forward_kernel, LOC_TILES),
        out_shape=jax.ShapeDtypeStruct(features.shape, jnp.float32),
        in_specs=[SMEM, SMEM, VMEM, VMEM],
        out_specs=VMEM,
        compiler_params=params(16 << 20),
        cost_estimate=pl.CostEstimate(flops=4 << 30, bytes_accessed=8 << 20, transcendentals=0),
        name="near_forward",
    )(tile_rows, tile_cols, tiles, features)


def unpack_slots(n, slots, chunks, packed, into, at):
    def pair(q, _):
        for c in range(0, chunks, 2):
            spot = slice(16 + c * slots, 16 + (c + 2) * slots)
            first = packed[2 * q, spot, :].astype(jnp.float32)
            second = packed[2 * q + 1, spot, :].astype(jnp.float32)
            for half in range(2):
                part = slice(half * slots, (half + 1) * slots)
                both = jnp.concatenate([first[part], second[part]], axis=0).astype(jnp.bfloat16)
                where = pl.ds(pl.multiple_of(at + q * 2 * slots, 2 * slots), 2 * slots)
                into[where, (c + half) * LANES : (c + half + 1) * LANES] = both
        return 0

    lax.fori_loop(0, n // 2, pair, 0)


def forward_kernel(
    n, slots, hubs, tile_rows, tile_cols, parity, tiles, received, near, weight, cotangent,
    output, grad_agg, keep, give, table, total, agg, grad_pre,
):
    size = tiles.shape[1]
    rows, width = near.shape
    chunks = width // LANES
    blocks = rows // size

    def four(q, _):
        parts = [received[4 * q + u, 0:16, :].astype(jnp.float32) for u in range(4)]
        for c in range(chunks):
            quad = jnp.concatenate([part[c * hubs : (c + 1) * hubs] for part in parts], axis=0)
            table[rows_at(q, 16), c * LANES : (c + 1) * LANES] = quad.astype(jnp.bfloat16)
        return 0

    lax.fori_loop(0, n // 4, four, 0)
    unpack_slots(n, slots, chunks, received, table, n * hubs)
    total[...] = near[...]

    def add(t):
        row, col = tile_rows[t], tile_cols[t]
        total[rows_at(row, size), :] += jnp.dot(
            tiles[t], table[rows_at(col - blocks, size), :], preferred_element_type=jnp.float32
        )

    def hub_tile(t, _):
        @pl.when(tile_cols[t] >= blocks)
        def _():
            add(t)

        return 0

    def far_tile(t, _):
        add(t)
        return 0

    lax.fori_loop(0, LOC_TILES, hub_tile, 0)
    lax.fori_loop(LOC_TILES, tiles.shape[0], far_tile, 0)
    step = 256

    def dense(b, _):
        at = rows_at(b, step)
        here = total[at, :].astype(jnp.bfloat16)
        agg[at, :] = here
        pre = jnp.dot(here, weight[...], preferred_element_type=jnp.float32)
        sig = jax.nn.sigmoid(pre)
        output[at, :] = (pre * sig).astype(jnp.bfloat16)
        gp = (cotangent[at, :].astype(jnp.float32) * sig * (1.0 + pre * (1.0 - sig))).astype(jnp.bfloat16)
        grad_pre[at, :] = gp
        grad_agg[at, :] = lax.dot_general(
            gp, weight[...], (((1,), (1,)), ((), ())), preferred_element_type=jnp.float32
        ).astype(jnp.bfloat16)
        return 0

    lax.fori_loop(0, rows // step, dense, 0)
    half = width // 2
    scale = float(rows * n) ** -0.5
    mine = parity[0]
    for h, target in ((mine, keep), (1 - mine, give)):
        term = lax.dot_general(
            agg[:, pl.ds(pl.multiple_of(h * half, half), half)],
            grad_pre[...],
            (((0,), (0,)), ((), ())),
            preferred_element_type=jnp.float32,
        )
        target[...] = (term * scale).astype(target.dtype)


def forward(n, slots, hubs, tile_rows, tile_cols, parity, tiles, received, near, weight, cotangent):
    rows, width = near.shape
    table_rows = n * (slots + hubs)
    shape = jax.ShapeDtypeStruct
    return pl.pallas_call(
        functools.partial(forward_kernel, n, slots, hubs),
        out_shape=(
            shape((rows, width), jnp.bfloat16),
            shape((rows, width), jnp.bfloat16),
            shape((width // 2, width), jnp.float32),
            shape((width // 2, width), jnp.bfloat16),
        ),
        in_specs=[SMEM, SMEM, SMEM] + [VMEM] * 5,
        out_specs=(VMEM,) * 4,
        scratch_shapes=[
            pltpu.VMEM((table_rows, width), jnp.bfloat16),
            pltpu.VMEM((rows, width), jnp.float32),
            pltpu.VMEM((rows, width), jnp.bfloat16),
            pltpu.VMEM((rows, width), jnp.bfloat16),
        ],
        compiler_params=params(32 << 20),
        name="forward",
    )(tile_rows, tile_cols, parity, tiles, received, near, weight, cotangent)


def transposed_product(tile, block):
    return lax.dot_general(tile, block, (((0,), (0,)), ((), ())), preferred_element_type=jnp.float32)


def far_backward_kernel(n, slots, hubs, tile_rows, tile_cols, tiles, grad_agg, out, total):
    size = tiles.shape[1]
    rows, width = grad_agg.shape
    chunks = width // LANES
    blocks = rows // size
    total[...] = jnp.zeros_like(total)

    def add(t):
        row, col = tile_rows[t], tile_cols[t]
        total[rows_at(col - blocks, size), :] += transposed_product(tiles[t], grad_agg[rows_at(row, size), :])

    def hub_tile(t, _):
        @pl.when(tile_cols[t] >= blocks)
        def _():
            add(t)

        return 0

    def far_tile(t, _):
        add(t)
        return 0

    lax.fori_loop(0, LOC_TILES, hub_tile, 0)
    lax.fori_loop(LOC_TILES, tiles.shape[0], far_tile, 0)

    def two(q, _):
        both = total[pl.ds(pl.multiple_of(q * 2 * hubs, 2 * hubs), 2 * hubs), :]
        for u in range(2):
            mine = both[u * hubs : (u + 1) * hubs]
            out[2 * q + u, 0:16, :] = jnp.concatenate(
                [mine[:, c * LANES : (c + 1) * LANES] for c in range(chunks)], axis=0
            ).astype(jnp.bfloat16)
            halo = total[pl.ds(pl.multiple_of(n * hubs + (2 * q + u) * slots, slots), slots), :]
            for c in range(0, chunks, 2):
                pair = jnp.concatenate(
                    [halo[:, c * LANES : (c + 1) * LANES], halo[:, (c + 1) * LANES : (c + 2) * LANES]], axis=0
                )
                out[2 * q + u, 16 + c * slots : 16 + (c + 2) * slots, :] = pair.astype(jnp.bfloat16)
        return 0

    lax.fori_loop(0, n // 2, two, 0)


def far_backward(n, slots, hubs, tile_rows, tile_cols, tiles, grad_agg):
    width = grad_agg.shape[1]
    packed = (slots + hubs) * width // LANES
    return pl.pallas_call(
        functools.partial(far_backward_kernel, n, slots, hubs),
        out_shape=jax.ShapeDtypeStruct((n, packed, LANES), jnp.bfloat16),
        in_specs=[SMEM, SMEM, VMEM, VMEM],
        out_specs=VMEM,
        scratch_shapes=[pltpu.VMEM((n * (slots + hubs), width), jnp.float32)],
        compiler_params=params(16 << 20),
        name="far_backward",
    )(tile_rows, tile_cols, tiles, grad_agg)


def near_backward_kernel(n, slots, hubs, tile_rows, tile_cols, send_rows, send_count, hub_rows, tiles, grad_agg, total, spread):
    size = tiles.shape[1]
    rows, width = grad_agg.shape
    chunks = width // LANES
    blocks = rows // size
    total[...] = jnp.zeros_like(total)

    def one(t, _):
        row, col = tile_rows[t], tile_cols[t]

        @pl.when(col < blocks)
        def _():
            total[rows_at(col, size), :] += transposed_product(tiles[t], grad_agg[rows_at(row, size), :])

        return 0

    lax.fori_loop(0, LOC_TILES, one, 0)
    lane = lax.broadcasted_iota(jnp.int32, (16, LANES), 1)
    sub = lax.broadcasted_iota(jnp.int32, (16, LANES), 0)

    def put(part, targets):
        def rows_of(b, _):
            hit = jnp.where(targets == sub + b * 16, 1.0, 0.0)
            spread[rows_at(b, 16), part * LANES : (part + 1) * LANES] = hit.astype(jnp.bfloat16)
            return 0

        lax.fori_loop(0, rows // 16, rows_of, 0, unroll=4)

    per = LANES // slots
    for part in range(n * slots // LANES):

        def dest(s, targets, part=part):
            count = send_count[0, part * per + s]
            for k in range(slots):
                row = jnp.where(k < count, send_rows[0, part * per + s, k], -1)
                targets = jnp.where(lane == s * slots + k, row, targets)
            return targets

        put(part, lax.fori_loop(0, per, dest, jnp.full((16, LANES), -1, jnp.int32)))
    targets = jnp.full((16, LANES), -1, jnp.int32)
    for at in range(2 * hubs * chunks):
        targets = jnp.where(lane == at, hub_rows[at % hubs], targets)
    put(n * slots // LANES, targets)


def near_backward(n, slots, hubs, tile_rows, tile_cols, send_rows, send_count, hub_rows, tiles, grad_agg):
    rows, width = grad_agg.shape
    return pl.pallas_call(
        functools.partial(near_backward_kernel, n, slots, hubs),
        out_shape=(
            jax.ShapeDtypeStruct((rows, width), jnp.float32),
            jax.ShapeDtypeStruct((rows, n * slots + LANES), jnp.bfloat16),
        ),
        in_specs=[SMEM] * 5 + [VMEM] * 2,
        out_specs=(VMEM, VMEM),
        compiler_params=params(16 << 20),
        cost_estimate=pl.CostEstimate(flops=4 << 30, bytes_accessed=8 << 20, transcendentals=0),
        name="near_backward",
    )(tile_rows, tile_cols, send_rows, send_count, hub_rows, tiles, grad_agg)


def collect_kernel(n, slots, hubs, near, spread, returned, out, table):
    rows, width = near.shape
    chunks = width // LANES
    unpack_slots(n, slots, chunks, returned, table, 0)
    hub = lax.fori_loop(
        0,
        n,
        lambda s, held: held + returned[s, 0:16, :].astype(jnp.float32),
        jnp.zeros((16, LANES), jnp.float32),
        unroll=4,
    )
    group = lax.broadcasted_iota(jnp.int32, (16, LANES), 0) // hubs
    base = n * slots
    table[base : base + LANES, :] = jnp.zeros((LANES, width), jnp.bfloat16)
    upper = hub.astype(jnp.bfloat16).astype(jnp.float32)
    for at, part in ((0, upper), (16, hub - upper)):
        for c in range(chunks):
            table[base + at : base + at + 16, c * LANES : (c + 1) * LANES] = jnp.where(
                group == c, part, 0.0
            ).astype(jnp.bfloat16)

    def block(b, _):
        at = rows_at(b, 256)
        more = jnp.dot(spread[at, :], table[...], preferred_element_type=jnp.float32)
        out[at, :] = (near[at, :] + more).astype(jnp.bfloat16)
        return 0

    lax.fori_loop(0, rows // 256, block, 0)


def collect(n, slots, hubs, near, spread, returned):
    rows, width = near.shape
    return pl.pallas_call(
        functools.partial(collect_kernel, n, slots, hubs),
        out_shape=jax.ShapeDtypeStruct((rows, width), jnp.bfloat16),
        in_specs=[VMEM] * 3,
        out_specs=VMEM,
        scratch_shapes=[pltpu.VMEM((n * slots + LANES, width), jnp.bfloat16)],
        compiler_params=params(16 << 20),
        name="collect",
    )(near, spread, returned)


def swap_cores(x, n):
    return lax.ppermute(x, "dom", [(i, i ^ 1) for i in range(n)])


def exchange(x, groups=None):
    return lax.all_to_all(x, "dom", split_axis=0, concat_axis=0, tiled=True, axis_index_groups=groups)


def per_device(
    features, weight, cotangent, tile_values, tile_rows, tile_cols, hub_rows, send_rows, send_count
):
    n = lax.axis_size("dom")
    slots, hubs = send_rows.shape[2], hub_rows.shape[0]
    width = features.shape[1]
    parity = lax.rem(lax.axis_index("dom"), 2)
    same_core = [[2 * chip + core for chip in range(n // 2)] for core in range(2)]

    packed = pack_rows(n, send_rows, send_count, hub_rows, features)
    received = exchange(packed)
    near = near_forward(tile_rows, tile_cols, tile_values, features)
    output, grad_agg, keep, give = forward(
        n, slots, hubs, tile_rows, tile_cols, parity.reshape(1), tile_values, received, near, weight, cotangent
    )
    half = keep + swap_cores(give, n).astype(jnp.float32)
    share = half.shape[0] // (n // 2)
    terms = exchange(half.astype(jnp.bfloat16).reshape(n // 2, share, width), same_core)

    far = far_backward(n, slots, hubs, tile_rows, tile_cols, tile_values, grad_agg)
    returned = exchange(far)
    near_grad, spread = near_backward(
        n, slots, hubs, tile_rows, tile_cols, send_rows, send_count, hub_rows, tile_values, grad_agg
    )
    summed = jnp.sum(terms.astype(jnp.float32), axis=0).astype(jnp.bfloat16)
    mine = exchange(jnp.broadcast_to(summed, terms.shape), same_core).reshape(half.shape)
    other = swap_cores(mine, n)
    grad_features = collect(n, slots, hubs, near_grad, spread, returned)
    first = jnp.where(parity == 0, mine, other)
    second = jnp.where(parity == 0, other, mine)
    grad_weight = jnp.concatenate([first, second], axis=0).astype(jnp.float32)
    return (output, grad_features, grad_weight)


def solution(mesh):
    placed = (
        P("dom", None),
        P(),
        P("dom", None),
        P("dom", None, None),
        P("dom"),
        P("dom"),
        P("dom"),
        P("dom", None, None),
        P("dom", None),
    )
    return jax.shard_map(
        per_device,
        mesh=mesh,
        in_specs=placed,
        out_specs=(P("dom", None), P("dom", None), P()),
        check_vma=False,
    )
```

profile of v0, /device:TPU:0, one launch (start us, length us, event | category | flops | bytes accessed | tf_op | source)
XLA Modules:
  0.0 128.5 jit_solution(14794145466808030304)
XLA Ops:
  1.6 1.6 %copy-done.8 = bf16[2048,512]{1,0:T(8,128)(2,1)S(1)} copy-done((bf16[2048,512]{1,0:T(8,128)(2,1)S(1)}, bf16[2048,512]{1,0:T(8,128)(2,1)}, u32[]{:S(2)}) %copy-start.8) | copy-done | bytes 2097176
  4.5 2.6 %pack_rows.1 = bf16[32,48,128]{2,1,0:T(8,128)(2,1)S(1)} custom-call(s32[1,32,8]{2,1,0:T(8,128)S(1)} %copy.12.send_rows, s32[1,32]{1,0:T(1,128)S(1)} %copy-done.24, s32[4]{0:T(128)S(1)} %copy-done.26, bf16[2048,512]{1,0:T(8,128)(2,1)S(1)} %copy-done.8), custom_call_target="tpu_custom_call" | custom-call | tf_op jit(solution)/shard_map/pack_rows/pallas_call | solution.py:84
  7.9 7.3 %all-to-all-start = ((bf16[32,48,128]{2,1,0:T(8,128)(2,1)}), bf16[32,48,128]{2,1,0:T(8,128)(2,1)S(1)}, u32[]{:S(2)}, u32[]{:S(2)}) async-start(bf16[32,48,128]{2,1,0:T(8,128)(2,1)} %copy-done.11), calls=%async_computation | async-start | bytes 786432 | tf_op jit(solution)/shard_map/all_to_all | solution.py:406
  15.2 1.6 %copy-done.9 = bf16[2048,512]{1,0:T(8,128)(2,1)S(1)} copy-done((bf16[2048,512]{1,0:T(8,128)(2,1)S(1)}, bf16[2048,512]{1,0:T(8,128)(2,1)}, u32[]{:S(2)}) %copy-start.9) | copy-done | bytes 2097176
  18.1 11.7 %near_forward.1.near = f32[2048,512]{1,0:T(8,128)S(1)} custom-call(s32[96]{0:T(128)S(1)} %copy-done.16, s32[96]{0:T(128)S(1)} %copy-done.20, bf16[96,128,128]{2,1,0:T(8,128)(2,1)S(1)} %copy-done, bf16[2048,512]{1,0:T(8,128)(2,1)S(1)} %copy-done.9), custom_call_target="tpu_custom_call" | custom-call | flops 4294967296 | bytes 8388608 | tf_op jit(solution)/shard_map/near_forward/pallas_call | solution.py:115
  29.8 2.0 %copy-done.1 = f32[2048,512]{1,0:T(8,128)} copy-done((f32[2048,512]{1,0:T(8,128)}, f32[2048,512]{1,0:T(8,128)S(1)}, u32[]{:S(2)}) %copy-start.1) | copy-done | bytes 4194328
  31.7 2.2 %copy-done.2 = f32[2048,512]{1,0:T(8,128)S(1)} copy-done((f32[2048,512]{1,0:T(8,128)S(1)}, f32[2048,512]{1,0:T(8,128)}, u32[]{:S(2)}) %copy-start.2) | copy-done | bytes 4194328
  33.9 1.6 %copy-done.10 = bf16[2048,512]{1,0:T(8,128)(2,1)S(1)} copy-done((bf16[2048,512]{1,0:T(8,128)(2,1)S(1)}, bf16[2048,512]{1,0:T(8,128)(2,1)}, u32[]{:S(2)}) %copy-start.10) | copy-done | bytes 2097176
  37.9 15.2 %forward.1 = (bf16[2048,512]{1,0:T(8,128)(2,1)}, bf16[2048,512]{1,0:T(8,128)(2,1)S(1)}, f32[256,512]{1,0:T(8,128)S(1)}, bf16[256,512]{1,0:T(8,128)(2,1)S(1)}) custom-call(s32[96]{0:T(128)S(1)} %copy-done.17, s32[96]{0:T(128)S(1)} %copy-done.21, s32[1]{0:T(128)} %bitcast.parity, bf16[96,128,128]{2,1,0:T(8,128)(2,1)S(1)} %copy-done, ...), custom_call_target="tpu_custom_call" | custom-call | tf_op jit(solution)/shard_map/forward/pallas_call | solution.py:215
  53.1 1.3 %copy-done.5 = bf16[2048,512]{1,0:T(8,128)(2,1)} copy-done((bf16[2048,512]{1,0:T(8,128)(2,1)}, bf16[2048,512]{1,0:T(8,128)(2,1)S(1)}, u32[]{:S(2)}) %copy-start.5) | copy-done | bytes 2097176
  54.6 1.3 collective-permute-done
  56.0 16.8 %all_to_all.20 = bf16[16,16,512]{2,1,0:T(8,128)(2,1)S(1)} all-to-all(bf16[16,16,512]{2,1,0:T(8,128)(2,1)S(1)} %bitcast.6), channel_id=1, replica_groups={{0,2,4,6,8,10,12,14,16,18,20,22,24,26,28,30},{1,3,5,7,9,11,13,15,17,19,..., dimensions={0} | all-to-all | bytes 524288 | tf_op jit(solution)/shard_map/all_to_all | solution.py:406
  73.6 3.5 %all-to-all-start.3 = ((bf16[16,16,512]{2,1,0:T(8,128)(2,1)}), bf16[16,16,512]{2,1,0:T(8,128)(2,1)S(1)}, u32[]{:S(2)}, u32[]{:S(2)}) async-start(bf16[16,16,512]{2,1,0:T(8,128)(2,1)} %broadcast_in_dim.3), calls=%async_computation.3 | async-start | bytes 524288 | tf_op jit(solution)/shard_map/all_to_all | solution.py:406
  77.2 1.6 %copy-done.6 = bf16[2048,512]{1,0:T(8,128)(2,1)S(1)} copy-done((bf16[2048,512]{1,0:T(8,128)(2,1)S(1)}, bf16[2048,512]{1,0:T(8,128)(2,1)}, u32[]{:S(2)}) %copy-start.6) | copy-done | bytes 2097176
  78.8 9.0 %far_backward.1 = bf16[32,48,128]{2,1,0:T(8,128)(2,1)S(1)} custom-call(s32[96]{0:T(128)S(1)} %copy-done.18, s32[96]{0:T(128)S(1)} %copy-done.22, bf16[96,128,128]{2,1,0:T(8,128)(2,1)S(1)} %copy-done, bf16[2048,512]{1,0:T(8,128)(2,1)S(1)} %copy-done.6), custom_call_target="tpu_custom_call" | custom-call | tf_op jit(solution)/shard_map/far_backward/pallas_call | solution.py:286
  89.3 6.3 %all-to-all-start.1 = ((bf16[32,48,128]{2,1,0:T(8,128)(2,1)}), bf16[32,48,128]{2,1,0:T(8,128)(2,1)S(1)}, u32[]{:S(2)}, u32[]{:S(2)}) async-start(bf16[32,48,128]{2,1,0:T(8,128)(2,1)} %copy-done.12), calls=%async_computation.1 | async-start | bytes 786432 | tf_op jit(solution)/shard_map/all_to_all | solution.py:406
  95.9 1.6 %copy-done.7 = bf16[2048,512]{1,0:T(8,128)(2,1)S(1)} copy-done((bf16[2048,512]{1,0:T(8,128)(2,1)S(1)}, bf16[2048,512]{1,0:T(8,128)(2,1)}, u32[]{:S(2)}) %copy-start.7) | copy-done | bytes 2097176
  100.1 15.7 %near_backward.1 = (f32[2048,512]{1,0:T(8,128)S(1)}, bf16[2048,384]{1,0:T(8,128)(2,1)S(1)}) custom-call(s32[96]{0:T(128)S(1)} %copy-done.19, s32[96]{0:T(128)S(1)} %copy-done.23, s32[1,32,8]{2,1,0:T(8,128)S(1)} %copy.12.send_rows, s32[1,32]{1,0:T(1,128)S(1)} %copy-done.25, s32[4]{0:T(128)S(1)} %copy-done.27, bf16[96,128,128]{2,1,0:T(8,128)(2,1)S(1)} %copy-done, ...), custom_call_target="tpu_custom_call" | custom-call | flops 4294967296 | bytes 8388608 | tf_op jit(solution)/shard_map/near_backward/pallas_call | solution.py:344
  115.8 2.0 %copy-done.3 = f32[2048,512]{1,0:T(8,128)} copy-done((f32[2048,512]{1,0:T(8,128)}, f32[2048,512]{1,0:T(8,128)S(1)}, u32[]{:S(2)}) %copy-start.3) | copy-done | bytes 4194328
  117.7 1.1 copy-done.13
  118.9 2.2 %copy-done.4 = f32[2048,512]{1,0:T(8,128)S(1)} copy-done((f32[2048,512]{1,0:T(8,128)S(1)}, f32[2048,512]{1,0:T(8,128)}, u32[]{:S(2)}) %copy-start.4) | copy-done | bytes 4194328
  121.1 1.4 %copy-done.14 = bf16[2048,384]{1,0:T(8,128)(2,1)S(1)} copy-done((bf16[2048,384]{1,0:T(8,128)(2,1)S(1)}, bf16[2048,384]{1,0:T(8,128)(2,1)}, u32[]{:S(2)}) %copy-start.14) | copy-done | bytes 1572888
  122.5 3.9 %collect.1 = bf16[2048,512]{1,0:T(8,128)(2,1)} custom-call(f32[2048,512]{1,0:T(8,128)S(1)} %copy-done.4, bf16[2048,384]{1,0:T(8,128)(2,1)S(1)} %copy-done.14, bf16[32,48,128]{2,1,0:T(8,128)(2,1)S(1)} %all-to-all-done.1.returned), custom_call_target="tpu_custom_call" | custom-call | tf_op jit(solution)/shard_map/collect/pallas_call | solution.py:390
  127.4 1.1 maximum_convert_fusion
  (59 shorter events, 13.2 us)
Async XLA Ops:
  0.6 14.6 %copy-start = (bf16[96,128,128]{2,1,0:T(8,128)(2,1)S(1)}, bf16[96,128,128]{2,1,0:T(8,128)(2,1)}, u32[]{:S(2)}) copy-start(bf16[96,128,128]{2,1,0:T(8,128)(2,1)} %tiles.7) | copy-start | bytes 9437188
  1.6 1.6 %copy-start.8 = (bf16[2048,512]{1,0:T(8,128)(2,1)S(1)}, bf16[2048,512]{1,0:T(8,128)(2,1)}, u32[]{:S(2)}) copy-start(bf16[2048,512]{1,0:T(8,128)(2,1)} %feats.3) | copy-start | bytes 6291460
  7.1 0.7 copy-start.11
  7.9 23.9 %all-to-all-start = ((bf16[32,48,128]{2,1,0:T(8,128)(2,1)}), bf16[32,48,128]{2,1,0:T(8,128)(2,1)S(1)}, u32[]{:S(2)}, u32[]{:S(2)}) async-start(bf16[32,48,128]{2,1,0:T(8,128)(2,1)} %copy-done.11), calls=%async_computation | async-start | bytes 786432 | tf_op jit(solution)/shard_map/all_to_all | solution.py:406
  15.2 1.6 %copy-start.9 = (bf16[2048,512]{1,0:T(8,128)(2,1)S(1)}, bf16[2048,512]{1,0:T(8,128)(2,1)}, u32[]{:S(2)}) copy-start(bf16[2048,512]{1,0:T(8,128)(2,1)} %feats.3) | copy-start | bytes 6291460
  29.8 2.0 %copy-start.1 = (f32[2048,512]{1,0:T(8,128)}, f32[2048,512]{1,0:T(8,128)S(1)}, u32[]{:S(2)}) copy-start(f32[2048,512]{1,0:T(8,128)S(1)} %near_forward.1.near) | copy-start | bytes 12582916
  31.7 2.2 %copy-start.2 = (f32[2048,512]{1,0:T(8,128)S(1)}, f32[2048,512]{1,0:T(8,128)}, u32[]{:S(2)}) copy-start(f32[2048,512]{1,0:T(8,128)} %copy-done.1) | copy-start | bytes 12582916
  33.9 1.6 %copy-start.10 = (bf16[2048,512]{1,0:T(8,128)(2,1)S(1)}, bf16[2048,512]{1,0:T(8,128)(2,1)}, u32[]{:S(2)}) copy-start(bf16[2048,512]{1,0:T(8,128)(2,1)} %cotangent.1) | copy-start | bytes 6291460
  35.5 1.0 copy-start.15
  53.1 1.3 %copy-start.5 = (bf16[2048,512]{1,0:T(8,128)(2,1)}, bf16[2048,512]{1,0:T(8,128)(2,1)S(1)}, u32[]{:S(2)}) copy-start(bf16[2048,512]{1,0:T(8,128)(2,1)S(1)} %get-tuple-element.10.grad_agg) | copy-start | bytes 6291460
  54.4 22.8 %copy-start.18 = (s32[96]{0:T(128)S(1)}, s32[96]{0:T(128)}, u32[]{:S(2)}) copy-start(s32[96]{0:T(128)} %tile_rows.7) | copy-start | bytes 1156
  54.4 22.8 %copy-start.22 = (s32[96]{0:T(128)S(1)}, s32[96]{0:T(128)}, u32[]{:S(2)}) copy-start(s32[96]{0:T(128)} %tile_cols.7) | copy-start | bytes 1156
  54.4 1.5 %collective-permute-start = (bf16[256,512]{1,0:T(8,128)(2,1)S(1)}, bf16[256,512]{1,0:T(8,128)(2,1)S(1)}, u32[]{:S(2)}, u32[]{:S(2)}) collective-permute-start(bf16[256,512]{1,0:T(8,128)(2,1)S(1)} %get-tuple-element.14), channel_id=1, source_target_pairs={{0,1},{1,0},{2,3},{3,2},{4,5},{5,4},{6,7},{7,6},{8,9},{9,8},{10,11... | collective-permute-start | bytes 786440 | tf_op jit(solution)/shard_map/ppermute | solution.py:402
  73.6 14.9 %all-to-all-start.3 = ((bf16[16,16,512]{2,1,0:T(8,128)(2,1)}), bf16[16,16,512]{2,1,0:T(8,128)(2,1)S(1)}, u32[]{:S(2)}, u32[]{:S(2)}) async-start(bf16[16,16,512]{2,1,0:T(8,128)(2,1)} %broadcast_in_dim.3), calls=%async_computation.3 | async-start | bytes 524288 | tf_op jit(solution)/shard_map/all_to_all | solution.py:406
  77.2 1.6 %copy-start.6 = (bf16[2048,512]{1,0:T(8,128)(2,1)S(1)}, bf16[2048,512]{1,0:T(8,128)(2,1)}, u32[]{:S(2)}) copy-start(bf16[2048,512]{1,0:T(8,128)(2,1)} %copy-done.5) | copy-start | bytes 6291460
  87.8 0.7 copy-start.12
  89.3 29.6 %all-to-all-start.1 = ((bf16[32,48,128]{2,1,0:T(8,128)(2,1)}), bf16[32,48,128]{2,1,0:T(8,128)(2,1)S(1)}, u32[]{:S(2)}, u32[]{:S(2)}) async-start(bf16[32,48,128]{2,1,0:T(8,128)(2,1)} %copy-done.12), calls=%async_computation.1 | async-start | bytes 786432 | tf_op jit(solution)/shard_map/all_to_all | solution.py:406
  95.6 30.8 %collective-permute-start.1 = (bf16[256,512]{1,0:T(8,128)(2,1)}, bf16[256,512]{1,0:T(8,128)(2,1)}, u32[]{:S(2)}, u32[]{:S(2)}) collective-permute-start(bf16[256,512]{1,0:T(8,128)(2,1)} %bitcast.5), channel_id=1, source_target_pairs={{0,1},{1,0},{2,3},{3,2},{4,5},{5,4},{6,7},{7,6},{8,9},{9,8},{10,11... | collective-permute-start | bytes 786440 | tf_op jit(solution)/shard_map/ppermute | solution.py:402
  95.9 1.6 %copy-start.7 = (bf16[2048,512]{1,0:T(8,128)(2,1)S(1)}, bf16[2048,512]{1,0:T(8,128)(2,1)}, u32[]{:S(2)}) copy-start(bf16[2048,512]{1,0:T(8,128)(2,1)} %copy-done.5) | copy-start | bytes 6291460
  115.8 2.0 %copy-start.3 = (f32[2048,512]{1,0:T(8,128)}, f32[2048,512]{1,0:T(8,128)S(1)}, u32[]{:S(2)}) copy-start(f32[2048,512]{1,0:T(8,128)S(1)} %get-tuple-element.11.near) | copy-start | bytes 12582916
  117.7 1.1 copy-start.13
  118.9 2.2 %copy-start.4 = (f32[2048,512]{1,0:T(8,128)S(1)}, f32[2048,512]{1,0:T(8,128)}, u32[]{:S(2)}) copy-start(f32[2048,512]{1,0:T(8,128)} %copy-done.3) | copy-start | bytes 12582916
  121.1 1.4 %copy-start.14 = (bf16[2048,384]{1,0:T(8,128)(2,1)S(1)}, bf16[2048,384]{1,0:T(8,128)(2,1)}, u32[]{:S(2)}) copy-start(bf16[2048,384]{1,0:T(8,128)(2,1)} %copy-done.13) | copy-start | bytes 4718596
  122.5 3.9 %copy-start.29 = (bf16[16,16,512]{2,1,0:T(8,128)(2,1)S(1)}, bf16[16,16,512]{2,1,0:T(8,128)(2,1)}, u32[]{:S(2)}) copy-start(bf16[16,16,512]{2,1,0:T(8,128)(2,1)} %copy-done.28) | copy-start | bytes 786436
  (11 other events, 7.3 us)
where the time goes:
time: 129 us
  Pallas kernels  58 us (45%)
  local copies, waits for them, and re-layouts  31.6 us (24%)
  starting transfers between devices  17.7 us (14%)
  blocking collectives  16.8 us (13%)
  other arithmetic  2.22 us (2%)
  waiting for transfers between devices  1.29 us (1%)
    unnamed x61, local copies, waits for them, and re-layouts  30.9 us
    all_to_all x3, starting transfers between devices, exchange(): lax.all_to_all(x, 'dom', split_axis=0, concat_axis=0, tiled=True, axis_in...  17.1 us
    all_to_all x1, blocking collectives, exchange(): lax.all_to_all(x, 'dom', split_axis=0, concat_axis=0, tiled=True, axis_in...  16.8 us
    pallas_call x1, Pallas kernels, near_backward(): pl.pallas_call(functools.partial(near_backward_kernel, n, slots, hubs), o...  15.7 us
    pallas_call x1, Pallas kernels, forward(): pl.pallas_call(functools.partial(forward_kernel, n, slots, hubs), out_sha...  15.2 us
    pallas_call x1, Pallas kernels, near_forward(): pl.pallas_call(functools.partial(near_forward_kernel, LOC_TILES), out_sha...  11.7 us
    pallas_call x1, Pallas kernels, far_backward(): pl.pallas_call(functools.partial(far_backward_kernel, n, slots, hubs), ou...  8.99 us
    pallas_call x1, Pallas kernels, collect(): pl.pallas_call(functools.partial(collect_kernel, n, slots, hubs), out_sha...  3.91 us
  transfers between devices with their start and end apart: 5, of which 1 were waited for; matrix products, arithmetic and copies ran while one was open for 0% of the time, Pallas kernels for 31%

commit v1 on v0

v1 whole, which is shorter than its diff:
```python
import functools

import jax
import jax.numpy as jnp
from jax import lax
from jax.experimental import pallas as pl
from jax.experimental.pallas import tpu as pltpu
from jax.sharding import PartitionSpec as P

LOC_TILES = 64
LANES = 128
SUBS = 16
NONE = 255
KEYS = 32
LIST = 64
UNROLL = 4
NEAR_FWD, FAR_FWD, NEAR_BWD, FAR_BWD = range(4)
COUNTS = 4 * LIST
PLAN = COUNTS + LANES
VMEM = pl.BlockSpec(memory_space=pltpu.VMEM)
HBM = pl.BlockSpec(memory_space=pltpu.HBM)
DMA = pltpu.SemaphoreType.DMA
BF16, F32, I32 = jnp.bfloat16, jnp.float32, jnp.int32


def rows_at(block, size):
    return pl.ds(pl.multiple_of(block * size, size), size)


def params(limit):
    return pltpu.CompilerParams(vmem_limit_bytes=limit)


def in_hbm(*arrays):
    return [pltpu.with_memory_space_constraint(a, pltpu.HBM) for a in arrays]


def cost(flops, moved):
    return pl.CostEstimate(flops=flops, bytes_accessed=moved, transcendentals=0)


def start(source, target, sem):
    copy = pltpu.make_async_copy(source, target, sem)
    copy.start()
    return copy


def pack_kernel(
    n, slots, hubs, send_rows_in, send_count_in, hub_rows_in, feats_in, out,
    send_rows, send_count, hub_rows, feats, select, staged, sems, out_sems,
):
    rows, width = feats.shape
    chunks = width // LANES
    copies = [
        start(a, b, sems.at[i])
        for i, (a, b) in enumerate(
            (
                (send_rows_in, send_rows),
                (send_count_in, send_count),
                (hub_rows_in, hub_rows),
                (feats_in, feats),
            )
        )
    ]
    sub = lax.broadcasted_iota(I32, (2 * slots, LANES), 0)
    lane = lax.broadcasted_iota(I32, (2 * slots, LANES), 1)
    for copy in copies[:3]:
        copy.wait()

    def put(at, column):
        for part in range(rows // LANES):
            hit = jnp.where(column == lane + part * LANES, 1.0, 0.0)
            select[rows_at(at, 2 * slots), part * LANES : (part + 1) * LANES] = hit.astype(BF16)

    column = jnp.zeros((2 * slots, LANES), I32)
    for row in range(hubs * chunks):
        column = jnp.where(sub == row, hub_rows[row % hubs], column)
    put(0, column)

    def pair(q, _):
        column = jnp.full((2 * slots, LANES), -1, I32)
        for half in range(2):
            dest = 2 * q + half
            count = send_count[0, dest]
            for k in range(slots):
                row = jnp.where(k < count, send_rows[0, k, dest], -1)
                column = jnp.where(sub == half * slots + k, row, column)
        put(q + 1, column)
        return 0

    lax.fori_loop(0, n // 2, pair, 0, unroll=2)
    copies[3].wait()
    group = sub // hubs
    found = jnp.dot(select[0 : 2 * slots, :], feats[...], preferred_element_type=F32)
    hub = jnp.zeros((hubs * chunks, LANES), F32)
    for c in range(chunks):
        hub = jnp.where(group == c, found[:, c * LANES : (c + 1) * LANES], hub)
    hub = hub.astype(BF16)
    per = LANES // slots
    sent = []
    for b in range(n // per):
        got = jnp.dot(
            select[b * LANES + 2 * slots : (b + 1) * LANES + 2 * slots, :], feats[...], preferred_element_type=F32
        )
        for s in range(per):
            dest = b * per + s
            staged[dest, 0:SUBS, :] = hub
            mine = got[s * slots : (s + 1) * slots, :]
            for c in range(0, chunks, 2):
                both = jnp.concatenate(
                    [mine[:, c * LANES : (c + 1) * LANES], mine[:, (c + 1) * LANES : (c + 2) * LANES]], axis=0
                )
                staged[dest, SUBS + c * slots : SUBS + (c + 2) * slots, :] = both.astype(BF16)
        group_of = pl.ds(b * per, per)
        sent.append(start(staged.at[group_of], out.at[group_of], out_sems.at[b]))
    for copy in sent:
        copy.wait()


def pack_rows(n, send_rows, send_count, hub_rows, features):
    slots, hubs = send_rows.shape[1], hub_rows.shape[0]
    rows, width = features.shape
    packed = (n, (slots + hubs) * width // LANES, LANES)
    return pl.pallas_call(
        functools.partial(pack_kernel, n, slots, hubs),
        out_shape=pltpu.HBM(packed, BF16),
        in_specs=[HBM] * 4,
        out_specs=HBM,
        scratch_shapes=[
            pltpu.SMEM(send_rows.shape, I32),
            pltpu.SMEM(send_count.shape, I32),
            pltpu.SMEM(hub_rows.shape, I32),
            pltpu.VMEM((rows, width), BF16),
            pltpu.VMEM((n * slots + 2 * slots, rows), BF16),
            pltpu.VMEM(packed, BF16),
            DMA((4,)),
            DMA((n * slots // LANES,)),
        ],
        compiler_params=params(16 << 20),
        name="pack_rows",
    )(*in_hbm(send_rows, send_count, hub_rows, features))


def make_plan(tile_rows, tile_cols, blocks, plan, waiting):
    def clear(i, _):
        waiting[i] = NONE
        return 0

    lax.fori_loop(0, 4 * KEYS, clear, 0, unroll=8)
    for kind in range(4):
        plan[COUNTS + kind] = 0

    def add(kind, key, t):
        slot = kind * KEYS + key
        first, count = waiting[slot], plan[COUNTS + kind]
        pair = first != NONE
        plan[kind * LIST + count] = (key << 16) | (first << 8) | t
        plan[COUNTS + kind] = count + pair.astype(I32)
        waiting[slot] = jnp.where(pair, NONE, t)

    def tile(t, _):
        row, col = tile_rows[t], tile_cols[t]
        far = (col >= blocks).astype(I32)
        add(NEAR_FWD + far, row, t)
        add(NEAR_BWD + far, col - blocks * far, t)
        return 0

    lax.fori_loop(0, tile_rows.shape[0], tile, 0)
    for kind in range(4):

        def left(key, count, kind=kind):
            first = waiting[kind * KEYS + key]
            plan[kind * LIST + count] = (key << 16) | (first << 8) | NONE
            return count + (first != NONE).astype(I32)

        count = lax.fori_loop(0, KEYS, left, plan[COUNTS + kind])
        plan[COUNTS + kind] = count
        for u in range(UNROLL):
            plan[kind * LIST + count + u] = (NONE << 8) | NONE


def run_plan(kind, plan, tiles, source_of, source, total, transposed):
    size, last = tiles.shape[1], tiles.shape[0] - 1
    axis = 0 if transposed else 1

    def group(g, _):
        for u in range(UNROLL):
            word = plan[kind * LIST + g * UNROLL + u]
            key, picks = word >> 16, ((word >> 8) & 255, word & 255)
            left, right = [], []
            for pick in picks:
                t = jnp.minimum(pick, last)
                left.append(jnp.where(pick == NONE, jnp.zeros((size, size), BF16), tiles[t]))
                right.append(source[rows_at(source_of(t), size), :])
            total[rows_at(key, size), :] += lax.dot_general(
                jnp.concatenate(left, axis=axis),
                jnp.concatenate(right, axis=0),
                (((axis,), (0,)), ((), ())),
                preferred_element_type=F32,
            )
        return 0

    lax.fori_loop(0, (plan[COUNTS + kind] + UNROLL - 1) // UNROLL, group, 0)


def near_forward_kernel(
    tile_rows_in, tile_cols_in, tiles, feats_in, near_out, plan_out,
    tile_rows, tile_cols, feats, total, plan, waiting, sems,
):
    rows, width = feats.shape
    blocks = rows // tiles.shape[1]
    copies = [
        start(a, b, sems.at[i])
        for i, (a, b) in enumerate(((tile_rows_in, tile_rows), (tile_cols_in, tile_cols), (feats_in, feats)))
    ]
    total[...] = jnp.zeros_like(total)
    copies[0].wait()
    copies[1].wait()
    make_plan(tile_rows, tile_cols, blocks, plan, waiting)
    sent = start(plan, plan_out, sems.at[0])
    copies[2].wait()
    run_plan(NEAR_FWD, plan, tiles, lambda t: jnp.minimum(tile_cols[t], blocks - 1), feats, total, False)
    last = start(total, near_out, sems.at[1])
    sent.wait()
    last.wait()


def near_forward(tile_rows, tile_cols, tiles, features):
    rows, width = features.shape
    return pl.pallas_call(
        near_forward_kernel,
        out_shape=(pltpu.HBM((rows, width), F32), pltpu.HBM((PLAN,), I32)),
        in_specs=[HBM, HBM, VMEM, HBM],
        out_specs=(HBM, HBM),
        scratch_shapes=[
            pltpu.SMEM(tile_rows.shape, I32),
            pltpu.SMEM(tile_cols.shape, I32),
            pltpu.VMEM((rows, width), BF16),
            pltpu.VMEM((rows, width), F32),
            pltpu.SMEM((PLAN,), I32),
            pltpu.SMEM((4 * KEYS,), I32),
            DMA((3,)),
        ],
        compiler_params=params(12 << 20),
        cost_estimate=cost(4 << 30, 8 << 20),
        name="near_forward",
    )(*in_hbm(tile_rows, tile_cols), tiles, *in_hbm(features))


def unpack_slots(n, slots, chunks, packed, into, at):
    def pair(q, _):
        for c in range(0, chunks, 2):
            spot = slice(SUBS + c * slots, SUBS + (c + 2) * slots)
            first = packed[2 * q, spot, :].astype(F32)
            second = packed[2 * q + 1, spot, :].astype(F32)
            for half in range(2):
                part = slice(half * slots, (half + 1) * slots)
                both = jnp.concatenate([first[part], second[part]], axis=0).astype(BF16)
                where = pl.ds(pl.multiple_of(at + q * 2 * slots, 2 * slots), 2 * slots)
                into[where, (c + half) * LANES : (c + half + 1) * LANES] = both
        return 0

    lax.fori_loop(0, n // 2, pair, 0, unroll=4)


def reversed_bits(value, bits):
    out = jnp.zeros((), I32)
    for bit in range(bits):
        out = out | (((value >> bit) & 1) << (bits - 1 - bit))
    return out


def halvings(n, width):
    steps = 0
    while 2 << steps <= n and width >> (steps + 1) >= SUBS:
        steps += 1
    return steps


def forward_kernel(
    n, slots, hubs, tile_rows_in, tile_cols_in, plan_in, tiles, received, near_in, weight_in, cot_in,
    output, grad_pre_out, keep, give,
    tile_rows, tile_cols, plan, table, total, near, weight, cot, agg, grad_pre, out, sems, near_sems, cot_sems, out_sems, gp_sems,
):
    size = tiles.shape[1]
    rows, width = near.shape
    chunks = width // LANES
    blocks = rows // size
    step = 256
    steps = rows // step
    index = [
        start(a, b, sems.at[i])
        for i, (a, b) in enumerate(((plan_in, plan), (tile_rows_in, tile_rows), (tile_cols_in, tile_cols)))
    ]
    weight_copy = start(weight_in, weight, sems.at[3])
    pieces = [pl.ds(b * step, step) for b in range(steps)]
    near_copies = [start(near_in.at[at], near.at[at], near_sems.at[b]) for b, at in enumerate(pieces)]
    cot_copies = [start(cot_in.at[at], cot.at[at], cot_sems.at[b]) for b, at in enumerate(pieces)]
    total[...] = jnp.zeros_like(total)

    def four(q, _):
        parts = [received[4 * q + u, 0:SUBS, :].astype(F32) for u in range(4)]
        for c in range(chunks):
            quad = jnp.concatenate([part[c * hubs : (c + 1) * hubs] for part in parts], axis=0)
            table[rows_at(q, SUBS), c * LANES : (c + 1) * LANES] = quad.astype(BF16)
        return 0

    lax.fori_loop(0, n // 4, four, 0, unroll=2)
    unpack_slots(n, slots, chunks, received, table, n * hubs)
    for copy in index:
        copy.wait()
    run_plan(FAR_FWD, plan, tiles, lambda t: jnp.maximum(tile_cols[t] - blocks, 0), table, total, False)
    weight_copy.wait()
    sent = []
    for b, at in enumerate(pieces):
        near_copies[b].wait()
        cot_copies[b].wait()
        here = (total[at, :] + near[at, :]).astype(BF16)
        agg[at, :] = here
        pre = jnp.dot(here, weight[...], preferred_element_type=F32)
        sig = jax.nn.sigmoid(pre)
        out[at, :] = (pre * sig).astype(BF16)
        grad_pre[at, :] = (cot[at, :].astype(F32) * sig * (1.0 + pre * (1.0 - sig))).astype(BF16)
        sent.append(start(out.at[at], output.at[at], out_sems.at[b]))
        sent.append(start(grad_pre.at[at], grad_pre_out.at[at], gp_sems.at[b]))
    scale = float(rows * n) ** -0.5
    term = total.at[pl.ds(0, width)]
    for c in range(0, width, 256):
        term[c : c + 256, :] = (
            lax.dot_general(
                agg[:, c : c + 256], grad_pre[...], (((0,), (0,)), ((), ())), preferred_element_type=F32
            )
            * scale
        )
    bits = halvings(n, width)
    unit = width >> bits
    mine = reversed_bits(lax.axis_index("dom"), bits)
    half = 1 << (bits - 1)
    for b in range(half):
        spot = slice(b * unit, (b + 1) * unit)
        keep[spot, :] = term[rows_at(mine ^ b, unit), :]
        give[spot, :] = term[rows_at(mine ^ (b + half), unit), :].astype(BF16)
    for copy in sent:
        copy.wait()


def forward(n, slots, hubs, tile_rows, tile_cols, plan, tiles, received, near, weight, cotangent):
    rows, width = near.shape
    steps = rows // 256
    shape = jax.ShapeDtypeStruct
    return pl.pallas_call(
        functools.partial(forward_kernel, n, slots, hubs),
        out_shape=(
            pltpu.HBM((rows, width), BF16),
            pltpu.HBM((rows, width), BF16),
            shape((width // 2, width), F32),
            shape((width // 2, width), BF16),
        ),
        in_specs=[HBM, HBM, HBM, VMEM, VMEM, HBM, HBM, HBM],
        out_specs=(HBM, HBM, VMEM, VMEM),
        scratch_shapes=[
            pltpu.SMEM(tile_rows.shape, I32),
            pltpu.SMEM(tile_cols.shape, I32),
            pltpu.SMEM((PLAN,), I32),
            pltpu.VMEM((n * (slots + hubs), width), BF16),
            pltpu.VMEM((rows, width), F32),
            pltpu.VMEM((rows, width), F32),
            pltpu.VMEM((width, width), BF16),
            pltpu.VMEM((rows, width), BF16),
            pltpu.VMEM((rows, width), BF16),
            pltpu.VMEM((rows, width), BF16),
            pltpu.VMEM((rows, width), BF16),
            DMA((4,)),
            DMA((steps,)),
            DMA((steps,)),
            DMA((steps,)),
            DMA((steps,)),
        ],
        compiler_params=params(28 << 20),
        cost_estimate=cost(8 << 30, 16 << 20),
        name="forward",
    )(*in_hbm(tile_rows, tile_cols, plan), tiles, received, *in_hbm(near, weight, cotangent))


def far_backward_kernel(
    n, slots, hubs, tile_rows_in, plan_in, tiles, grad_pre_in, weight_in, out, grad_agg_out,
    tile_rows, plan, grad_pre, weight, grad_agg, total, staged, sems, in_sems, out_sems,
):
    rows, width = grad_pre.shape
    chunks = width // LANES
    step = 512
    pieces = [pl.ds(at, step) for at in range(0, rows, step)]
    weight_copy = start(weight_in, weight, sems.at[0])
    copies = [start(grad_pre_in.at[at], grad_pre.at[at], in_sems.at[b]) for b, at in enumerate(pieces)]
    index = [start(plan_in, plan, sems.at[1]), start(tile_rows_in, tile_rows, sems.at[2])]
    total[...] = jnp.zeros_like(total)
    weight_copy.wait()
    sent = []
    for b, at in enumerate(pieces):
        copies[b].wait()
        grad_agg[at, :] = lax.dot_general(
            grad_pre[at, :], weight[...], (((1,), (1,)), ((), ())), preferred_element_type=F32
        ).astype(BF16)
        sent.append(start(grad_agg.at[at], grad_agg_out.at[at], out_sems.at[b]))
    for copy in index:
        copy.wait()
    run_plan(FAR_BWD, plan, tiles, lambda t: tile_rows[t], grad_agg, total, True)

    def two(q, _):
        both = total[rows_at(q, 2 * hubs), :]
        for u in range(2):
            mine = both[u * hubs : (u + 1) * hubs]
            staged[2 * q + u, 0:SUBS, :] = jnp.concatenate(
                [mine[:, c * LANES : (c + 1) * LANES] for c in range(chunks)], axis=0
            ).astype(BF16)
            halo = total[pl.ds(pl.multiple_of(n * hubs + (2 * q + u) * slots, slots), slots), :]
            for c in range(0, chunks, 2):
                pair = jnp.concatenate(
                    [halo[:, c * LANES : (c + 1) * LANES], halo[:, (c + 1) * LANES : (c + 2) * LANES]], axis=0
                )
                staged[2 * q + u, SUBS + c * slots : SUBS + (c + 2) * slots, :] = pair.astype(BF16)
        return 0

    lax.fori_loop(0, n // 2, two, 0, unroll=2)
    sent.append(start(staged, out, sems.at[0]))
    for copy in sent:
        copy.wait()


def far_backward(n, slots, hubs, tile_rows, plan, tiles, grad_pre, weight):
    rows, width = grad_pre.shape
    packed = (n, (slots + hubs) * width // LANES, LANES)
    return pl.pallas_call(
        functools.partial(far_backward_kernel, n, slots, hubs),
        out_shape=(pltpu.HBM(packed, BF16), pltpu.HBM((rows, width), BF16)),
        in_specs=[HBM, HBM, VMEM, HBM, HBM],
        out_specs=(HBM, HBM),
        scratch_shapes=[
            pltpu.SMEM(tile_rows.shape, I32),
            pltpu.SMEM((PLAN,), I32),
            pltpu.VMEM((rows, width), BF16),
            pltpu.VMEM((width, width), BF16),
            pltpu.VMEM((rows, width), BF16),
            pltpu.VMEM((n * (slots + hubs), width), F32),
            pltpu.VMEM(packed, BF16),
            DMA((3,)),
            DMA((rows // 512,)),
            DMA((rows // 512,)),
        ],
        compiler_params=params(16 << 20),
        cost_estimate=cost(4 << 30, 8 << 20),
        name="far_backward",
    )(*in_hbm(tile_rows, plan), tiles, *in_hbm(grad_pre, weight))


def near_backward_kernel(
    n, slots, hubs, tile_rows_in, plan_in, send_rows_in, send_count_in, hub_rows_in, tiles, grad_agg_in, total_out, spread_out,
    tile_rows, plan, send_rows, send_count, hub_rows, grad_agg, total, spread, sems,
):
    rows, width = grad_agg.shape
    chunks = width // LANES
    copies = [
        start(a, b, sems.at[i])
        for i, (a, b) in enumerate(
            (
                (tile_rows_in, tile_rows),
                (plan_in, plan),
                (send_rows_in, send_rows),
                (send_count_in, send_count),
                (hub_rows_in, hub_rows),
                (grad_agg_in, grad_agg),
            )
        )
    ]
    total[...] = jnp.zeros_like(total)
    for copy in copies:
        copy.wait()
    run_plan(NEAR_BWD, plan, tiles, lambda t: tile_rows[t], grad_agg, total, True)
    sent = start(total, total_out, sems.at[0])
    lane = lax.broadcasted_iota(I32, (SUBS, LANES), 1)
    sub = lax.broadcasted_iota(I32, (SUBS, LANES), 0)

    def put(part, targets):
        def rows_of(b, _):
            hit = jnp.where(targets == sub + b * SUBS, 1.0, 0.0)
            spread[rows_at(b, SUBS), part * LANES : (part + 1) * LANES] = hit.astype(BF16)
            return 0

        lax.fori_loop(0, rows // SUBS, rows_of, 0, unroll=8)

    per = LANES // slots
    for part in range(n * slots // LANES):

        def dest(s, targets, part=part):
            count = send_count[0, part * per + s]
            for k in range(slots):
                row = jnp.where(k < count, send_rows[0, k, part * per + s], -1)
                targets = jnp.where(lane == s * slots + k, row, targets)
            return targets

        put(part, lax.fori_loop(0, per, dest, jnp.full((SUBS, LANES), -1, I32)))
    targets = jnp.full((SUBS, LANES), -1, I32)
    for at in range(2 * hubs * chunks):
        targets = jnp.where(lane == at, hub_rows[at % hubs], targets)
    put(n * slots // LANES, targets)
    last = start(spread, spread_out, sems.at[1])
    sent.wait()
    last.wait()


def near_backward(n, slots, hubs, tile_rows, plan, send_rows, send_count, hub_rows, tiles, grad_agg):
    rows, width = grad_agg.shape
    table = n * slots + LANES
    return pl.pallas_call(
        functools.partial(near_backward_kernel, n, slots, hubs),
        out_shape=(pltpu.HBM((rows, width), F32), pltpu.HBM((rows, table), BF16)),
        in_specs=[HBM] * 5 + [VMEM, HBM],
        out_specs=(HBM, HBM),
        scratch_shapes=[
            pltpu.SMEM(tile_rows.shape, I32),
            pltpu.SMEM((PLAN,), I32),
            pltpu.SMEM(send_rows.shape, I32),
            pltpu.SMEM(send_count.shape, I32),
            pltpu.SMEM(hub_rows.shape, I32),
            pltpu.VMEM((rows, width), BF16),
            pltpu.VMEM((rows, width), F32),
            pltpu.VMEM((rows, table), BF16),
            DMA((6,)),
        ],
        compiler_params=params(20 << 20),
        cost_estimate=cost(4 << 30, 8 << 20),
        name="near_backward",
    )(*in_hbm(tile_rows, plan, send_rows, send_count, hub_rows), tiles, *in_hbm(grad_agg))


def collect_kernel(n, slots, hubs, near_in, spread_in, returned, out, near, spread, table, staged, near_sems, spread_sems, out_sems):
    rows, width = near.shape
    chunks = width // LANES
    step = 256
    pieces = [pl.ds(at, step) for at in range(0, rows, step)]
    copies = []
    for b, at in enumerate(pieces):
        copies.append(start(spread_in.at[at], spread.at[at], spread_sems.at[b]))
        copies.append(start(near_in.at[at], near.at[at], near_sems.at[b]))
    unpack_slots(n, slots, chunks, returned, table, 0)
    hub = lax.fori_loop(
        0, n, lambda s, held: held + returned[s, 0:SUBS, :].astype(F32), jnp.zeros((SUBS, LANES), F32), unroll=8
    )
    group = lax.broadcasted_iota(I32, (SUBS, LANES), 0) // hubs
    base = n * slots
    table[base : base + LANES, :] = jnp.zeros((LANES, width), BF16)
    upper = hub.astype(BF16).astype(F32)
    for at, part in ((0, upper), (SUBS, hub - upper)):
        for c in range(chunks):
            table[base + at : base + at + SUBS, c * LANES : (c + 1) * LANES] = jnp.where(
                group == c, part, 0.0
            ).astype(BF16)
    sent = []
    for b, at in enumerate(pieces):
        copies[2 * b].wait()
        more = jnp.dot(spread[at, :], table[...], preferred_element_type=F32)
        copies[2 * b + 1].wait()
        staged[at, :] = (near[at, :] + more).astype(BF16)
        sent.append(start(staged.at[at], out.at[at], out_sems.at[b]))
    for copy in sent:
        copy.wait()


def collect(n, slots, hubs, near, spread, returned):
    rows, width = near.shape
    table = n * slots + LANES
    steps = rows // 256
    return pl.pallas_call(
        functools.partial(collect_kernel, n, slots, hubs),
        out_shape=pltpu.HBM((rows, width), BF16),
        in_specs=[HBM, HBM, VMEM],
        out_specs=HBM,
        scratch_shapes=[
            pltpu.VMEM((rows, width), F32),
            pltpu.VMEM((rows, table), BF16),
            pltpu.VMEM((table, width), BF16),
            pltpu.VMEM((rows, width), BF16),
            DMA((steps,)),
            DMA((steps,)),
            DMA((steps,)),
        ],
        compiler_params=params(20 << 20),
        cost_estimate=cost(2 << 30, 8 << 20),
        name="collect",
    )(*in_hbm(near, spread), returned)


def order_kernel(bits, first, second, out):
    width = out.shape[0]
    unit = width >> bits
    half = 1 << (bits - 1)
    mine = reversed_bits(lax.axis_index("dom"), bits)
    for b in range(half):
        spot = slice(b * unit, (b + 1) * unit)
        out[rows_at(mine ^ b, unit), :] = first[spot, :].astype(F32)
        out[rows_at(mine ^ (b + half), unit), :] = second[spot, :].astype(F32)


def exchange(x, n, bit):
    return lax.ppermute(x, "dom", [(i, i ^ (1 << bit)) for i in range(n)])


def sum_weight(n, keep, give):
    width = keep.shape[1]
    bits = halvings(n, width)
    for bit in range(bits):
        keep = keep + exchange(give, n, bit).astype(F32)
        if bit + 1 < bits:
            half = keep.shape[0] // 2
            keep, give = keep[:half], keep[half:].astype(BF16)
    for bit in range(bits, n.bit_length() - 1):
        keep = keep + exchange(keep.astype(BF16), n, bit).astype(F32)
    held = keep.astype(BF16)
    for bit in reversed(range(1, bits)):
        held = jnp.concatenate([held, exchange(held, n, bit)], axis=0)
    return pl.pallas_call(
        functools.partial(order_kernel, bits),
        out_shape=jax.ShapeDtypeStruct((width, width), F32),
        in_specs=[VMEM, VMEM],
        out_specs=VMEM,
        compiler_params=params(4 << 20),
        name="order",
    )(held, exchange(held, n, 0))


def all_to_all(x):
    return lax.all_to_all(x, "dom", split_axis=0, concat_axis=0, tiled=True)


def per_device(
    features, weight, cotangent, tile_values, tile_rows, tile_cols, hub_rows, send_rows, send_count
):
    n = lax.axis_size("dom")
    slots, hubs = send_rows.shape[2], hub_rows.shape[0]
    send_rows = jnp.swapaxes(send_rows, 1, 2)

    packed = pack_rows(n, send_rows, send_count, hub_rows, features)
    received = all_to_all(packed)
    near, plan = near_forward(tile_rows, tile_cols, tile_values, features)
    output, grad_pre, keep, give = forward(
        n, slots, hubs, tile_rows, tile_cols, plan, tile_values, received, near, weight, cotangent
    )
    far, grad_agg = far_backward(n, slots, hubs, tile_rows, plan, tile_values, grad_pre, weight)
    returned = all_to_all(far)
    near_grad, spread = near_backward(
        n, slots, hubs, tile_rows, plan, send_rows, send_count, hub_rows, tile_values, grad_agg
    )
    grad_features = collect(n, slots, hubs, near_grad, spread, returned)
    grad_weight = sum_weight(n, keep, give)
    return (output, grad_features, grad_weight)


def solution(mesh):
    placed = (
        P("dom", None),
        P(),
        P("dom", None),
        P("dom", None, None),
        P("dom"),
        P("dom"),
        P("dom"),
        P("dom", None, None),
        P("dom", None),
    )
    return jax.shard_map(
        per_device,
        mesh=mesh,
        in_specs=placed,
        out_specs=(P("dom", None), P("dom", None), P()),
        check_vma=False,
    )
```

time: 129 us -> 95 us (0.74)
  waiting for transfers between devices: 1.29 us -> 32.7 us
  local copies, waits for them, and re-layouts: 31.6 us -> 1.96 us
  Pallas kernels: 58 us -> 38.6 us
  blocking collectives: 16.8 us -> 0 us
  starting transfers between devices: 17.7 us -> 19.9 us
  other arithmetic: 2.22 us -> 0.15 us
    unnamed x61 -> x9, local copies, waits for them, and re-layouts: 30.9 us -> 1.91 us
    ppermute x2 -> x10, waiting for transfers between devices: 1.29 us -> 28.5 us  [exchange(): return lax.ppermute(x, 'dom', [(i, i ^ 1 << bit) for i in range(n)])]
    all_to_all x1 -> x0, blocking collectives: 16.8 us -> none  [exchange(): lax.all_to_all(x, 'dom', split_axis=0, concat_axis=0, tiled=True, axis_in...]
    ppermute x2 -> x10, starting transfers between devices: 0.57 us -> 10 us  [exchange(): return lax.ppermute(x, 'dom', [(i, i ^ 1 << bit) for i in range(n)])]
    pallas_call x1, Pallas kernels: 15.7 us -> 6.83 us  [near_backward(): pl.pallas_call(functools.partial(near_backward_kernel, n, slots, hubs), o...]
    pallas_call x1, Pallas kernels: 15.2 us -> 7.69 us  [forward(): pl.pallas_call(functools.partial(forward_kernel, n, slots, hubs), out_sha...]
    all_to_all x3 -> x2, starting transfers between devices: 17.1 us -> 9.92 us  [all_to_all(): return lax.all_to_all(x, 'dom', split_axis=0, concat_axis=0, tiled=True)]
    all_to_all x3 -> x2, waiting for transfers between devices: 0.01 us -> 4.21 us  [all_to_all(): return lax.all_to_all(x, 'dom', split_axis=0, concat_axis=0, tiled=True)]
  transfers between devices with their start and end apart: 5 -> 12, of which waited for: 1 -> 9; matrix products, arithmetic and copies ran while one was open for 0% -> 0% of each run, Pallas kernels for 31% -> 28%
where the time goes in v1:
time: 95 us; the launch traced here: 94.2 us
  Pallas kernels  38.6 us (41%)
  waiting for transfers between devices  32.7 us (34%)
  starting transfers between devices  19.9 us (21%)
  local copies, waits for them, and re-layouts  1.96 us (2%)
    ppermute x10, waiting for transfers between devices, exchange(): return lax.ppermute(x, 'dom', [(i, i ^ 1 << bit) for i in range(n)])  28.5 us
    ppermute x10, starting transfers between devices, exchange(): return lax.ppermute(x, 'dom', [(i, i ^ 1 << bit) for i in range(n)])  10 us
    all_to_all x2, starting transfers between devices, all_to_all(): return lax.all_to_all(x, 'dom', split_axis=0, concat_axis=0, tiled=True)  9.92 us
    pallas_call x1, Pallas kernels, near_forward(): pl.pallas_call(near_forward_kernel, out_shape=(pltpu.HBM((rows, width), F...  8.95 us
    pallas_call x1, Pallas kernels, forward(): pl.pallas_call(functools.partial(forward_kernel, n, slots, hubs), out_sha...  7.69 us
    pallas_call x1, Pallas kernels, near_backward(): pl.pallas_call(functools.partial(near_backward_kernel, n, slots, hubs), o...  6.83 us
    pallas_call x1, Pallas kernels, far_backward(): pl.pallas_call(functools.partial(far_backward_kernel, n, slots, hubs), ou...  6.12 us
    pallas_call x1, Pallas kernels, collect(): pl.pallas_call(functools.partial(collect_kernel, n, slots, hubs), out_sha...  4.55 us
  transfers between devices with their start and end apart: 12, of which 9 were waited for; matrix products, arithmetic and copies ran while one was open for 0% of the time, Pallas kernels for 28%

profile of v1, /device:TPU:0, one launch (start us, length us, event | category | flops | bytes accessed | tf_op | source)
XLA Modules:
  0.0 94.2 jit_solution(6262227884081991862)
XLA Ops:
  0.6 3.5 %pack_rows.1 = bf16[32,48,128]{2,1,0:T(8,128)(2,1)} custom-call(s32[1,8,32]{2,1,0:T(8,128)} %bitcast.1, s32[1,32]{1,0:T(1,128)} %send_count_in.3, s32[4]{0:T(128)} %hub_rows_in.3, bf16[2048,512]{1,0:T(8,128)(2,1)} %feats_in.3), custom_call_target="tpu_custom_call" | custom-call | tf_op jit(solution)/shard_map/pack_rows/pallas_call | solution.py:124
  4.1 7.3 %all-to-all-start = ((bf16[32,48,128]{2,1,0:T(8,128)(2,1)}), bf16[32,48,128]{2,1,0:T(8,128)(2,1)S(1)}, u32[]{:S(2)}, u32[]{:S(2)}) async-start(bf16[32,48,128]{2,1,0:T(8,128)(2,1)} %pack_rows.1), calls=%async_computation | async-start | bytes 786432 | tf_op jit(solution)/shard_map/all_to_all | solution.py:632
  11.4 9.0 %near_forward.1 = (f32[2048,512]{1,0:T(8,128)}, s32[384]{0:T(512)}) custom-call(s32[96]{0:T(128)} %tile_rows_in.7, s32[96]{0:T(128)} %tile_cols_in.3, bf16[96,128,128]{2,1,0:T(8,128)(2,1)S(1)} %copy-done, bf16[2048,512]{1,0:T(8,128)(2,1)} %feats_in.3), custom_call_target="tpu_custom_call" | custom-call | flops 4294967296 | bytes 8388608 | tf_op jit(solution)/shard_map/near_forward/pallas_call | solution.py:230
  20.4 4.2 %all-to-all-done.received = bf16[32,48,128]{2,1,0:T(8,128)(2,1)S(1)} async-done(((bf16[32,48,128]{2,1,0:T(8,128)(2,1)}), bf16[32,48,128]{2,1,0:T(8,128)(2,1)S(1)}, u32[]{:S(2)}, u32[]{:S(2)}) %all-to-all-start) | async-done | bytes 393248 | tf_op jit(solution)/shard_map/all_to_all | solution.py:632
  24.6 7.7 %forward.1 = (bf16[2048,512]{1,0:T(8,128)(2,1)}, bf16[2048,512]{1,0:T(8,128)(2,1)}, f32[256,512]{1,0:T(8,128)S(1)}, bf16[256,512]{1,0:T(8,128)(2,1)S(1)}) custom-call(s32[96]{0:T(128)} %tile_rows_in.7, s32[96]{0:T(128)} %tile_cols_in.3, s32[384]{0:T(512)} %get-tuple-element.13.plan_in, bf16[96,128,128]{2,1,0:T(8,128)(2,1)S(1)} %copy-done, ...), custom_call_target="tpu_custom_call" | custom-call | flops 8589934592 | bytes 16777216 | tf_op jit(solution)/shard_map/forward/pallas_call | solution.py:351
  32.4 1.5 %collective-permute-done = bf16[256,512]{1,0:T(8,128)(2,1)S(1)} collective-permute-done((bf16[256,512]{1,0:T(8,128)(2,1)S(1)}, bf16[256,512]{1,0:T(8,128)(2,1)S(1)}, u32[]{:S(2)}, u32[]{:S(2)}) %collective-permute-start) | collective-permute-done | bytes 262176 | tf_op jit(solution)/shard_map/ppermute | solution.py:605
  34.7 4.9 %collective-permute-done.1 = bf16[128,512]{1,0:T(8,128)(2,1)S(1)} collective-permute-done((bf16[128,512]{1,0:T(8,128)(2,1)S(1)}, bf16[128,512]{1,0:T(8,128)(2,1)S(1)}, u32[]{:S(2)}, u32[]{:S(2)}) %collective-permute-start.1) | collective-permute-done | bytes 131104 | tf_op jit(solution)/shard_map/ppermute | solution.py:605
  39.7 1.0 %collective-permute-start.2 = (bf16[64,512]{1,0:T(8,128)(2,1)S(1)}, bf16[64,512]{1,0:T(8,128)(2,1)S(1)}, u32[]{:S(2)}, u32[]{:S(2)}) collective-permute-start(bf16[64,512]{1,0:T(8,128)(2,1)S(1)} %slice.55), channel_id=1, source_target_pairs={{0,4},{1,5},{2,6},{3,7},{4,0},{5,1},{6,2},{7,3},{8,12},{9,13},{10,... | collective-permute-start | bytes 196616 | tf_op jit(solution)/shard_map/ppermute | solution.py:605
  40.7 3.3 %collective-permute-done.2 = bf16[64,512]{1,0:T(8,128)(2,1)S(1)} collective-permute-done((bf16[64,512]{1,0:T(8,128)(2,1)S(1)}, bf16[64,512]{1,0:T(8,128)(2,1)S(1)}, u32[]{:S(2)}, u32[]{:S(2)}) %collective-permute-start.2) | collective-permute-done | bytes 65568 | tf_op jit(solution)/shard_map/ppermute | solution.py:605
  44.0 1.1 %collective-permute-start.3 = (bf16[32,512]{1,0:T(8,128)(2,1)S(1)}, bf16[32,512]{1,0:T(8,128)(2,1)S(1)}, u32[]{:S(2)}, u32[]{:S(2)}) collective-permute-start(bf16[32,512]{1,0:T(8,128)(2,1)S(1)} %slice.56), channel_id=1, source_target_pairs={{0,8},{1,9},{2,10},{3,11},{4,12},{5,13},{6,14},{7,15},{8,0},{9,1},... | collective-permute-start | bytes 98312 | tf_op jit(solution)/shard_map/ppermute | solution.py:605
  45.1 2.9 %collective-permute-done.3 = bf16[32,512]{1,0:T(8,128)(2,1)S(1)} collective-permute-done((bf16[32,512]{1,0:T(8,128)(2,1)S(1)}, bf16[32,512]{1,0:T(8,128)(2,1)S(1)}, u32[]{:S(2)}, u32[]{:S(2)}) %collective-permute-start.3) | collective-permute-done | bytes 32800 | tf_op jit(solution)/shard_map/ppermute | solution.py:605
  49.0 3.9 %collective-permute-done.4 = bf16[16,512]{1,0:T(8,128)(2,1)S(1)} collective-permute-done((bf16[16,512]{1,0:T(8,128)(2,1)S(1)}, bf16[16,512]{1,0:T(8,128)(2,1)S(1)}, u32[]{:S(2)}, u32[]{:S(2)}) %collective-permute-start.4) | collective-permute-done | bytes 16416 | tf_op jit(solution)/shard_map/ppermute | solution.py:605
  53.8 3.8 %collective-permute-done.5 = bf16[16,512]{1,0:T(8,128)(2,1)S(1)} collective-permute-done((bf16[16,512]{1,0:T(8,128)(2,1)S(1)}, bf16[16,512]{1,0:T(8,128)(2,1)S(1)}, u32[]{:S(2)}, u32[]{:S(2)}) %collective-permute-start.5) | collective-permute-done | bytes 16416 | tf_op jit(solution)/shard_map/ppermute | solution.py:605
  57.6 1.0 %collective-permute-start.6 = (bf16[32,512]{1,0:T(8,128)(2,1)S(1)}, bf16[32,512]{1,0:T(8,128)(2,1)S(1)}, u32[]{:S(2)}, u32[]{:S(2)}) collective-permute-start(bf16[32,512]{1,0:T(8,128)(2,1)S(1)} %pad_maximum_fusion.2), channel_id=1, source_target_pairs={{0,8},{1,9},{2,10},{3,11},{4,12},{5,13},{6,14},{7,15},{8,0},{9,1},... | collective-permute-start | bytes 98312 | tf_op jit(solution)/shard_map/ppermute | solution.py:605
  58.6 6.1 %far_backward.1 = (bf16[32,48,128]{2,1,0:T(8,128)(2,1)}, bf16[2048,512]{1,0:T(8,128)(2,1)}) custom-call(s32[96]{0:T(128)} %tile_rows_in.7, s32[384]{0:T(512)} %get-tuple-element.13.plan_in, bf16[96,128,128]{2,1,0:T(8,128)(2,1)S(1)} %copy-done.1, bf16[2048,512]{1,0:T(8,128)(2,1)} %get-tuple-element.16.grad_pre_in, bf16[512,512]{1,0:T(8,128)(2,1)} %weight_in.3), custom_call_target="tpu_custom_call" | custom-call | flops 4294967296 | bytes 8388608 | tf_op jit(solution)/shard_map/far_backward/pallas_call | solution.py:433
  64.7 2.6 %all-to-all-start.1 = ((bf16[32,48,128]{2,1,0:T(8,128)(2,1)}), bf16[32,48,128]{2,1,0:T(8,128)(2,1)S(1)}, u32[]{:S(2)}, u32[]{:S(2)}) async-start(bf16[32,48,128]{2,1,0:T(8,128)(2,1)} %get-tuple-element.20), calls=%async_computation.1 | async-start | bytes 786432 | tf_op jit(solution)/shard_map/all_to_all | solution.py:632
  67.3 1.7 %collective-permute-start.7 = (bf16[64,512]{1,0:T(8,128)(2,1)S(1)}, bf16[64,512]{1,0:T(8,128)(2,1)S(1)}, u32[]{:S(2)}, u32[]{:S(2)}) collective-permute-start(bf16[64,512]{1,0:T(8,128)(2,1)S(1)} %pad_maximum_fusion.1), channel_id=1, source_target_pairs={{0,4},{1,5},{2,6},{3,7},{4,0},{5,1},{6,2},{7,3},{8,12},{9,13},{10,... | collective-permute-start | bytes 196616 | tf_op jit(solution)/shard_map/ppermute | solution.py:605
  69.1 4.2 %collective-permute-done.7 = bf16[64,512]{1,0:T(8,128)(2,1)S(1)} collective-permute-done((bf16[64,512]{1,0:T(8,128)(2,1)S(1)}, bf16[64,512]{1,0:T(8,128)(2,1)S(1)}, u32[]{:S(2)}, u32[]{:S(2)}) %collective-permute-start.7) | collective-permute-done | bytes 65568 | tf_op jit(solution)/shard_map/ppermute | solution.py:605
  73.3 2.5 %collective-permute-start.8 = (bf16[128,512]{1,0:T(8,128)(2,1)S(1)}, bf16[128,512]{1,0:T(8,128)(2,1)S(1)}, u32[]{:S(2)}, u32[]{:S(2)}) collective-permute-start(bf16[128,512]{1,0:T(8,128)(2,1)S(1)} %pad_maximum_fusion), channel_id=1, source_target_pairs={{0,2},{1,3},{2,0},{3,1},{4,6},{5,7},{6,4},{7,5},{8,10},{9,11},{10,... | collective-permute-start | bytes 393224 | tf_op jit(solution)/shard_map/ppermute | solution.py:605
  75.8 4.0 %collective-permute-done.8 = bf16[128,512]{1,0:T(8,128)(2,1)S(1)} collective-permute-done((bf16[128,512]{1,0:T(8,128)(2,1)S(1)}, bf16[128,512]{1,0:T(8,128)(2,1)S(1)}, u32[]{:S(2)}, u32[]{:S(2)}) %collective-permute-start.8) | collective-permute-done | bytes 131104 | tf_op jit(solution)/shard_map/ppermute | solution.py:605
  79.9 1.9 %copy-done.2 = bf16[96,128,128]{2,1,0:T(8,128)(2,1)S(1)} copy-done((bf16[96,128,128]{2,1,0:T(8,128)(2,1)S(1)}, bf16[96,128,128]{2,1,0:T(8,128)(2,1)}, u32[]{:S(2)}) %copy-start.2) | copy-done | bytes 3145752
  81.8 6.8 %near_backward.1 = (f32[2048,512]{1,0:T(8,128)}, bf16[2048,384]{1,0:T(8,128)(2,1)}) custom-call(s32[96]{0:T(128)} %tile_rows_in.7, s32[384]{0:T(512)} %get-tuple-element.13.plan_in, s32[1,8,32]{2,1,0:T(8,128)} %bitcast.2, s32[1,32]{1,0:T(1,128)} %send_count_in.3, s32[4]{0:T(128)} %hub_rows_in.3, bf16[96,128,128]{2,1,0:T(8,128)(2,1)S(1)} %copy-done.2, ...), custom_call_target="tpu_custom_call" | custom-call | flops 4294967296 | bytes 8388608 | tf_op jit(solution)/shard_map/near_backward/pallas_call | solution.py:514
  88.6 4.5 %collect.1 = bf16[2048,512]{1,0:T(8,128)(2,1)} custom-call(f32[2048,512]{1,0:T(8,128)} %get-tuple-element.18.near_in, bf16[2048,384]{1,0:T(8,128)(2,1)} %get-tuple-element.19.spread_in, bf16[32,48,128]{2,1,0:T(8,128)(2,1)S(1)} %all-to-all-done.1.returned), custom_call_target="tpu_custom_call" | custom-call | flops 2147483648 | bytes 8388608 | tf_op jit(solution)/shard_map/collect/pallas_call | solution.py:573
  93.2 1.1 %order.1 = f32[512,512]{1,0:T(8,128)} custom-call(bf16[256,512]{1,0:T(8,128)(2,1)S(1)} %constant_dynamic-update-slice_fusion.first, bf16[256,512]{1,0:T(8,128)(2,1)S(1)} %collective-permute-done.9.second), custom_call_target="tpu_custom_call" | custom-call | tf_op jit(solution)/shard_map/order/pallas_call | solution.py:621
  (29 shorter events, 2.9 us)
Async XLA Ops:
  0.6 10.8 %copy-start = (bf16[96,128,128]{2,1,0:T(8,128)(2,1)S(1)}, bf16[96,128,128]{2,1,0:T(8,128)(2,1)}, u32[]{:S(2)}) copy-start(bf16[96,128,128]{2,1,0:T(8,128)(2,1)} %tiles.7) | copy-start | bytes 9437188
  4.1 20.5 %all-to-all-start = ((bf16[32,48,128]{2,1,0:T(8,128)(2,1)}), bf16[32,48,128]{2,1,0:T(8,128)(2,1)S(1)}, u32[]{:S(2)}, u32[]{:S(2)}) async-start(bf16[32,48,128]{2,1,0:T(8,128)(2,1)} %pack_rows.1), calls=%async_computation | async-start | bytes 786432 | tf_op jit(solution)/shard_map/all_to_all | solution.py:632
  24.6 34.0 %copy-start.1 = (bf16[96,128,128]{2,1,0:T(8,128)(2,1)S(1)}, bf16[96,128,128]{2,1,0:T(8,128)(2,1)}, u32[]{:S(2)}) copy-start(bf16[96,128,128]{2,1,0:T(8,128)(2,1)} %tiles.7) | copy-start | bytes 9437188
  32.3 1.6 %collective-permute-start = (bf16[256,512]{1,0:T(8,128)(2,1)S(1)}, bf16[256,512]{1,0:T(8,128)(2,1)S(1)}, u32[]{:S(2)}, u32[]{:S(2)}) collective-permute-start(bf16[256,512]{1,0:T(8,128)(2,1)S(1)} %get-tuple-element.22), channel_id=1, source_target_pairs={{0,1},{1,0},{2,3},{3,2},{4,5},{5,4},{6,7},{7,6},{8,9},{9,8},{10,11... | collective-permute-start | bytes 786440 | tf_op jit(solution)/shard_map/ppermute | solution.py:605
  34.0 5.6 %collective-permute-start.1 = (bf16[128,512]{1,0:T(8,128)(2,1)S(1)}, bf16[128,512]{1,0:T(8,128)(2,1)S(1)}, u32[]{:S(2)}, u32[]{:S(2)}) collective-permute-start(bf16[128,512]{1,0:T(8,128)(2,1)S(1)} %slice.54), channel_id=1, source_target_pairs={{0,2},{1,3},{2,0},{3,1},{4,6},{5,7},{6,4},{7,5},{8,10},{9,11},{10,... | collective-permute-start | bytes 393224 | tf_op jit(solution)/shard_map/ppermute | solution.py:605
  39.7 4.3 %collective-permute-start.2 = (bf16[64,512]{1,0:T(8,128)(2,1)S(1)}, bf16[64,512]{1,0:T(8,128)(2,1)S(1)}, u32[]{:S(2)}, u32[]{:S(2)}) collective-permute-start(bf16[64,512]{1,0:T(8,128)(2,1)S(1)} %slice.55), channel_id=1, source_target_pairs={{0,4},{1,5},{2,6},{3,7},{4,0},{5,1},{6,2},{7,3},{8,12},{9,13},{10,... | collective-permute-start | bytes 196616 | tf_op jit(solution)/shard_map/ppermute | solution.py:605
  44.0 4.0 %collective-permute-start.3 = (bf16[32,512]{1,0:T(8,128)(2,1)S(1)}, bf16[32,512]{1,0:T(8,128)(2,1)S(1)}, u32[]{:S(2)}, u32[]{:S(2)}) collective-permute-start(bf16[32,512]{1,0:T(8,128)(2,1)S(1)} %slice.56), channel_id=1, source_target_pairs={{0,8},{1,9},{2,10},{3,11},{4,12},{5,13},{6,14},{7,15},{8,0},{9,1},... | collective-permute-start | bytes 98312 | tf_op jit(solution)/shard_map/ppermute | solution.py:605
  48.0 4.9 %collective-permute-start.4 = (bf16[16,512]{1,0:T(8,128)(2,1)S(1)}, bf16[16,512]{1,0:T(8,128)(2,1)S(1)}, u32[]{:S(2)}, u32[]{:S(2)}) collective-permute-start(bf16[16,512]{1,0:T(8,128)(2,1)S(1)} %slice.57), channel_id=1, source_target_pairs={{0,16},{1,17},{2,18},{3,19},{4,20},{5,21},{6,22},{7,23},{8,24},{9,... | collective-permute-start | bytes 49160 | tf_op jit(solution)/shard_map/ppermute | solution.py:605
  52.9 4.6 %collective-permute-start.5 = (bf16[16,512]{1,0:T(8,128)(2,1)S(1)}, bf16[16,512]{1,0:T(8,128)(2,1)S(1)}, u32[]{:S(2)}, u32[]{:S(2)}) collective-permute-start(bf16[16,512]{1,0:T(8,128)(2,1)S(1)} %get-tuple-element.24), channel_id=1, source_target_pairs={{0,16},{1,17},{2,18},{3,19},{4,20},{5,21},{6,22},{7,23},{8,24},{9,... | collective-permute-start | bytes 49160 | tf_op jit(solution)/shard_map/ppermute | solution.py:605
  57.6 9.8 %collective-permute-start.6 = (bf16[32,512]{1,0:T(8,128)(2,1)S(1)}, bf16[32,512]{1,0:T(8,128)(2,1)S(1)}, u32[]{:S(2)}, u32[]{:S(2)}) collective-permute-start(bf16[32,512]{1,0:T(8,128)(2,1)S(1)} %pad_maximum_fusion.2), channel_id=1, source_target_pairs={{0,8},{1,9},{2,10},{3,11},{4,12},{5,13},{6,14},{7,15},{8,0},{9,1},... | collective-permute-start | bytes 98312 | tf_op jit(solution)/shard_map/ppermute | solution.py:605
  64.7 23.9 %all-to-all-start.1 = ((bf16[32,48,128]{2,1,0:T(8,128)(2,1)}), bf16[32,48,128]{2,1,0:T(8,128)(2,1)S(1)}, u32[]{:S(2)}, u32[]{:S(2)}) async-start(bf16[32,48,128]{2,1,0:T(8,128)(2,1)} %get-tuple-element.20), calls=%async_computation.1 | async-start | bytes 786432 | tf_op jit(solution)/shard_map/all_to_all | solution.py:632
  67.3 5.9 %collective-permute-start.7 = (bf16[64,512]{1,0:T(8,128)(2,1)S(1)}, bf16[64,512]{1,0:T(8,128)(2,1)S(1)}, u32[]{:S(2)}, u32[]{:S(2)}) collective-permute-start(bf16[64,512]{1,0:T(8,128)(2,1)S(1)} %pad_maximum_fusion.1), channel_id=1, source_target_pairs={{0,4},{1,5},{2,6},{3,7},{4,0},{5,1},{6,2},{7,3},{8,12},{9,13},{10,... | collective-permute-start | bytes 196616 | tf_op jit(solution)/shard_map/ppermute | solution.py:605
  73.3 6.5 %collective-permute-start.8 = (bf16[128,512]{1,0:T(8,128)(2,1)S(1)}, bf16[128,512]{1,0:T(8,128)(2,1)S(1)}, u32[]{:S(2)}, u32[]{:S(2)}) collective-permute-start(bf16[128,512]{1,0:T(8,128)(2,1)S(1)} %pad_maximum_fusion), channel_id=1, source_target_pairs={{0,2},{1,3},{2,0},{3,1},{4,6},{5,7},{6,4},{7,5},{8,10},{9,11},{10,... | collective-permute-start | bytes 393224 | tf_op jit(solution)/shard_map/ppermute | solution.py:605
  79.8 13.4 %collective-permute-start.9 = (bf16[256,512]{1,0:T(8,128)(2,1)S(1)}, bf16[256,512]{1,0:T(8,128)(2,1)S(1)}, u32[]{:S(2)}, u32[]{:S(2)}) collective-permute-start(bf16[256,512]{1,0:T(8,128)(2,1)S(1)} %constant_dynamic-update-slice_fusion.first), channel_id=1, source_target_pairs={{0,1},{1,0},{2,3},{3,2},{4,5},{5,4},{6,7},{7,6},{8,9},{9,8},{10,11... | collective-permute-start | bytes 786440 | tf_op jit(solution)/shard_map/ppermute | solution.py:605
  79.9 1.9 %copy-start.2 = (bf16[96,128,128]{2,1,0:T(8,128)(2,1)S(1)}, bf16[96,128,128]{2,1,0:T(8,128)(2,1)}, u32[]{:S(2)}) copy-start(bf16[96,128,128]{2,1,0:T(8,128)(2,1)} %tiles.7) | copy-start | bytes 9437188

commit v2 on v1

--- a/solution.py
+++ b/solution.py
@@ -14,6 +14,7 @@
 KEYS = 32
 LIST = 64
 UNROLL = 4
+HALVED = (0, 3, 4)
 NEAR_FWD, FAR_FWD, NEAR_BWD, FAR_BWD = range(4)
 COUNTS = 4 * LIST
 PLAN = COUNTS + LANES
@@ -33,6 +34,10 @@
 
 def in_hbm(*arrays):
     return [pltpu.with_memory_space_constraint(a, pltpu.HBM) for a in arrays]
+
+
+def in_vmem(*arrays):
+    return [pltpu.with_memory_space_constraint(a, pltpu.VMEM) for a in arrays]
 
 
 def cost(flops, moved):
@@ -203,48 +208,100 @@
     lax.fori_loop(0, (plan[COUNTS + kind] + UNROLL - 1) // UNROLL, group, 0)
 
 
+def make_spread(n, slots, hubs, chunks, send_rows, send_count, hub_rows, spread):
+    rows = spread.shape[0]
+    lane = lax.broadcasted_iota(I32, (SUBS, LANES), 1)
+    sub = lax.broadcasted_iota(I32, (SUBS, LANES), 0)
+
+    def put(part, targets):
+        def rows_of(b, _):
+            hit = jnp.where(targets == sub + b * SUBS, 1.0, 0.0)
+            spread[rows_at(b, SUBS), part * LANES : (part + 1) * LANES] = hit.astype(BF16)
+            return 0
+
+        lax.fori_loop(0, rows // SUBS, rows_of, 0, unroll=8)
+
+    per = LANES // slots
+    for part in range(n * slots // LANES):
+
+        def dest(s, targets, part=part):
+            count = send_count[0, part * per + s]
+            for k in range(slots):
+                row = jnp.where(k < count, send_rows[0, k, part * per + s], -1)
+                targets = jnp.where(lane == s * slots + k, row, targets)
+            return targets
+
+        put(part, lax.fori_loop(0, per, dest, jnp.full((SUBS, LANES), -1, I32)))
+    targets = jnp.full((SUBS, LANES), -1, I32)
+    for at in range(2 * hubs * chunks):
+        targets = jnp.where(lane == at, hub_rows[at % hubs], targets)
+    put(n * slots // LANES, targets)
+
+
 def near_forward_kernel(
-    tile_rows_in, tile_cols_in, tiles, feats_in, near_out, plan_out,
-    tile_rows, tile_cols, feats, total, plan, waiting, sems,
+    n, slots, hubs, tile_rows_in, tile_cols_in, send_rows_in, send_count_in, hub_rows_in, tiles, feats_in,
+    near_out, plan_out, spread_out,
+    tile_rows, tile_cols, send_rows, send_count, hub_rows, feats, total, spread, plan, waiting, sems,
 ):
     rows, width = feats.shape
     blocks = rows // tiles.shape[1]
-    copies = [
-        start(a, b, sems.at[i])
-        for i, (a, b) in enumerate(((tile_rows_in, tile_rows), (tile_cols_in, tile_cols), (feats_in, feats)))
-    ]
+    moves = (
+        (tile_rows_in, tile_rows),
+        (tile_cols_in, tile_cols),
+        (send_rows_in, send_rows),
+        (send_count_in, send_count),
+        (hub_rows_in, hub_rows),
+        (feats_in, feats),
+    )
+    copies = [start(a, b, sems.at[i]) for i, (a, b) in enumerate(moves)]
     total[...] = jnp.zeros_like(total)
     copies[0].wait()
     copies[1].wait()
     make_plan(tile_rows, tile_cols, blocks, plan, waiting)
-    sent = start(plan, plan_out, sems.at[0])
-    copies[2].wait()
+    sent = [start(plan, plan_out, sems.at[0])]
+    for copy in copies[2:]:
+        copy.wait()
     run_plan(NEAR_FWD, plan, tiles, lambda t: jnp.minimum(tile_cols[t], blocks - 1), feats, total, False)
-    last = start(total, near_out, sems.at[1])
-    sent.wait()
-    last.wait()
-
-
-def near_forward(tile_rows, tile_cols, tiles, features):
+    sent.append(start(total, near_out, sems.at[1]))
+    make_spread(n, slots, hubs, width // LANES, send_rows, send_count, hub_rows, spread)
+    sent.append(start(spread, spread_out, sems.at[2]))
+    for copy in sent:
+        copy.wait()
+
+
+def near_forward(n, tile_rows, tile_cols, send_rows, send_count, hub_rows, tiles, features):
     rows, width = features.shape
+    slots, hubs = send_rows.shape[1], hub_rows.shape[0]
     return pl.pallas_call(
-        near_forward_kernel,
-        out_shape=(pltpu.HBM((rows, width), F32), pltpu.HBM((PLAN,), I32)),
-        in_specs=[HBM, HBM, VMEM, HBM],
-        out_specs=(HBM, HBM),
+        functools.partial(near_forward_kernel, n, slots, hubs),
+        out_shape=(
+            pltpu.HBM((rows, width), F32),
+            pltpu.HBM((PLAN,), I32),
+            pltpu.HBM((rows, n * slots + LANES), BF16),
+        ),
+        in_specs=[HBM] * 5 + [VMEM, HBM],
+        out_specs=(HBM, HBM, HBM),
         scratch_shapes=[
             pltpu.SMEM(tile_rows.shape, I32),
             pltpu.SMEM(tile_cols.shape, I32),
+            pltpu.SMEM(send_rows.shape, I32),
+            pltpu.SMEM(send_count.shape, I32),
+            pltpu.SMEM(hub_rows.shape, I32),
             pltpu.VMEM((rows, width), BF16),
             pltpu.VMEM((rows, width), F32),
+            pltpu.VMEM((rows, n * slots + LANES), BF16),
             pltpu.SMEM((PLAN,), I32),
             pltpu.SMEM((4 * KEYS,), I32),
-            DMA((3,)),
+            DMA((6,)),
         ],
-        compiler_params=params(12 << 20),
+        compiler_params=params(20 << 20),
         cost_estimate=cost(4 << 30, 8 << 20),
         name="near_forward",
-    )(*in_hbm(tile_rows, tile_cols), tiles, *in_hbm(features))
+    )(
+        *in_hbm(tile_rows, tile_cols, send_rows, send_count, hub_rows),
+        *in_vmem(tiles),
+        *in_hbm(features),
+    )
 
 
 def unpack_slots(n, slots, chunks, packed, into, at):
@@ -263,24 +320,18 @@
     lax.fori_loop(0, n // 2, pair, 0, unroll=4)
 
 
-def reversed_bits(value, bits):
+def place():
+    device = lax.axis_index("dom")
     out = jnp.zeros((), I32)
-    for bit in range(bits):
-        out = out | (((value >> bit) & 1) << (bits - 1 - bit))
+    for at, bit in enumerate(HALVED):
+        out = out | (((device >> bit) & 1) << (len(HALVED) - 1 - at))
     return out
-
-
-def halvings(n, width):
-    steps = 0
-    while 2 << steps <= n and width >> (steps + 1) >= SUBS:
-        steps += 1
-    return steps
 
 
 def forward_kernel(
     n, slots, hubs, tile_rows_in, tile_cols_in, plan_in, tiles, received, near_in, weight_in, cot_in,
-    output, grad_pre_out, keep, give,
-    tile_rows, tile_cols, plan, table, total, near, weight, cot, agg, grad_pre, out, sems, near_sems, cot_sems, out_sems, gp_sems,
+    output, grad_agg_out, keep, give,
+    tile_rows, tile_cols, plan, table, total, near, weight, cot, agg, grad_pre, grad_agg, out, sems, near_sems, cot_sems, out_sems, ga_sems,
 ):
     size = tiles.shape[1]
     rows, width = near.shape
@@ -294,8 +345,10 @@
     ]
     weight_copy = start(weight_in, weight, sems.at[3])
     pieces = [pl.ds(b * step, step) for b in range(steps)]
-    near_copies = [start(near_in.at[at], near.at[at], near_sems.at[b]) for b, at in enumerate(pieces)]
-    cot_copies = [start(cot_in.at[at], cot.at[at], cot_sems.at[b]) for b, at in enumerate(pieces)]
+    arrivals = [
+        (start(near_in.at[at], near.at[at], near_sems.at[b]), start(cot_in.at[at], cot.at[at], cot_sems.at[b]))
+        for b, at in enumerate(pieces)
+    ]
     total[...] = jnp.zeros_like(total)
 
     def four(q, _):
@@ -311,18 +364,29 @@
         copy.wait()
     run_plan(FAR_FWD, plan, tiles, lambda t: jnp.maximum(tile_cols[t] - blocks, 0), table, total, False)
     weight_copy.wait()
-    sent = []
-    for b, at in enumerate(pieces):
-        near_copies[b].wait()
-        cot_copies[b].wait()
+    for pair in arrivals:
+        for copy in pair:
+            copy.wait()
+
+    def first(at):
         here = (total[at, :] + near[at, :]).astype(BF16)
         agg[at, :] = here
-        pre = jnp.dot(here, weight[...], preferred_element_type=F32)
-        sig = jax.nn.sigmoid(pre)
+        return jnp.dot(here, weight[...], preferred_element_type=F32)
+
+    sent = []
+    pre = first(pieces[0])
+    for b, at in enumerate(pieces):
+        following = first(pieces[b + 1]) if b + 1 < steps else None
+        sig = 0.5 * jnp.tanh(0.5 * pre) + 0.5
         out[at, :] = (pre * sig).astype(BF16)
-        grad_pre[at, :] = (cot[at, :].astype(F32) * sig * (1.0 + pre * (1.0 - sig))).astype(BF16)
+        gp = (cot[at, :].astype(F32) * sig * (1.0 + pre * (1.0 - sig))).astype(BF16)
+        grad_pre[at, :] = gp
+        grad_agg[at, :] = lax.dot_general(
+            gp, weight[...], (((1,), (1,)), ((), ())), preferred_element_type=F32
+        ).astype(BF16)
         sent.append(start(out.at[at], output.at[at], out_sems.at[b]))
-        sent.append(start(grad_pre.at[at], grad_pre_out.at[at], gp_sems.at[b]))
+        sent.append(start(grad_agg.at[at], grad_agg_out.at[at], ga_sems.at[b]))
+        pre = following
     scale = float(rows * n) ** -0.5
     term = total.at[pl.ds(0, width)]
     for c in range(0, width, 256):
@@ -332,10 +396,9 @@
             )
             * scale
         )
-    bits = halvings(n, width)
-    unit = width >> bits
-    mine = reversed_bits(lax.axis_index("dom"), bits)
-    half = 1 << (bits - 1)
+    half = 1 << (len(HALVED) - 1)
+    unit = width // (2 * half)
+    mine = place()
     for b in range(half):
         spot = slice(b * unit, (b + 1) * unit)
         keep[spot, :] = term[rows_at(mine ^ b, unit), :]
@@ -347,14 +410,13 @@
 def forward(n, slots, hubs, tile_rows, tile_cols, plan, tiles, received, near, weight, cotangent):
     rows, width = near.shape
     steps = rows // 256
-    shape = jax.ShapeDtypeStruct
     return pl.pallas_call(
         functools.partial(forward_kernel, n, slots, hubs),
         out_shape=(
             pltpu.HBM((rows, width), BF16),
             pltpu.HBM((rows, width), BF16),
-            shape((width // 2, width), F32),
-            shape((width // 2, width), BF16),
+            pltpu.VMEM((width // 2, width), F32),
+            pltpu.VMEM((width // 2, width), BF16),
         ),
         in_specs=[HBM, HBM, HBM, VMEM, VMEM, HBM, HBM, HBM],
         out_specs=(HBM, HBM, VMEM, VMEM),
@@ -370,6 +432,7 @@
             pltpu.VMEM((rows, width), BF16),
             pltpu.VMEM((rows, width), BF16),
             pltpu.VMEM((rows, width), BF16),
+            pltpu.VMEM((rows, width), BF16),
             DMA((4,)),
             DMA((steps,)),
             DMA((steps,)),
@@ -379,30 +442,17 @@
         compiler_params=params(28 << 20),
         cost_estimate=cost(8 << 30, 16 << 20),
         name="forward",
-    )(*in_hbm(tile_rows, tile_cols, plan), tiles, received, *in_hbm(near, weight, cotangent))
+    )(*in_hbm(tile_rows, tile_cols, plan), *in_vmem(tiles, received), *in_hbm(near, weight, cotangent))
 
 
 def far_backward_kernel(
-    n, slots, hubs, tile_rows_in, plan_in, tiles, grad_pre_in, weight_in, out, grad_agg_out,
-    tile_rows, plan, grad_pre, weight, grad_agg, total, staged, sems, in_sems, out_sems,
+    n, slots, hubs, tile_rows_in, plan_in, tiles, grad_agg_in, out, tile_rows, plan, grad_agg, total, staged, sems
 ):
-    rows, width = grad_pre.shape
-    chunks = width // LANES
-    step = 512
-    pieces = [pl.ds(at, step) for at in range(0, rows, step)]
-    weight_copy = start(weight_in, weight, sems.at[0])
-    copies = [start(grad_pre_in.at[at], grad_pre.at[at], in_sems.at[b]) for b, at in enumerate(pieces)]
-    index = [start(plan_in, plan, sems.at[1]), start(tile_rows_in, tile_rows, sems.at[2])]
+    chunks = grad_agg.shape[1] // LANES
+    moves = ((plan_in, plan), (tile_rows_in, tile_rows), (grad_agg_in, grad_agg))
+    copies = [start(a, b, sems.at[i]) for i, (a, b) in enumerate(moves)]
     total[...] = jnp.zeros_like(total)
-    weight_copy.wait()
-    sent = []
-    for b, at in enumerate(pieces):
-        copies[b].wait()
-        grad_agg[at, :] = lax.dot_general(
-            grad_pre[at, :], weight[...], (((1,), (1,)), ((), ())), preferred_element_type=F32
-        ).astype(BF16)
-        sent.append(start(grad_agg.at[at], grad_agg_out.at[at], out_sems.at[b]))
-    for copy in index:
+    for copy in copies:
         copy.wait()
     run_plan(FAR_BWD, plan, tiles, lambda t: tile_rows[t], grad_agg, total, True)
 
@@ -422,126 +472,72 @@
         return 0
 
     lax.fori_loop(0, n // 2, two, 0, unroll=2)
-    sent.append(start(staged, out, sems.at[0]))
-    for copy in sent:
-        copy.wait()
-
-
-def far_backward(n, slots, hubs, tile_rows, plan, tiles, grad_pre, weight):
-    rows, width = grad_pre.shape
+    start(staged, out, sems.at[0]).wait()
+
+
+def far_backward(n, slots, hubs, tile_rows, plan, tiles, grad_agg):
+    width = grad_agg.shape[1]
     packed = (n, (slots + hubs) * width // LANES, LANES)
     return pl.pallas_call(
         functools.partial(far_backward_kernel, n, slots, hubs),
-        out_shape=(pltpu.HBM(packed, BF16), pltpu.HBM((rows, width), BF16)),
-        in_specs=[HBM, HBM, VMEM, HBM, HBM],
-        out_specs=(HBM, HBM),
+        out_shape=pltpu.HBM(packed, BF16),
+        in_specs=[HBM, HBM, VMEM, HBM],
+        out_specs=HBM,
         scratch_shapes=[
             pltpu.SMEM(tile_rows.shape, I32),
             pltpu.SMEM((PLAN,), I32),
-            pltpu.VMEM((rows, width), BF16),
-            pltpu.VMEM((width, width), BF16),
-            pltpu.VMEM((rows, width), BF16),
+            pltpu.VMEM(grad_agg.shape, BF16),
             pltpu.VMEM((n * (slots + hubs), width), F32),
             pltpu.VMEM(packed, BF16),
             DMA((3,)),
-            DMA((rows // 512,)),
-            DMA((rows // 512,)),
+        ],
+        compiler_params=params(12 << 20),
+        cost_estimate=cost(4 << 30, 8 << 20),
+        name="far_backward",
+    )(*in_hbm(tile_rows, plan), *in_vmem(tiles), *in_hbm(grad_agg))
+
+
+def near_backward_kernel(
+    tile_rows_in, plan_in, tiles_in, grad_agg_in, out, tile_rows, plan, tiles, grad_agg, total, sems
+):
+    near = tiles_in.at[pl.ds(0, LOC_TILES)]
+    moves = ((tile_rows_in, tile_rows), (plan_in, plan), (grad_agg_in, grad_agg), (near, tiles))
+    copies = [start(a, b, sems.at[i]) for i, (a, b) in enumerate(moves)]
+    total[...] = jnp.zeros_like(total)
+    for copy in copies:
+        copy.wait()
+    run_plan(NEAR_BWD, plan, tiles, lambda t: tile_rows[t], grad_agg, total, True)
+    out[...] = total[...].astype(BF16)
+
+
+def near_backward(tile_rows, plan, tiles, grad_agg):
+    return pl.pallas_call(
+        near_backward_kernel,
+        out_shape=pltpu.VMEM(grad_agg.shape, BF16),
+        in_specs=[HBM] * 4,
+        out_specs=VMEM,
+        scratch_shapes=[
+            pltpu.SMEM(tile_rows.shape, I32),
+            pltpu.SMEM((PLAN,), I32),
+            pltpu.VMEM((LOC_TILES,) + tiles.shape[1:], BF16),
+            pltpu.VMEM(grad_agg.shape, BF16),
+            pltpu.VMEM(grad_agg.shape, F32),
+            DMA((4,)),
         ],
         compiler_params=params(16 << 20),
         cost_estimate=cost(4 << 30, 8 << 20),
-        name="far_backward",
-    )(*in_hbm(tile_rows, plan), tiles, *in_hbm(grad_pre, weight))
-
-
-def near_backward_kernel(
-    n, slots, hubs, tile_rows_in, plan_in, send_rows_in, send_count_in, hub_rows_in, tiles, grad_agg_in, total_out, spread_out,
-    tile_rows, plan, send_rows, send_count, hub_rows, grad_agg, total, spread, sems,
+        name="near_backward",
+    )(*in_hbm(tile_rows, plan, tiles, grad_agg))
+
+
+def collect_kernel(
+    n, slots, hubs, near, spread_in, returned, out, spread, table, staged, spread_sems, out_sems
 ):
-    rows, width = grad_agg.shape
-    chunks = width // LANES
-    copies = [
-        start(a, b, sems.at[i])
-        for i, (a, b) in enumerate(
-            (
-                (tile_rows_in, tile_rows),
-                (plan_in, plan),
-                (send_rows_in, send_rows),
-                (send_count_in, send_count),
-                (hub_rows_in, hub_rows),
-                (grad_agg_in, grad_agg),
-            )
-        )
-    ]
-    total[...] = jnp.zeros_like(total)
-    for copy in copies:
-        copy.wait()
-    run_plan(NEAR_BWD, plan, tiles, lambda t: tile_rows[t], grad_agg, total, True)
-    sent = start(total, total_out, sems.at[0])
-    lane = lax.broadcasted_iota(I32, (SUBS, LANES), 1)
-    sub = lax.broadcasted_iota(I32, (SUBS, LANES), 0)
-
-    def put(part, targets):
-        def rows_of(b, _):
-            hit = jnp.where(targets == sub + b * SUBS, 1.0, 0.0)
-            spread[rows_at(b, SUBS), part * LANES : (part + 1) * LANES] = hit.astype(BF16)
-            return 0
-
-        lax.fori_loop(0, rows // SUBS, rows_of, 0, unroll=8)
-
-    per = LANES // slots
-    for part in range(n * slots // LANES):
-
-        def dest(s, targets, part=part):
-            count = send_count[0, part * per + s]
-            for k in range(slots):
-                row = jnp.where(k < count, send_rows[0, k, part * per + s], -1)
-                targets = jnp.where(lane == s * slots + k, row, targets)
-            return targets
-
-        put(part, lax.fori_loop(0, per, dest, jnp.full((SUBS, LANES), -1, I32)))
-    targets = jnp.full((SUBS, LANES), -1, I32)
-    for at in range(2 * hubs * chunks):
-        targets = jnp.where(lane == at, hub_rows[at % hubs], targets)
-    put(n * slots // LANES, targets)
-    last = start(spread, spread_out, sems.at[1])
-    sent.wait()
-    last.wait()
-
-
-def near_backward(n, slots, hubs, tile_rows, plan, send_rows, send_count, hub_rows, tiles, grad_agg):
-    rows, width = grad_agg.shape
-    table = n * slots + LANES
-    return pl.pallas_call(
-        functools.partial(near_backward_kernel, n, slots, hubs),
-        out_shape=(pltpu.HBM((rows, width), F32), pltpu.HBM((rows, table), BF16)),
-        in_specs=[HBM] * 5 + [VMEM, HBM],
-        out_specs=(HBM, HBM),
-        scratch_shapes=[
-            pltpu.SMEM(tile_rows.shape, I32),
-            pltpu.SMEM((PLAN,), I32),
-            pltpu.SMEM(send_rows.shape, I32),
-            pltpu.SMEM(send_count.shape, I32),
-            pltpu.SMEM(hub_rows.shape, I32),
-            pltpu.VMEM((rows, width), BF16),
-            pltpu.VMEM((rows, width), F32),
-            pltpu.VMEM((rows, table), BF16),
-            DMA((6,)),
-        ],
-        compiler_params=params(20 << 20),
-        cost_estimate=cost(4 << 30, 8 << 20),
-        name="near_backward",
-    )(*in_hbm(tile_rows, plan, send_rows, send_count, hub_rows), tiles, *in_hbm(grad_agg))
-
-
-def collect_kernel(n, slots, hubs, near_in, spread_in, returned, out, near, spread, table, staged, near_sems, spread_sems, out_sems):
-    rows, width = near.shape
+    rows, width = staged.shape
     chunks = width // LANES
     step = 256
     pieces = [pl.ds(at, step) for at in range(0, rows, step)]
-    copies = []
-    for b, at in enumerate(pieces):
-        copies.append(start(spread_in.at[at], spread.at[at], spread_sems.at[b]))
-        copies.append(start(near_in.at[at], near.at[at], near_sems.at[b]))
+    arrival = start(spread_in, spread, spread_sems.at[0])
     unpack_slots(n, slots, chunks, returned, table, 0)
     hub = lax.fori_loop(
         0, n, lambda s, held: held + returned[s, 0:SUBS, :].astype(F32), jnp.zeros((SUBS, LANES), F32), unroll=8
@@ -556,11 +552,10 @@
                 group == c, part, 0.0
             ).astype(BF16)
     sent = []
+    arrival.wait()
     for b, at in enumerate(pieces):
-        copies[2 * b].wait()
         more = jnp.dot(spread[at, :], table[...], preferred_element_type=F32)
-        copies[2 * b + 1].wait()
-        staged[at, :] = (near[at, :] + more).astype(BF16)
+        staged[at, :] = (near[at, :].astype(F32) + more).astype(BF16)
         sent.append(start(staged.at[at], out.at[at], out_sems.at[b]))
     for copy in sent:
         copy.wait()
@@ -569,32 +564,28 @@
 def collect(n, slots, hubs, near, spread, returned):
     rows, width = near.shape
     table = n * slots + LANES
-    steps = rows // 256
     return pl.pallas_call(
         functools.partial(collect_kernel, n, slots, hubs),
         out_shape=pltpu.HBM((rows, width), BF16),
-        in_specs=[HBM, HBM, VMEM],
+        in_specs=[VMEM, HBM, VMEM],
         out_specs=HBM,
         scratch_shapes=[
-            pltpu.VMEM((rows, width), F32),
             pltpu.VMEM((rows, table), BF16),
             pltpu.VMEM((table, width), BF16),
             pltpu.VMEM((rows, width), BF16),
-            DMA((steps,)),
-            DMA((steps,)),
-            DMA((steps,)),
+            DMA((1,)),
+            DMA((rows // 256,)),
         ],
-        compiler_params=params(20 << 20),
-        cost_estimate=cost(2 << 30, 8 << 20),
+        compiler_params=params(16 << 20),
+        cost_estimate=cost(32 << 30, 8 << 20),
         name="collect",
-    )(*in_hbm(near, spread), returned)
-
-
-def order_kernel(bits, first, second, out):
-    width = out.shape[0]
-    unit = width >> bits
-    half = 1 << (bits - 1)
-    mine = reversed_bits(lax.axis_index("dom"), bits)
+    )(*in_vmem(near), *in_hbm(spread), *in_vmem(returned))
+
+
+def order_kernel(first, second, out):
+    half = 1 << (len(HALVED) - 1)
+    unit = out.shape[0] // (2 * half)
+    mine = place()
     for b in range(half):
         spot = slice(b * unit, (b + 1) * unit)
         out[rows_at(mine ^ b, unit), :] = first[spot, :].astype(F32)
@@ -605,27 +596,8 @@
     return lax.ppermute(x, "dom", [(i, i ^ (1 << bit)) for i in range(n)])
 
 
-def sum_weight(n, keep, give):
-    width = keep.shape[1]
-    bits = halvings(n, width)
-    for bit in range(bits):
-        keep = keep + exchange(give, n, bit).astype(F32)
-        if bit + 1 < bits:
-            half = keep.shape[0] // 2
-            keep, give = keep[:half], keep[half:].astype(BF16)
-    for bit in range(bits, n.bit_length() - 1):
-        keep = keep + exchange(keep.astype(BF16), n, bit).astype(F32)
-    held = keep.astype(BF16)
-    for bit in reversed(range(1, bits)):
-        held = jnp.concatenate([held, exchange(held, n, bit)], axis=0)
-    return pl.pallas_call(
-        functools.partial(order_kernel, bits),
-        out_shape=jax.ShapeDtypeStruct((width, width), F32),
-        in_specs=[VMEM, VMEM],
-        out_specs=VMEM,
-        compiler_params=params(4 << 20),
-        name="order",
-    )(held, exchange(held, n, 0))
+def tie(*arrays):
+    return lax.optimization_barrier(arrays)
 
 
 def all_to_all(x):
@@ -641,17 +613,45 @@
 
     packed = pack_rows(n, send_rows, send_count, hub_rows, features)
     received = all_to_all(packed)
-    near, plan = near_forward(tile_rows, tile_cols, tile_values, features)
-    output, grad_pre, keep, give = forward(
+    near, plan, spread = near_forward(
+        n, tile_rows, tile_cols, send_rows, send_count, hub_rows, tile_values, features
+    )
+    output, grad_agg, keep, give = forward(
         n, slots, hubs, tile_rows, tile_cols, plan, tile_values, received, near, weight, cotangent
     )
-    far, grad_agg = far_backward(n, slots, hubs, tile_rows, plan, tile_values, grad_pre, weight)
+    width = keep.shape[1]
+    keep = keep + exchange(give, n, HALVED[0]).astype(F32)
+    half = keep.shape[0] // 2
+    keep, give, grad_agg = tie(keep[:half].astype(BF16), keep[half:].astype(BF16), grad_agg)
+    got = exchange(give, n, HALVED[1])
+    far = far_backward(n, slots, hubs, tile_rows, plan, tile_values, grad_agg)
+    half = half // 2
+    give = (keep[half:].astype(F32) + got[half:].astype(F32)).astype(BF16)
+    keep = (keep[:half].astype(F32) + got[:half].astype(F32)).astype(BF16)
+    keep, give, far = tie(keep, give, far)
+    got = exchange(give, n, HALVED[2])
     returned = all_to_all(far)
-    near_grad, spread = near_backward(
-        n, slots, hubs, tile_rows, plan, send_rows, send_count, hub_rows, tile_values, grad_agg
-    )
+    held, grad_agg = tie((keep.astype(F32) + got.astype(F32)).astype(BF16), grad_agg)
+    for bit in range(n.bit_length() - 1):
+        if bit not in HALVED:
+            got = exchange(held, n, bit)
+            if bit == 2:
+                near_grad = near_backward(tile_rows, plan, tile_values, grad_agg)
+            held, grad_agg = tie((held.astype(F32) + got.astype(F32)).astype(BF16), grad_agg)
+    held, near_grad = tie(held, near_grad)
+    got = exchange(held, n, HALVED[2])
+    held, returned = tie(jnp.concatenate([held, got], axis=0), returned)
+    got = exchange(held, n, HALVED[1])
     grad_features = collect(n, slots, hubs, near_grad, spread, returned)
-    grad_weight = sum_weight(n, keep, give)
+    held, grad_features = tie(jnp.concatenate([held, got], axis=0), grad_features)
+    grad_weight = pl.pallas_call(
+        order_kernel,
+        out_shape=jax.ShapeDtypeStruct((width, width), F32),
+        in_specs=[VMEM, VMEM],
+        out_specs=VMEM,
+        compiler_params=params(4 << 20),
+        name="order",
+    )(held, exchange(held, n, HALVED[0]))
     return (output, grad_features, grad_weight)
 
 

time: 95 us -> 72.2 us (0.76)
  waiting for transfers between devices: 32.7 us -> 18.2 us
  Pallas kernels: 38.6 us -> 35.2 us
  starting transfers between devices: 19.9 us -> 17.4 us
  local copies, waits for them, and re-layouts: 1.96 us -> 0.03 us
    ppermute x10 -> x8, waiting for transfers between devices: 28.5 us -> 14.9 us  [exchange(): return lax.ppermute(x, 'dom', [(i, i ^ 1 << bit) for i in range(n)])]
    ppermute x10 -> x8, starting transfers between devices: 10 us -> 7.5 us  [exchange(): return lax.ppermute(x, 'dom', [(i, i ^ 1 << bit) for i in range(n)])]
    pallas_call x1, Pallas kernels: 6.12 us -> 4.18 us  [far_backward(): pl.pallas_call(functools.partial(far_backward_kernel, n, slots, hubs), ou...]
    unnamed x9 -> x2, local copies, waits for them, and re-layouts: 1.91 us -> 0.01 us
    pallas_call x1, Pallas kernels: 4.55 us -> 3.44 us  [collect(): pl.pallas_call(functools.partial(collect_kernel, n, slots, hubs), out_sha...]
  transfers between devices with their start and end apart: 12 -> 10, of which waited for: 9 -> 8; matrix products, arithmetic and copies ran while one was open for 0% -> 0% of each run, Pallas kernels for 28% -> 32%
where the time goes in v2:
time: 72.2 us; the launch traced here: 71.8 us
  Pallas kernels  35.2 us (49%)
  waiting for transfers between devices  18.2 us (25%)
  starting transfers between devices  17.4 us (24%)
  between operations  0.79 us (1%)
    ppermute x8, waiting for transfers between devices, exchange(): return lax.ppermute(x, 'dom', [(i, i ^ 1 << bit) for i in range(n)])  14.9 us
    all_to_all x2, starting transfers between devices, all_to_all(): return lax.all_to_all(x, 'dom', split_axis=0, concat_axis=0, tiled=True)  9.91 us
    pallas_call x1, Pallas kernels, near_forward(): pl.pallas_call(functools.partial(near_forward_kernel, n, slots, hubs), ou...  9.88 us
    pallas_call x1, Pallas kernels, forward(): pl.pallas_call(functools.partial(forward_kernel, n, slots, hubs), out_sha...  7.64 us
    ppermute x8, starting transfers between devices, exchange(): return lax.ppermute(x, 'dom', [(i, i ^ 1 << bit) for i in range(n)])  7.5 us
    pallas_call x1, Pallas kernels, near_backward(): pl.pallas_call(near_backward_kernel, out_shape=pltpu.VMEM(grad_agg.shape,...  5.55 us
    pallas_call x1, Pallas kernels, far_backward(): pl.pallas_call(functools.partial(far_backward_kernel, n, slots, hubs), ou...  4.18 us
    pallas_call x1, Pallas kernels, pack_rows(): pl.pallas_call(functools.partial(pack_kernel, n, slots, hubs), out_shape=...  3.46 us
  transfers between devices with their start and end apart: 10, of which 8 were waited for; matrix products, arithmetic and copies ran while one was open for 0% of the time, Pallas kernels for 32%

profile of v2, /device:TPU:0, one launch (start us, length us, event | category | flops | bytes accessed | tf_op | source)
XLA Modules:
  0.0 71.8 jit_solution(1011798914463697000)
XLA Ops:
  0.6 3.5 %pack_rows.1 = bf16[32,48,128]{2,1,0:T(8,128)(2,1)} custom-call(s32[1,8,32]{2,1,0:T(8,128)} %bitcast.1, s32[1,32]{1,0:T(1,128)} %send_count_in.3, s32[4]{0:T(128)} %hub_rows_in.3, bf16[2048,512]{1,0:T(8,128)(2,1)} %feats_in.3), custom_call_target="tpu_custom_call" | custom-call | tf_op jit(solution)/shard_map/pack_rows/pallas_call | solution.py:129
  4.1 7.3 %all-to-all-start = ((bf16[32,48,128]{2,1,0:T(8,128)(2,1)}), bf16[32,48,128]{2,1,0:T(8,128)(2,1)S(1)}, u32[]{:S(2)}, u32[]{:S(2)}) async-start(bf16[32,48,128]{2,1,0:T(8,128)(2,1)} %pack_rows.1), calls=%async_computation | async-start | bytes 786432 | tf_op jit(solution)/shard_map/all_to_all | solution.py:604
  11.4 9.9 %near_forward.1 = (f32[2048,512]{1,0:T(8,128)}, s32[384]{0:T(512)}, bf16[2048,384]{1,0:T(8,128)(2,1)}) custom-call(s32[96]{0:T(128)} %tile_rows_in.7, s32[96]{0:T(128)} %tile_cols_in.3, s32[1,8,32]{2,1,0:T(8,128)} %bitcast.2, s32[1,32]{1,0:T(1,128)} %send_count_in.3, s32[4]{0:T(128)} %hub_rows_in.3, bf16[96,128,128]{2,1,0:T(8,128)(2,1)S(1)} %copy-done, ...), custom_call_target="tpu_custom_call" | custom-call | flops 4294967296 | bytes 8388608 | tf_op jit(solution)/shard_map/near_forward/pallas_call | solution.py:275
  21.3 3.3 %all-to-all-done.received = bf16[32,48,128]{2,1,0:T(8,128)(2,1)S(1)} async-done(((bf16[32,48,128]{2,1,0:T(8,128)(2,1)}), bf16[32,48,128]{2,1,0:T(8,128)(2,1)S(1)}, u32[]{:S(2)}, u32[]{:S(2)}) %all-to-all-start) | async-done | bytes 393248 | tf_op jit(solution)/shard_map/all_to_all | solution.py:604
  24.6 7.6 %forward.1 = (bf16[2048,512]{1,0:T(8,128)(2,1)}, bf16[2048,512]{1,0:T(8,128)(2,1)}, f32[256,512]{1,0:T(8,128)S(1)}, bf16[256,512]{1,0:T(8,128)(2,1)S(1)}) custom-call(s32[96]{0:T(128)} %tile_rows_in.7, s32[96]{0:T(128)} %tile_cols_in.3, s32[384]{0:T(512)} %get-tuple-element.27.plan_in, bf16[96,128,128]{2,1,0:T(8,128)(2,1)S(1)} %copy-done, ...), custom_call_target="tpu_custom_call" | custom-call | flops 8589934592 | bytes 16777216 | tf_op jit(solution)/shard_map/forward/pallas_call | solution.py:413
  32.3 0.1 collective-permute-start
  32.3 1.5 %collective-permute-done = bf16[256,512]{1,0:T(8,128)(2,1)S(1)} collective-permute-done((bf16[256,512]{1,0:T(8,128)(2,1)S(1)}, bf16[256,512]{1,0:T(8,128)(2,1)S(1)}, u32[]{:S(2)}, u32[]{:S(2)}) %collective-permute-start) | collective-permute-done | bytes 262176 | tf_op jit(solution)/shard_map/ppermute | solution.py:596
  34.0 1.1 %collective-permute-start.1 = (bf16[128,512]{1,0:T(8,128)(2,1)S(1)}, bf16[128,512]{1,0:T(8,128)(2,1)S(1)}, u32[]{:S(2)}, u32[]{:S(2)}) collective-permute-start(bf16[128,512]{1,0:T(8,128)(2,1)S(1)} %get-tuple-element.34), channel_id=1, source_target_pairs={{0,8},{1,9},{2,10},{3,11},{4,12},{5,13},{6,14},{7,15},{8,0},{9,1},... | collective-permute-start | bytes 393224 | tf_op jit(solution)/shard_map/ppermute | solution.py:596
  35.0 4.2 %far_backward.1 = bf16[32,48,128]{2,1,0:T(8,128)(2,1)} custom-call(s32[96]{0:T(128)} %tile_rows_in.7, s32[384]{0:T(512)} %get-tuple-element.27.plan_in, bf16[96,128,128]{2,1,0:T(8,128)(2,1)S(1)} %copy-done, bf16[2048,512]{1,0:T(8,128)(2,1)} %get-tuple-element.41.grad_agg_in), custom_call_target="tpu_custom_call" | custom-call | flops 4294967296 | bytes 8388608 | tf_op jit(solution)/shard_map/far_backward/pallas_call | solution.py:481
  39.2 0.3 collective-permute-done.1
  39.6 1.0 %collective-permute-start.2 = (bf16[64,512]{1,0:T(8,128)(2,1)S(1)}, bf16[64,512]{1,0:T(8,128)(2,1)S(1)}, u32[]{:S(2)}, u32[]{:S(2)}) collective-permute-start(bf16[64,512]{1,0:T(8,128)(2,1)S(1)} %get-tuple-element.37), channel_id=1, source_target_pairs={{0,16},{1,17},{2,18},{3,19},{4,20},{5,21},{6,22},{7,23},{8,24},{9,... | collective-permute-start | bytes 196616 | tf_op jit(solution)/shard_map/ppermute | solution.py:596
  40.6 5.0 %collective-permute-done.2 = bf16[64,512]{1,0:T(8,128)(2,1)S(1)} collective-permute-done((bf16[64,512]{1,0:T(8,128)(2,1)S(1)}, bf16[64,512]{1,0:T(8,128)(2,1)S(1)}, u32[]{:S(2)}, u32[]{:S(2)}) %collective-permute-start.2) | collective-permute-done | bytes 65568 | tf_op jit(solution)/shard_map/ppermute | solution.py:596
  45.5 0.9 %collective-permute-start.3 = (bf16[64,512]{1,0:T(8,128)(2,1)S(1)}, bf16[64,512]{1,0:T(8,128)(2,1)S(1)}, u32[]{:S(2)}, u32[]{:S(2)}) collective-permute-start(bf16[64,512]{1,0:T(8,128)(2,1)S(1)} %add_convert_fusion.3), channel_id=1, source_target_pairs={{0,2},{1,3},{2,0},{3,1},{4,6},{5,7},{6,4},{7,5},{8,10},{9,11},{10,... | collective-permute-start | bytes 196616 | tf_op jit(solution)/shard_map/ppermute | solution.py:596
  46.4 2.6 %all-to-all-start.1 = ((bf16[32,48,128]{2,1,0:T(8,128)(2,1)}), bf16[32,48,128]{2,1,0:T(8,128)(2,1)S(1)}, u32[]{:S(2)}, u32[]{:S(2)}) async-start(bf16[32,48,128]{2,1,0:T(8,128)(2,1)} %far_backward.1), calls=%async_computation.1 | async-start | bytes 786432 | tf_op jit(solution)/shard_map/all_to_all | solution.py:604
  49.0 0.9 %collective-permute-done.3 = bf16[64,512]{1,0:T(8,128)(2,1)S(1)} collective-permute-done((bf16[64,512]{1,0:T(8,128)(2,1)S(1)}, bf16[64,512]{1,0:T(8,128)(2,1)S(1)}, u32[]{:S(2)}, u32[]{:S(2)}) %collective-permute-start.3) | collective-permute-done | bytes 65568 | tf_op jit(solution)/shard_map/ppermute | solution.py:596
  49.9 1.0 %collective-permute-start.4 = (bf16[64,512]{1,0:T(8,128)(2,1)S(1)}, bf16[64,512]{1,0:T(8,128)(2,1)S(1)}, u32[]{:S(2)}, u32[]{:S(2)}) collective-permute-start(bf16[64,512]{1,0:T(8,128)(2,1)S(1)} %add_convert_fusion.2), channel_id=1, source_target_pairs={{0,4},{1,5},{2,6},{3,7},{4,0},{5,1},{6,2},{7,3},{8,12},{9,13},{10,... | collective-permute-start | bytes 196616 | tf_op jit(solution)/shard_map/ppermute | solution.py:596
  50.9 5.5 %near_backward.1.near = bf16[2048,512]{1,0:T(8,128)(2,1)S(1)} custom-call(s32[96]{0:T(128)} %tile_rows_in.7, s32[384]{0:T(512)} %get-tuple-element.27.plan_in, bf16[96,128,128]{2,1,0:T(8,128)(2,1)} %tiles_in.1, bf16[2048,512]{1,0:T(8,128)(2,1)} %get-tuple-element.41.grad_agg_in), custom_call_target="tpu_custom_call" | custom-call | flops 4294967296 | bytes 8388608 | tf_op jit(solution)/shard_map/near_backward/pallas_call | solution.py:514
  56.5 2.8 %collective-permute-start.5 = (bf16[64,512]{1,0:T(8,128)(2,1)S(1)}, bf16[64,512]{1,0:T(8,128)(2,1)S(1)}, u32[]{:S(2)}, u32[]{:S(2)}) collective-permute-start(bf16[64,512]{1,0:T(8,128)(2,1)S(1)} %add_convert_fusion.1), channel_id=1, source_target_pairs={{0,16},{1,17},{2,18},{3,19},{4,20},{5,21},{6,22},{7,23},{8,24},{9,... | collective-permute-start | bytes 196616 | tf_op jit(solution)/shard_map/ppermute | solution.py:596
  59.3 4.7 %collective-permute-done.5 = bf16[64,512]{1,0:T(8,128)(2,1)S(1)} collective-permute-done((bf16[64,512]{1,0:T(8,128)(2,1)S(1)}, bf16[64,512]{1,0:T(8,128)(2,1)S(1)}, u32[]{:S(2)}, u32[]{:S(2)}) %collective-permute-start.5) | collective-permute-done | bytes 65568 | tf_op jit(solution)/shard_map/ppermute | solution.py:596
  64.0 0.7 collective-permute-start.6
  64.7 3.4 %collect.1 = bf16[2048,512]{1,0:T(8,128)(2,1)} custom-call(bf16[2048,512]{1,0:T(8,128)(2,1)S(1)} %near_backward.1.near, bf16[2048,384]{1,0:T(8,128)(2,1)} %get-tuple-element.47.spread_in, bf16[32,48,128]{2,1,0:T(8,128)(2,1)S(1)} %all-to-all-done.1.returned), custom_call_target="tpu_custom_call" | custom-call | flops 34359738368 | bytes 8388608 | tf_op jit(solution)/shard_map/collect/pallas_call | solution.py:567
  68.1 1.0 %collective-permute-done.6 = bf16[128,512]{1,0:T(8,128)(2,1)S(1)} collective-permute-done((bf16[128,512]{1,0:T(8,128)(2,1)S(1)}, bf16[128,512]{1,0:T(8,128)(2,1)S(1)}, u32[]{:S(2)}, u32[]{:S(2)}) %collective-permute-start.6) | collective-permute-done | bytes 131104 | tf_op jit(solution)/shard_map/ppermute | solution.py:596
  69.2 1.5 %collective-permute-done.7.second = bf16[256,512]{1,0:T(8,128)(2,1)S(1)} collective-permute-done((bf16[256,512]{1,0:T(8,128)(2,1)S(1)}, bf16[256,512]{1,0:T(8,128)(2,1)S(1)}, u32[]{:S(2)}, u32[]{:S(2)}) %collective-permute-start.7) | collective-permute-done | bytes 262176 | tf_op jit(solution)/shard_map/ppermute | solution.py:596
  70.8 1.0 %order.1 = f32[512,512]{1,0:T(8,128)} custom-call(bf16[256,512]{1,0:T(8,128)(2,1)S(1)} %pad_maximum_fusion.first, bf16[256,512]{1,0:T(8,128)(2,1)S(1)} %collective-permute-done.7.second), custom_call_target="tpu_custom_call" | custom-call | tf_op jit(solution)/shard_map/order/pallas_call | solution.py:647
  (13 shorter events, 0.3 us)
Async XLA Ops:
  0.6 10.8 %copy-start = (bf16[96,128,128]{2,1,0:T(8,128)(2,1)S(1)}, bf16[96,128,128]{2,1,0:T(8,128)(2,1)}, u32[]{:S(2)}) copy-start(bf16[96,128,128]{2,1,0:T(8,128)(2,1)} %tiles_in.1) | copy-start | bytes 9437188
  4.1 20.5 %all-to-all-start = ((bf16[32,48,128]{2,1,0:T(8,128)(2,1)}), bf16[32,48,128]{2,1,0:T(8,128)(2,1)S(1)}, u32[]{:S(2)}, u32[]{:S(2)}) async-start(bf16[32,48,128]{2,1,0:T(8,128)(2,1)} %pack_rows.1), calls=%async_computation | async-start | bytes 786432 | tf_op jit(solution)/shard_map/all_to_all | solution.py:604
  32.3 1.6 %collective-permute-start = (bf16[256,512]{1,0:T(8,128)(2,1)S(1)}, bf16[256,512]{1,0:T(8,128)(2,1)S(1)}, u32[]{:S(2)}, u32[]{:S(2)}) collective-permute-start(bf16[256,512]{1,0:T(8,128)(2,1)S(1)} %get-tuple-element.31), channel_id=1, source_target_pairs={{0,1},{1,0},{2,3},{3,2},{4,5},{5,4},{6,7},{7,6},{8,9},{9,8},{10,11... | collective-permute-start | bytes 786440 | tf_op jit(solution)/shard_map/ppermute | solution.py:596
  34.0 5.6 %collective-permute-start.1 = (bf16[128,512]{1,0:T(8,128)(2,1)S(1)}, bf16[128,512]{1,0:T(8,128)(2,1)S(1)}, u32[]{:S(2)}, u32[]{:S(2)}) collective-permute-start(bf16[128,512]{1,0:T(8,128)(2,1)S(1)} %get-tuple-element.34), channel_id=1, source_target_pairs={{0,8},{1,9},{2,10},{3,11},{4,12},{5,13},{6,14},{7,15},{8,0},{9,1},... | collective-permute-start | bytes 393224 | tf_op jit(solution)/shard_map/ppermute | solution.py:596
  39.6 5.9 %collective-permute-start.2 = (bf16[64,512]{1,0:T(8,128)(2,1)S(1)}, bf16[64,512]{1,0:T(8,128)(2,1)S(1)}, u32[]{:S(2)}, u32[]{:S(2)}) collective-permute-start(bf16[64,512]{1,0:T(8,128)(2,1)S(1)} %get-tuple-element.37), channel_id=1, source_target_pairs={{0,16},{1,17},{2,18},{3,19},{4,20},{5,21},{6,22},{7,23},{8,24},{9,... | collective-permute-start | bytes 196616 | tf_op jit(solution)/shard_map/ppermute | solution.py:596
  45.5 4.3 %collective-permute-start.3 = (bf16[64,512]{1,0:T(8,128)(2,1)S(1)}, bf16[64,512]{1,0:T(8,128)(2,1)S(1)}, u32[]{:S(2)}, u32[]{:S(2)}) collective-permute-start(bf16[64,512]{1,0:T(8,128)(2,1)S(1)} %add_convert_fusion.3), channel_id=1, source_target_pairs={{0,2},{1,3},{2,0},{3,1},{4,6},{5,7},{6,4},{7,5},{8,10},{9,11},{10,... | collective-permute-start | bytes 196616 | tf_op jit(solution)/shard_map/ppermute | solution.py:596
  46.4 17.6 %all-to-all-start.1 = ((bf16[32,48,128]{2,1,0:T(8,128)(2,1)}), bf16[32,48,128]{2,1,0:T(8,128)(2,1)S(1)}, u32[]{:S(2)}, u32[]{:S(2)}) async-start(bf16[32,48,128]{2,1,0:T(8,128)(2,1)} %far_backward.1), calls=%async_computation.1 | async-start | bytes 786432 | tf_op jit(solution)/shard_map/all_to_all | solution.py:604
  49.9 6.6 %collective-permute-start.4 = (bf16[64,512]{1,0:T(8,128)(2,1)S(1)}, bf16[64,512]{1,0:T(8,128)(2,1)S(1)}, u32[]{:S(2)}, u32[]{:S(2)}) collective-permute-start(bf16[64,512]{1,0:T(8,128)(2,1)S(1)} %add_convert_fusion.2), channel_id=1, source_target_pairs={{0,4},{1,5},{2,6},{3,7},{4,0},{5,1},{6,2},{7,3},{8,12},{9,13},{10,... | collective-permute-start | bytes 196616 | tf_op jit(solution)/shard_map/ppermute | solution.py:596
  56.5 7.5 %collective-permute-start.5 = (bf16[64,512]{1,0:T(8,128)(2,1)S(1)}, bf16[64,512]{1,0:T(8,128)(2,1)S(1)}, u32[]{:S(2)}, u32[]{:S(2)}) collective-permute-start(bf16[64,512]{1,0:T(8,128)(2,1)S(1)} %add_convert_fusion.1), channel_id=1, source_target_pairs={{0,16},{1,17},{2,18},{3,19},{4,20},{5,21},{6,22},{7,23},{8,24},{9,... | collective-permute-start | bytes 196616 | tf_op jit(solution)/shard_map/ppermute | solution.py:596
  64.0 5.1 %collective-permute-start.6 = (bf16[128,512]{1,0:T(8,128)(2,1)S(1)}, bf16[128,512]{1,0:T(8,128)(2,1)S(1)}, u32[]{:S(2)}, u32[]{:S(2)}) collective-permute-start(bf16[128,512]{1,0:T(8,128)(2,1)S(1)} %pad_maximum_fusion.1), channel_id=1, source_target_pairs={{0,8},{1,9},{2,10},{3,11},{4,12},{5,13},{6,14},{7,15},{8,0},{9,1},... | collective-permute-start | bytes 393224 | tf_op jit(solution)/shard_map/ppermute | solution.py:596
  69.2 1.6 %collective-permute-start.7 = (bf16[256,512]{1,0:T(8,128)(2,1)S(1)}, bf16[256,512]{1,0:T(8,128)(2,1)S(1)}, u32[]{:S(2)}, u32[]{:S(2)}) collective-permute-start(bf16[256,512]{1,0:T(8,128)(2,1)S(1)} %pad_maximum_fusion.first), channel_id=1, source_target_pairs={{0,1},{1,0},{2,3},{3,2},{4,5},{5,4},{6,7},{7,6},{8,9},{9,8},{10,11... | collective-permute-start | bytes 786440 | tf_op jit(solution)/shard_map/ppermute | solution.py:596

commit v3 on v2

--- a/solution.py
+++ b/solution.py
@@ -525,7 +525,7 @@
             DMA((4,)),
         ],
         compiler_params=params(16 << 20),
-        cost_estimate=cost(4 << 30, 8 << 20),
+        cost_estimate=cost(0, 0),
         name="near_backward",
     )(*in_hbm(tile_rows, plan, tiles, grad_agg))
 
@@ -592,8 +592,8 @@
         out[rows_at(mine ^ (b + half), unit), :] = second[spot, :].astype(F32)
 
 
-def exchange(x, n, bit):
-    return lax.ppermute(x, "dom", [(i, i ^ (1 << bit)) for i in range(n)])
+def exchange(x, n, mask):
+    return lax.ppermute(x, "dom", [(i, i ^ mask) for i in range(n)])
 
 
 def tie(*arrays):
@@ -620,30 +620,32 @@
         n, slots, hubs, tile_rows, tile_cols, plan, tile_values, received, near, weight, cotangent
     )
     width = keep.shape[1]
-    keep = keep + exchange(give, n, HALVED[0]).astype(F32)
+    keep = keep + exchange(give, n, 1 << HALVED[0]).astype(F32)
     half = keep.shape[0] // 2
     keep, give, grad_agg = tie(keep[:half].astype(BF16), keep[half:].astype(BF16), grad_agg)
-    got = exchange(give, n, HALVED[1])
+    got = exchange(give, n, 1 << HALVED[1])
     far = far_backward(n, slots, hubs, tile_rows, plan, tile_values, grad_agg)
     half = half // 2
     give = (keep[half:].astype(F32) + got[half:].astype(F32)).astype(BF16)
     keep = (keep[:half].astype(F32) + got[:half].astype(F32)).astype(BF16)
     keep, give, far = tie(keep, give, far)
-    got = exchange(give, n, HALVED[2])
+    got = exchange(give, n, 1 << HALVED[2])
     returned = all_to_all(far)
     held, grad_agg = tie((keep.astype(F32) + got.astype(F32)).astype(BF16), grad_agg)
     for bit in range(n.bit_length() - 1):
         if bit not in HALVED:
-            got = exchange(held, n, bit)
-            if bit == 2:
+            got = exchange(held, n, 1 << bit)
+            held = (held.astype(F32) + got.astype(F32)).astype(BF16)
+            if bit == 1:
                 near_grad = near_backward(tile_rows, plan, tile_values, grad_agg)
-            held, grad_agg = tie((held.astype(F32) + got.astype(F32)).astype(BF16), grad_agg)
-    held, near_grad = tie(held, near_grad)
-    got = exchange(held, n, HALVED[2])
-    held, returned = tie(jnp.concatenate([held, got], axis=0), returned)
-    got = exchange(held, n, HALVED[1])
+                held, near_grad = tie(held, near_grad)
+            else:
+                held = lax.optimization_barrier(held)
+    held, near_grad, returned = tie(held, near_grad, returned)
+    one, other = 1 << HALVED[1], 1 << HALVED[2]
+    parts = [exchange(held, n, mask) for mask in (other, one, one | other)]
     grad_features = collect(n, slots, hubs, near_grad, spread, returned)
-    held, grad_features = tie(jnp.concatenate([held, got], axis=0), grad_features)
+    held, grad_features = tie(jnp.concatenate([held] + parts, axis=0), grad_features)
     grad_weight = pl.pallas_call(
         order_kernel,
         out_shape=jax.ShapeDtypeStruct((width, width), F32),
@@ -651,7 +653,7 @@
         out_specs=VMEM,
         compiler_params=params(4 << 20),
         name="order",
-    )(held, exchange(held, n, HALVED[0]))
+    )(held, exchange(held, n, 1 << HALVED[0]))
     return (output, grad_features, grad_weight)
 
 

time: 72.2 us -> 68.9 us (0.954)
  waiting for transfers between devices: 18.2 us -> 13 us
  starting transfers between devices: 17.4 us -> 19.3 us
    ppermute x8 -> x9, waiting for transfers between devices: 14.9 us -> 9.05 us  [exchange(): return lax.ppermute(x, 'dom', [(i, i ^ mask) for i in range(n)])]
    ppermute x8 -> x9, starting transfers between devices: 7.5 us -> 8.66 us  [exchange(): return lax.ppermute(x, 'dom', [(i, i ^ mask) for i in range(n)])]
    all_to_all x2, starting transfers between devices: 9.91 us -> 10.7 us  [all_to_all(): return lax.all_to_all(x, 'dom', split_axis=0, concat_axis=0, tiled=True)]
  transfers between devices with their start and end apart: 10 -> 11, of which waited for: 8 -> 8; matrix products, arithmetic and copies ran while one was open for 0% -> 0% of each run, Pallas kernels for 32% -> 34%
where the time goes in v3:
time: 68.9 us; the launch traced here: 68.6 us
  Pallas kernels  35.2 us (51%)
  starting transfers between devices  19.3 us (28%)
  waiting for transfers between devices  13 us (19%)
  between operations  0.79 us (1%)
    all_to_all x2, starting transfers between devices, all_to_all(): return lax.all_to_all(x, 'dom', split_axis=0, concat_axis=0, tiled=True)  10.7 us
    pallas_call x1, Pallas kernels, near_forward(): pl.pallas_call(functools.partial(near_forward_kernel, n, slots, hubs), ou...  9.89 us
    ppermute x9, waiting for transfers between devices, exchange(): return lax.ppermute(x, 'dom', [(i, i ^ mask) for i in range(n)])  9.05 us
    ppermute x9, starting transfers between devices, exchange(): return lax.ppermute(x, 'dom', [(i, i ^ mask) for i in range(n)])  8.66 us
    pallas_call x1, Pallas kernels, forward(): pl.pallas_call(functools.partial(forward_kernel, n, slots, hubs), out_sha...  7.64 us
    pallas_call x1, Pallas kernels, near_backward(): pl.pallas_call(near_backward_kernel, out_shape=pltpu.VMEM(grad_agg.shape,...  5.55 us
    pallas_call x1, Pallas kernels, far_backward(): pl.pallas_call(functools.partial(far_backward_kernel, n, slots, hubs), ou...  4.18 us
    all_to_all x2, waiting for transfers between devices, all_to_all(): return lax.all_to_all(x, 'dom', split_axis=0, concat_axis=0, tiled=True)  3.99 us
  transfers between devices with their start and end apart: 11, of which 8 were waited for; matrix products, arithmetic and copies ran while one was open for 0% of the time, Pallas kernels for 34%

profile of v3, /device:TPU:0, one launch (start us, length us, event | category | flops | bytes accessed | tf_op | source)
XLA Modules:
  0.0 68.6 jit_solution(5788798762804841754)
XLA Ops:
  0.6 3.5 %pack_rows.1 = bf16[32,48,128]{2,1,0:T(8,128)(2,1)} custom-call(s32[1,8,32]{2,1,0:T(8,128)} %bitcast.1, s32[1,32]{1,0:T(1,128)} %send_count_in.3, s32[4]{0:T(128)} %hub_rows_in.3, bf16[2048,512]{1,0:T(8,128)(2,1)} %feats_in.3), custom_call_target="tpu_custom_call" | custom-call | tf_op jit(solution)/shard_map/pack_rows/pallas_call | solution.py:129
  4.1 7.3 %all-to-all-start = ((bf16[32,48,128]{2,1,0:T(8,128)(2,1)}), bf16[32,48,128]{2,1,0:T(8,128)(2,1)S(1)}, u32[]{:S(2)}, u32[]{:S(2)}) async-start(bf16[32,48,128]{2,1,0:T(8,128)(2,1)} %pack_rows.1), calls=%async_computation | async-start | bytes 786432 | tf_op jit(solution)/shard_map/all_to_all | solution.py:604
  11.4 9.9 %near_forward.1 = (f32[2048,512]{1,0:T(8,128)}, s32[384]{0:T(512)}, bf16[2048,384]{1,0:T(8,128)(2,1)}) custom-call(s32[96]{0:T(128)} %tile_rows_in.7, s32[96]{0:T(128)} %tile_cols_in.3, s32[1,8,32]{2,1,0:T(8,128)} %bitcast.2, s32[1,32]{1,0:T(1,128)} %send_count_in.3, s32[4]{0:T(128)} %hub_rows_in.3, bf16[96,128,128]{2,1,0:T(8,128)(2,1)S(1)} %copy-done, ...), custom_call_target="tpu_custom_call" | custom-call | flops 4294967296 | bytes 8388608 | tf_op jit(solution)/shard_map/near_forward/pallas_call | solution.py:275
  21.3 3.3 %all-to-all-done.received = bf16[32,48,128]{2,1,0:T(8,128)(2,1)S(1)} async-done(((bf16[32,48,128]{2,1,0:T(8,128)(2,1)}), bf16[32,48,128]{2,1,0:T(8,128)(2,1)S(1)}, u32[]{:S(2)}, u32[]{:S(2)}) %all-to-all-start) | async-done | bytes 393248 | tf_op jit(solution)/shard_map/all_to_all | solution.py:604
  24.6 7.6 %forward.1 = (bf16[2048,512]{1,0:T(8,128)(2,1)}, bf16[2048,512]{1,0:T(8,128)(2,1)}, f32[256,512]{1,0:T(8,128)S(1)}, bf16[256,512]{1,0:T(8,128)(2,1)S(1)}) custom-call(s32[96]{0:T(128)} %tile_rows_in.7, s32[96]{0:T(128)} %tile_cols_in.3, s32[384]{0:T(512)} %get-tuple-element.25.plan_in, bf16[96,128,128]{2,1,0:T(8,128)(2,1)S(1)} %copy-done, ...), custom_call_target="tpu_custom_call" | custom-call | flops 8589934592 | bytes 16777216 | tf_op jit(solution)/shard_map/forward/pallas_call | solution.py:413
  32.3 0.1 collective-permute-start
  32.3 1.5 %collective-permute-done = bf16[256,512]{1,0:T(8,128)(2,1)S(1)} collective-permute-done((bf16[256,512]{1,0:T(8,128)(2,1)S(1)}, bf16[256,512]{1,0:T(8,128)(2,1)S(1)}, u32[]{:S(2)}, u32[]{:S(2)}) %collective-permute-start) | collective-permute-done | bytes 262176 | tf_op jit(solution)/shard_map/ppermute | solution.py:596
  34.0 1.1 %collective-permute-start.1 = (bf16[128,512]{1,0:T(8,128)(2,1)S(1)}, bf16[128,512]{1,0:T(8,128)(2,1)S(1)}, u32[]{:S(2)}, u32[]{:S(2)}) collective-permute-start(bf16[128,512]{1,0:T(8,128)(2,1)S(1)} %get-tuple-element.32), channel_id=1, source_target_pairs={{0,8},{1,9},{2,10},{3,11},{4,12},{5,13},{6,14},{7,15},{8,0},{9,1},... | collective-permute-start | bytes 393224 | tf_op jit(solution)/shard_map/ppermute | solution.py:596
  35.0 4.2 %far_backward.1 = bf16[32,48,128]{2,1,0:T(8,128)(2,1)} custom-call(s32[96]{0:T(128)} %tile_rows_in.7, s32[384]{0:T(512)} %get-tuple-element.25.plan_in, bf16[96,128,128]{2,1,0:T(8,128)(2,1)S(1)} %copy-done, bf16[2048,512]{1,0:T(8,128)(2,1)} %get-tuple-element.37.grad_agg_in), custom_call_target="tpu_custom_call" | custom-call | flops 4294967296 | bytes 8388608 | tf_op jit(solution)/shard_map/far_backward/pallas_call | solution.py:481
  39.2 0.3 collective-permute-done.1
  39.6 1.0 %collective-permute-start.2 = (bf16[64,512]{1,0:T(8,128)(2,1)S(1)}, bf16[64,512]{1,0:T(8,128)(2,1)S(1)}, u32[]{:S(2)}, u32[]{:S(2)}) collective-permute-start(bf16[64,512]{1,0:T(8,128)(2,1)S(1)} %get-tuple-element.35), channel_id=1, source_target_pairs={{0,16},{1,17},{2,18},{3,19},{4,20},{5,21},{6,22},{7,23},{8,24},{9,... | collective-permute-start | bytes 196616 | tf_op jit(solution)/shard_map/ppermute | solution.py:596
  40.6 3.4 %all-to-all-start.1 = ((bf16[32,48,128]{2,1,0:T(8,128)(2,1)}), bf16[32,48,128]{2,1,0:T(8,128)(2,1)S(1)}, u32[]{:S(2)}, u32[]{:S(2)}) async-start(bf16[32,48,128]{2,1,0:T(8,128)(2,1)} %far_backward.1), calls=%async_computation.1 | async-start | bytes 786432 | tf_op jit(solution)/shard_map/all_to_all | solution.py:604
  43.9 1.6 %collective-permute-done.2 = bf16[64,512]{1,0:T(8,128)(2,1)S(1)} collective-permute-done((bf16[64,512]{1,0:T(8,128)(2,1)S(1)}, bf16[64,512]{1,0:T(8,128)(2,1)S(1)}, u32[]{:S(2)}, u32[]{:S(2)}) %collective-permute-start.2) | collective-permute-done | bytes 65568 | tf_op jit(solution)/shard_map/ppermute | solution.py:596
  45.5 0.9 %collective-permute-start.3 = (bf16[64,512]{1,0:T(8,128)(2,1)S(1)}, bf16[64,512]{1,0:T(8,128)(2,1)S(1)}, u32[]{:S(2)}, u32[]{:S(2)}) collective-permute-start(bf16[64,512]{1,0:T(8,128)(2,1)S(1)} %add_convert_fusion.3), channel_id=1, source_target_pairs={{0,2},{1,3},{2,0},{3,1},{4,6},{5,7},{6,4},{7,5},{8,10},{9,11},{10,... | collective-permute-start | bytes 196616 | tf_op jit(solution)/shard_map/ppermute | solution.py:596
  46.4 5.5 %near_backward.1.near = bf16[2048,512]{1,0:T(8,128)(2,1)S(1)} custom-call(s32[96]{0:T(128)} %tile_rows_in.7, s32[384]{0:T(512)} %get-tuple-element.25.plan_in, bf16[96,128,128]{2,1,0:T(8,128)(2,1)} %tiles_in.1, bf16[2048,512]{1,0:T(8,128)(2,1)} %get-tuple-element.37.grad_agg_in), custom_call_target="tpu_custom_call" | custom-call | tf_op jit(solution)/shard_map/near_backward/pallas_call | solution.py:514
  52.0 1.2 %collective-permute-start.4 = (bf16[64,512]{1,0:T(8,128)(2,1)S(1)}, bf16[64,512]{1,0:T(8,128)(2,1)S(1)}, u32[]{:S(2)}, u32[]{:S(2)}) collective-permute-start(bf16[64,512]{1,0:T(8,128)(2,1)S(1)} %add_convert_fusion.2), channel_id=1, source_target_pairs={{0,4},{1,5},{2,6},{3,7},{4,0},{5,1},{6,2},{7,3},{8,12},{9,13},{10,... | collective-permute-start | bytes 196616 | tf_op jit(solution)/shard_map/ppermute | solution.py:596
  53.2 3.1 %collective-permute-done.4 = bf16[64,512]{1,0:T(8,128)(2,1)S(1)} collective-permute-done((bf16[64,512]{1,0:T(8,128)(2,1)S(1)}, bf16[64,512]{1,0:T(8,128)(2,1)S(1)}, u32[]{:S(2)}, u32[]{:S(2)}) %collective-permute-start.4) | collective-permute-done | bytes 65568 | tf_op jit(solution)/shard_map/ppermute | solution.py:596
  56.4 0.7 %all-to-all-done.1.returned = bf16[32,48,128]{2,1,0:T(8,128)(2,1)S(1)} async-done(((bf16[32,48,128]{2,1,0:T(8,128)(2,1)}), bf16[32,48,128]{2,1,0:T(8,128)(2,1)S(1)}, u32[]{:S(2)}, u32[]{:S(2)}) %all-to-all-start.1) | async-done | bytes 393248 | tf_op jit(solution)/shard_map/all_to_all | solution.py:604
  57.1 2.0 %collective-permute-start.7 = (bf16[64,512]{1,0:T(8,128)(2,1)S(1)}, bf16[64,512]{1,0:T(8,128)(2,1)S(1)}, u32[]{:S(2)}, u32[]{:S(2)}) collective-permute-start(bf16[64,512]{1,0:T(8,128)(2,1)S(1)} %add_convert_fusion.1), channel_id=1, source_target_pairs={{0,24},{1,25},{2,26},{3,27},{4,28},{5,29},{6,30},{7,31},{8,16},{9,... | collective-permute-start | bytes 196616 | tf_op jit(solution)/shard_map/ppermute | solution.py:596
  59.1 2.3 %collective-permute-start.5 = (bf16[64,512]{1,0:T(8,128)(2,1)S(1)}, bf16[64,512]{1,0:T(8,128)(2,1)S(1)}, u32[]{:S(2)}, u32[]{:S(2)}) collective-permute-start(bf16[64,512]{1,0:T(8,128)(2,1)S(1)} %add_convert_fusion.1), channel_id=1, source_target_pairs={{0,16},{1,17},{2,18},{3,19},{4,20},{5,21},{6,22},{7,23},{8,24},{9,... | collective-permute-start | bytes 196616 | tf_op jit(solution)/shard_map/ppermute | solution.py:596
  61.5 3.4 %collect.1 = bf16[2048,512]{1,0:T(8,128)(2,1)} custom-call(bf16[2048,512]{1,0:T(8,128)(2,1)S(1)} %near_backward.1.near, bf16[2048,384]{1,0:T(8,128)(2,1)} %get-tuple-element.43.spread_in, bf16[32,48,128]{2,1,0:T(8,128)(2,1)S(1)} %all-to-all-done.1.returned), custom_call_target="tpu_custom_call" | custom-call | flops 34359738368 | bytes 8388608 | tf_op jit(solution)/shard_map/collect/pallas_call | solution.py:567
  65.0 0.9 %collective-permute-done.5 = bf16[64,512]{1,0:T(8,128)(2,1)S(1)} collective-permute-done((bf16[64,512]{1,0:T(8,128)(2,1)S(1)}, bf16[64,512]{1,0:T(8,128)(2,1)S(1)}, u32[]{:S(2)}, u32[]{:S(2)}) %collective-permute-start.5) | collective-permute-done | bytes 65568 | tf_op jit(solution)/shard_map/ppermute | solution.py:596
  66.0 1.5 %collective-permute-done.8.second = bf16[256,512]{1,0:T(8,128)(2,1)S(1)} collective-permute-done((bf16[256,512]{1,0:T(8,128)(2,1)S(1)}, bf16[256,512]{1,0:T(8,128)(2,1)S(1)}, u32[]{:S(2)}, u32[]{:S(2)}) %collective-permute-start.8) | collective-permute-done | bytes 262176 | tf_op jit(solution)/shard_map/ppermute | solution.py:596
  67.5 1.0 %order.1 = f32[512,512]{1,0:T(8,128)} custom-call(bf16[256,512]{1,0:T(8,128)(2,1)S(1)} %pad_maximum_fusion.first, bf16[256,512]{1,0:T(8,128)(2,1)S(1)} %collective-permute-done.8.second), custom_call_target="tpu_custom_call" | custom-call | tf_op jit(solution)/shard_map/order/pallas_call | solution.py:649
  (14 shorter events, 0.3 us)
Async XLA Ops:
  0.6 10.8 %copy-start = (bf16[96,128,128]{2,1,0:T(8,128)(2,1)S(1)}, bf16[96,128,128]{2,1,0:T(8,128)(2,1)}, u32[]{:S(2)}) copy-start(bf16[96,128,128]{2,1,0:T(8,128)(2,1)} %tiles_in.1) | copy-start | bytes 9437188
  4.1 20.5 %all-to-all-start = ((bf16[32,48,128]{2,1,0:T(8,128)(2,1)}), bf16[32,48,128]{2,1,0:T(8,128)(2,1)S(1)}, u32[]{:S(2)}, u32[]{:S(2)}) async-start(bf16[32,48,128]{2,1,0:T(8,128)(2,1)} %pack_rows.1), calls=%async_computation | async-start | bytes 786432 | tf_op jit(solution)/shard_map/all_to_all | solution.py:604
  32.3 1.6 %collective-permute-start = (bf16[256,512]{1,0:T(8,128)(2,1)S(1)}, bf16[256,512]{1,0:T(8,128)(2,1)S(1)}, u32[]{:S(2)}, u32[]{:S(2)}) collective-permute-start(bf16[256,512]{1,0:T(8,128)(2,1)S(1)} %get-tuple-element.29), channel_id=1, source_target_pairs={{0,1},{1,0},{2,3},{3,2},{4,5},{5,4},{6,7},{7,6},{8,9},{9,8},{10,11... | collective-permute-start | bytes 786440 | tf_op jit(solution)/shard_map/ppermute | solution.py:596
  34.0 5.6 %collective-permute-start.1 = (bf16[128,512]{1,0:T(8,128)(2,1)S(1)}, bf16[128,512]{1,0:T(8,128)(2,1)S(1)}, u32[]{:S(2)}, u32[]{:S(2)}) collective-permute-start(bf16[128,512]{1,0:T(8,128)(2,1)S(1)} %get-tuple-element.32), channel_id=1, source_target_pairs={{0,8},{1,9},{2,10},{3,11},{4,12},{5,13},{6,14},{7,15},{8,0},{9,1},... | collective-permute-start | bytes 393224 | tf_op jit(solution)/shard_map/ppermute | solution.py:596
  39.6 5.9 %collective-permute-start.2 = (bf16[64,512]{1,0:T(8,128)(2,1)S(1)}, bf16[64,512]{1,0:T(8,128)(2,1)S(1)}, u32[]{:S(2)}, u32[]{:S(2)}) collective-permute-start(bf16[64,512]{1,0:T(8,128)(2,1)S(1)} %get-tuple-element.35), channel_id=1, source_target_pairs={{0,16},{1,17},{2,18},{3,19},{4,20},{5,21},{6,22},{7,23},{8,24},{9,... | collective-permute-start | bytes 196616 | tf_op jit(solution)/shard_map/ppermute | solution.py:596
  40.6 16.5 %all-to-all-start.1 = ((bf16[32,48,128]{2,1,0:T(8,128)(2,1)}), bf16[32,48,128]{2,1,0:T(8,128)(2,1)S(1)}, u32[]{:S(2)}, u32[]{:S(2)}) async-start(bf16[32,48,128]{2,1,0:T(8,128)(2,1)} %far_backward.1), calls=%async_computation.1 | async-start | bytes 786432 | tf_op jit(solution)/shard_map/all_to_all | solution.py:604
  45.5 6.4 %collective-permute-start.3 = (bf16[64,512]{1,0:T(8,128)(2,1)S(1)}, bf16[64,512]{1,0:T(8,128)(2,1)S(1)}, u32[]{:S(2)}, u32[]{:S(2)}) collective-permute-start(bf16[64,512]{1,0:T(8,128)(2,1)S(1)} %add_convert_fusion.3), channel_id=1, source_target_pairs={{0,2},{1,3},{2,0},{3,1},{4,6},{5,7},{6,4},{7,5},{8,10},{9,11},{10,... | collective-permute-start | bytes 196616 | tf_op jit(solution)/shard_map/ppermute | solution.py:596
  52.0 4.3 %collective-permute-start.4 = (bf16[64,512]{1,0:T(8,128)(2,1)S(1)}, bf16[64,512]{1,0:T(8,128)(2,1)S(1)}, u32[]{:S(2)}, u32[]{:S(2)}) collective-permute-start(bf16[64,512]{1,0:T(8,128)(2,1)S(1)} %add_convert_fusion.2), channel_id=1, source_target_pairs={{0,4},{1,5},{2,6},{3,7},{4,0},{5,1},{6,2},{7,3},{8,12},{9,13},{10,... | collective-permute-start | bytes 196616 | tf_op jit(solution)/shard_map/ppermute | solution.py:596
  57.1 7.8 %collective-permute-start.7 = (bf16[64,512]{1,0:T(8,128)(2,1)S(1)}, bf16[64,512]{1,0:T(8,128)(2,1)S(1)}, u32[]{:S(2)}, u32[]{:S(2)}) collective-permute-start(bf16[64,512]{1,0:T(8,128)(2,1)S(1)} %add_convert_fusion.1), channel_id=1, source_target_pairs={{0,24},{1,25},{2,26},{3,27},{4,28},{5,29},{6,30},{7,31},{8,16},{9,... | collective-permute-start | bytes 196616 | tf_op jit(solution)/shard_map/ppermute | solution.py:596
  59.1 5.8 %collective-permute-start.6 = (bf16[64,512]{1,0:T(8,128)(2,1)S(1)}, bf16[64,512]{1,0:T(8,128)(2,1)S(1)}, u32[]{:S(2)}, u32[]{:S(2)}) collective-permute-start(bf16[64,512]{1,0:T(8,128)(2,1)S(1)} %add_convert_fusion.1), channel_id=1, source_target_pairs={{0,8},{1,9},{2,10},{3,11},{4,12},{5,13},{6,14},{7,15},{8,0},{9,1},... | collective-permute-start | bytes 196616 | tf_op jit(solution)/shard_map/ppermute | solution.py:596
  59.1 6.7 %collective-permute-start.5 = (bf16[64,512]{1,0:T(8,128)(2,1)S(1)}, bf16[64,512]{1,0:T(8,128)(2,1)S(1)}, u32[]{:S(2)}, u32[]{:S(2)}) collective-permute-start(bf16[64,512]{1,0:T(8,128)(2,1)S(1)} %add_convert_fusion.1), channel_id=1, source_target_pairs={{0,16},{1,17},{2,18},{3,19},{4,20},{5,21},{6,22},{7,23},{8,24},{9,... | collective-permute-start | bytes 196616 | tf_op jit(solution)/shard_map/ppermute | solution.py:596
  65.9 1.6 %collective-permute-start.8 = (bf16[256,512]{1,0:T(8,128)(2,1)S(1)}, bf16[256,512]{1,0:T(8,128)(2,1)S(1)}, u32[]{:S(2)}, u32[]{:S(2)}) collective-permute-start(bf16[256,512]{1,0:T(8,128)(2,1)S(1)} %pad_maximum_fusion.first), channel_id=1, source_target_pairs={{0,1},{1,0},{2,3},{3,2},{4,5},{5,4},{6,7},{7,6},{8,9},{9,8},{10,11... | collective-permute-start | bytes 786440 | tf_op jit(solution)/shard_map/ppermute | solution.py:596

commit v4 on v3

--- a/solution.py
+++ b/solution.py
@@ -13,8 +13,8 @@
 NONE = 255
 KEYS = 32
 LIST = 64
-UNROLL = 4
-HALVED = (0, 3, 4)
+UNROLL = 8
+HALVED = (0, 2, 1)
 NEAR_FWD, FAR_FWD, NEAR_BWD, FAR_BWD = range(4)
 COUNTS = 4 * LIST
 PLAN = COUNTS + LANES
@@ -52,7 +52,7 @@
 
 def pack_kernel(
     n, slots, hubs, send_rows_in, send_count_in, hub_rows_in, feats_in, out,
-    send_rows, send_count, hub_rows, feats, select, staged, sems, out_sems,
+    send_rows, send_count, hub_rows, feats, select, found, staged, sems, feat_sems, out_sems,
 ):
     rows, width = feats.shape
     chunks = width // LANES
@@ -63,13 +63,14 @@
                 (send_rows_in, send_rows),
                 (send_count_in, send_count),
                 (hub_rows_in, hub_rows),
-                (feats_in, feats),
             )
         )
     ]
+    pieces = [slice(at, at + rows // 2) for at in range(0, rows, rows // 2)]
+    arrivals = [start(feats_in.at[at], feats.at[at], feat_sems.at[k]) for k, at in enumerate(pieces)]
     sub = lax.broadcasted_iota(I32, (2 * slots, LANES), 0)
     lane = lax.broadcasted_iota(I32, (2 * slots, LANES), 1)
-    for copy in copies[:3]:
+    for copy in copies:
         copy.wait()
 
     def put(at, column):
@@ -94,23 +95,22 @@
         return 0
 
     lax.fori_loop(0, n // 2, pair, 0, unroll=2)
-    copies[3].wait()
     group = sub // hubs
-    found = jnp.dot(select[0 : 2 * slots, :], feats[...], preferred_element_type=F32)
+    for k, at in enumerate(pieces):
+        arrivals[k].wait()
+        part = jnp.dot(select[:, at], feats[at, :], preferred_element_type=F32)
+        found[...] = part if k == 0 else found[...] + part
     hub = jnp.zeros((hubs * chunks, LANES), F32)
     for c in range(chunks):
-        hub = jnp.where(group == c, found[:, c * LANES : (c + 1) * LANES], hub)
+        hub = jnp.where(group == c, found[0 : 2 * slots, c * LANES : (c + 1) * LANES], hub)
     hub = hub.astype(BF16)
     per = LANES // slots
     sent = []
     for b in range(n // per):
-        got = jnp.dot(
-            select[b * LANES + 2 * slots : (b + 1) * LANES + 2 * slots, :], feats[...], preferred_element_type=F32
-        )
         for s in range(per):
             dest = b * per + s
             staged[dest, 0:SUBS, :] = hub
-            mine = got[s * slots : (s + 1) * slots, :]
+            mine = found[2 * slots + dest * slots : 2 * slots + (dest + 1) * slots, :]
             for c in range(0, chunks, 2):
                 both = jnp.concatenate(
                     [mine[:, c * LANES : (c + 1) * LANES], mine[:, (c + 1) * LANES : (c + 2) * LANES]], axis=0
@@ -137,8 +137,10 @@
             pltpu.SMEM(hub_rows.shape, I32),
             pltpu.VMEM((rows, width), BF16),
             pltpu.VMEM((n * slots + 2 * slots, rows), BF16),
+            pltpu.VMEM((n * slots + 2 * slots, width), F32),
             pltpu.VMEM(packed, BF16),
-            DMA((4,)),
+            DMA((3,)),
+            DMA((2,)),
             DMA((n * slots // LANES,)),
         ],
         compiler_params=params(16 << 20),
@@ -320,6 +322,25 @@
     lax.fori_loop(0, n // 2, pair, 0, unroll=4)
 
 
+def pack_grads(n, slots, hubs, chunks, total, staged):
+    def two(q, _):
+        both = total[rows_at(q, 2 * hubs), :]
+        for u in range(2):
+            mine = both[u * hubs : (u + 1) * hubs]
+            staged[2 * q + u, 0:SUBS, :] = jnp.concatenate(
+                [mine[:, c * LANES : (c + 1) * LANES] for c in range(chunks)], axis=0
+            ).astype(BF16)
+            halo = total[pl.ds(pl.multiple_of(n * hubs + (2 * q + u) * slots, slots), slots), :]
+            for c in range(0, chunks, 2):
+                pair = jnp.concatenate(
+                    [halo[:, c * LANES : (c + 1) * LANES], halo[:, (c + 1) * LANES : (c + 2) * LANES]], axis=0
+                )
+                staged[2 * q + u, SUBS + c * slots : SUBS + (c + 2) * slots, :] = pair.astype(BF16)
+        return 0
+
+    lax.fori_loop(0, n // 2, two, 0, unroll=2)
+
+
 def place():
     device = lax.axis_index("dom")
     out = jnp.zeros((), I32)
@@ -330,8 +351,8 @@
 
 def forward_kernel(
     n, slots, hubs, tile_rows_in, tile_cols_in, plan_in, tiles, received, near_in, weight_in, cot_in,
-    output, grad_agg_out, keep, give,
-    tile_rows, tile_cols, plan, table, total, near, weight, cot, agg, grad_pre, grad_agg, out, sems, near_sems, cot_sems, out_sems, ga_sems,
+    output, grad_agg_out, far_out, keep, give,
+    tile_rows, tile_cols, plan, table, total, far_total, staged, near, weight, cot, agg, grad_pre, grad_agg, out, sems, near_sems, cot_sems, out_sems, ga_sems,
 ):
     size = tiles.shape[1]
     rows, width = near.shape
@@ -350,6 +371,7 @@
         for b, at in enumerate(pieces)
     ]
     total[...] = jnp.zeros_like(total)
+    far_total[...] = jnp.zeros_like(far_total)
 
     def four(q, _):
         parts = [received[4 * q + u, 0:SUBS, :].astype(F32) for u in range(4)]
@@ -364,9 +386,11 @@
         copy.wait()
     run_plan(FAR_FWD, plan, tiles, lambda t: jnp.maximum(tile_cols[t] - blocks, 0), table, total, False)
     weight_copy.wait()
-    for pair in arrivals:
-        for copy in pair:
-            copy.wait()
+
+    def arrive(blocks_of):
+        for pair in arrivals[blocks_of]:
+            for copy in pair:
+                copy.wait()
 
     def first(at):
         here = (total[at, :] + near[at, :]).astype(BF16)
@@ -374,8 +398,11 @@
         return jnp.dot(here, weight[...], preferred_element_type=F32)
 
     sent = []
+    arrive(slice(0, steps // 2))
     pre = first(pieces[0])
     for b, at in enumerate(pieces):
+        if b + 1 == steps // 2:
+            arrive(slice(steps // 2, steps))
         following = first(pieces[b + 1]) if b + 1 < steps else None
         sig = 0.5 * jnp.tanh(0.5 * pre) + 0.5
         out[at, :] = (pre * sig).astype(BF16)
@@ -387,6 +414,9 @@
         sent.append(start(out.at[at], output.at[at], out_sems.at[b]))
         sent.append(start(grad_agg.at[at], grad_agg_out.at[at], ga_sems.at[b]))
         pre = following
+    run_plan(FAR_BWD, plan, tiles, lambda t: tile_rows[t], grad_agg, far_total, True)
+    pack_grads(n, slots, hubs, chunks, far_total, staged)
+    sent.append(start(staged, far_out, sems.at[0]))
     scale = float(rows * n) ** -0.5
     term = total.at[pl.ds(0, width)]
     for c in range(0, width, 256):
@@ -409,23 +439,27 @@
 
 def forward(n, slots, hubs, tile_rows, tile_cols, plan, tiles, received, near, weight, cotangent):
     rows, width = near.shape
+    packed = (n, (slots + hubs) * width // LANES, LANES)
     steps = rows // 256
     return pl.pallas_call(
         functools.partial(forward_kernel, n, slots, hubs),
         out_shape=(
             pltpu.HBM((rows, width), BF16),
             pltpu.HBM((rows, width), BF16),
+            pltpu.HBM(packed, BF16),
             pltpu.VMEM((width // 2, width), F32),
             pltpu.VMEM((width // 2, width), BF16),
         ),
         in_specs=[HBM, HBM, HBM, VMEM, VMEM, HBM, HBM, HBM],
-        out_specs=(HBM, HBM, VMEM, VMEM),
+        out_specs=(HBM, HBM, HBM, VMEM, VMEM),
         scratch_shapes=[
             pltpu.SMEM(tile_rows.shape, I32),
             pltpu.SMEM(tile_cols.shape, I32),
             pltpu.SMEM((PLAN,), I32),
             pltpu.VMEM((n * (slots + hubs), width), BF16),
             pltpu.VMEM((rows, width), F32),
+            pltpu.VMEM((n * (slots + hubs), width), F32),
+            pltpu.VMEM(packed, BF16),
             pltpu.VMEM((rows, width), F32),
             pltpu.VMEM((width, width), BF16),
             pltpu.VMEM((rows, width), BF16),
@@ -443,58 +477,6 @@
         cost_estimate=cost(8 << 30, 16 << 20),
         name="forward",
     )(*in_hbm(tile_rows, tile_cols, plan), *in_vmem(tiles, received), *in_hbm(near, weight, cotangent))
-
-
-def far_backward_kernel(
-    n, slots, hubs, tile_rows_in, plan_in, tiles, grad_agg_in, out, tile_rows, plan, grad_agg, total, staged, sems
-):
-    chunks = grad_agg.shape[1] // LANES
-    moves = ((plan_in, plan), (tile_rows_in, tile_rows), (grad_agg_in, grad_agg))
-    copies = [start(a, b, sems.at[i]) for i, (a, b) in enumerate(moves)]
-    total[...] = jnp.zeros_like(total)
-    for copy in copies:
-        copy.wait()
-    run_plan(FAR_BWD, plan, tiles, lambda t: tile_rows[t], grad_agg, total, True)
-
-    def two(q, _):
-        both = total[rows_at(q, 2 * hubs), :]
-        for u in range(2):
-            mine = both[u * hubs : (u + 1) * hubs]
-            staged[2 * q + u, 0:SUBS, :] = jnp.concatenate(
-                [mine[:, c * LANES : (c + 1) * LANES] for c in range(chunks)], axis=0
-            ).astype(BF16)
-            halo = total[pl.ds(pl.multiple_of(n * hubs + (2 * q + u) * slots, slots), slots), :]
-            for c in range(0, chunks, 2):
-                pair = jnp.concatenate(
-                    [halo[:, c * LANES : (c + 1) * LANES], halo[:, (c + 1) * LANES : (c + 2) * LANES]], axis=0
-                )
-                staged[2 * q + u, SUBS + c * slots : SUBS + (c + 2) * slots, :] = pair.astype(BF16)
-        return 0
-
-    lax.fori_loop(0, n // 2, two, 0, unroll=2)
-    start(staged, out, sems.at[0]).wait()
-
-
-def far_backward(n, slots, hubs, tile_rows, plan, tiles, grad_agg):
-    width = grad_agg.shape[1]
-    packed = (n, (slots + hubs) * width // LANES, LANES)
-    return pl.pallas_call(
-        functools.partial(far_backward_kernel, n, slots, hubs),
-        out_shape=pltpu.HBM(packed, BF16),
-        in_specs=[HBM, HBM, VMEM, HBM],
-        out_specs=HBM,
-        scratch_shapes=[
-            pltpu.SMEM(tile_rows.shape, I32),
-            pltpu.SMEM((PLAN,), I32),
-            pltpu.VMEM(grad_agg.shape, BF16),
-            pltpu.VMEM((n * (slots + hubs), width), F32),
-            pltpu.VMEM(packed, BF16),
-            DMA((3,)),
-        ],
-        compiler_params=params(12 << 20),
-        cost_estimate=cost(4 << 30, 8 << 20),
-        name="far_backward",
-    )(*in_hbm(tile_rows, plan), *in_vmem(tiles), *in_hbm(grad_agg))
 
 
 def near_backward_kernel(
@@ -609,6 +591,7 @@
 ):
     n = lax.axis_size("dom")
     slots, hubs = send_rows.shape[2], hub_rows.shape[0]
+    width = features.shape[1]
     send_rows = jnp.swapaxes(send_rows, 1, 2)
 
     packed = pack_rows(n, send_rows, send_count, hub_rows, features)
@@ -616,33 +599,24 @@
     near, plan, spread = near_forward(
         n, tile_rows, tile_cols, send_rows, send_count, hub_rows, tile_values, features
     )
-    output, grad_agg, keep, give = forward(
+    output, grad_agg, far, keep, give = forward(
         n, slots, hubs, tile_rows, tile_cols, plan, tile_values, received, near, weight, cotangent
     )
-    width = keep.shape[1]
-    keep = keep + exchange(give, n, 1 << HALVED[0]).astype(F32)
-    half = keep.shape[0] // 2
-    keep, give, grad_agg = tie(keep[:half].astype(BF16), keep[half:].astype(BF16), grad_agg)
-    got = exchange(give, n, 1 << HALVED[1])
-    far = far_backward(n, slots, hubs, tile_rows, plan, tile_values, grad_agg)
-    half = half // 2
-    give = (keep[half:].astype(F32) + got[half:].astype(F32)).astype(BF16)
-    keep = (keep[:half].astype(F32) + got[:half].astype(F32)).astype(BF16)
-    keep, give, far = tie(keep, give, far)
-    got = exchange(give, n, 1 << HALVED[2])
+    core, one, other = (1 << bit for bit in HALVED)
+    got = exchange(give, n, core)
+    quarters = (keep + got.astype(F32)).astype(BF16).reshape(4, keep.shape[0] // 4, width)
+    *quarters, far, grad_agg = tie(*(quarters[i] for i in range(4)), far, grad_agg)
+    parts = [quarters[0]] + [exchange(quarters[i], n, mask) for i, mask in ((1, other), (2, one), (3, one | other))]
     returned = all_to_all(far)
-    held, grad_agg = tie((keep.astype(F32) + got.astype(F32)).astype(BF16), grad_agg)
-    for bit in range(n.bit_length() - 1):
-        if bit not in HALVED:
-            got = exchange(held, n, 1 << bit)
-            held = (held.astype(F32) + got.astype(F32)).astype(BF16)
-            if bit == 1:
-                near_grad = near_backward(tile_rows, plan, tile_values, grad_agg)
-                held, near_grad = tie(held, near_grad)
-            else:
-                held = lax.optimization_barrier(held)
+    a, b, c, d = (part.astype(F32) for part in parts)
+    near_grad = near_backward(tile_rows, plan, tile_values, grad_agg)
+    held, near_grad = tie(((a + b) + (c + d)).astype(BF16), near_grad)
+    parts = [held] + [exchange(held, n, mask) for mask in (8, 16, 24)]
+    a, b, c, d = (part.astype(F32) for part in parts)
+    held = lax.optimization_barrier(((a + b) + (c + d)).astype(BF16))
+    for bit in range(5, n.bit_length() - 1):
+        held = (held.astype(F32) + exchange(held, n, 1 << bit).astype(F32)).astype(BF16)
     held, near_grad, returned = tie(held, near_grad, returned)
-    one, other = 1 << HALVED[1], 1 << HALVED[2]
     parts = [exchange(held, n, mask) for mask in (other, one, one | other)]
     grad_features = collect(n, slots, hubs, near_grad, spread, returned)
     held, grad_features = tie(jnp.concatenate([held] + parts, axis=0), grad_features)
@@ -653,7 +627,7 @@
         out_specs=VMEM,
         compiler_params=params(4 << 20),
         name="order",
-    )(held, exchange(held, n, 1 << HALVED[0]))
+    )(held, exchange(held, n, core))
     return (output, grad_features, grad_weight)
 
 

time: 68.9 us -> 67.2 us (0.975)
  Pallas kernels: 35.2 us -> 31 us
  starting transfers between devices: 19.3 us -> 21.7 us
    pallas_call x1 -> x0, Pallas kernels: 4.18 us -> none  [far_backward(): pl.pallas_call(functools.partial(far_backward_kernel, n, slots, hubs), ou...]
    ppermute x9 -> x11, starting transfers between devices: 8.66 us -> 11.8 us  [exchange(): return lax.ppermute(x, 'dom', [(i, i ^ mask) for i in range(n)])]
    pallas_call x1, Pallas kernels: 7.64 us -> 9.29 us  [forward(): pl.pallas_call(functools.partial(forward_kernel, n, slots, hubs), out_sha...]
    all_to_all x2, starting transfers between devices: 10.7 us -> 9.95 us  [all_to_all(): return lax.all_to_all(x, 'dom', split_axis=0, concat_axis=0, tiled=True)]
    ppermute x9 -> x11, waiting for transfers between devices: 9.05 us -> 9.23 us  [exchange(): return lax.ppermute(x, 'dom', [(i, i ^ mask) for i in range(n)])]
  transfers between devices with their start and end apart: 11 -> 13, of which waited for: 8 -> 6; matrix products, arithmetic and copies ran while one was open for 0% -> 0% of each run, Pallas kernels for 34% -> 26%
where the time goes in v4:
time: 67.2 us; the launch traced here: 66.8 us
  Pallas kernels  31 us (46%)
  starting transfers between devices  21.7 us (32%)
  waiting for transfers between devices  13.1 us (19%)
  between operations  0.8 us (1%)
    ppermute x11, starting transfers between devices, exchange(): return lax.ppermute(x, 'dom', [(i, i ^ mask) for i in range(n)])  11.8 us
    all_to_all x2, starting transfers between devices, all_to_all(): return lax.all_to_all(x, 'dom', split_axis=0, concat_axis=0, tiled=True)  9.95 us
    pallas_call x1, Pallas kernels, near_forward(): pl.pallas_call(functools.partial(near_forward_kernel, n, slots, hubs), ou...  9.29 us
    pallas_call x1, Pallas kernels, forward(): pl.pallas_call(functools.partial(forward_kernel, n, slots, hubs), out_sha...  9.29 us
    ppermute x11, waiting for transfers between devices, exchange(): return lax.ppermute(x, 'dom', [(i, i ^ mask) for i in range(n)])  9.23 us
    pallas_call x1, Pallas kernels, near_backward(): pl.pallas_call(near_backward_kernel, out_shape=pltpu.VMEM(grad_agg.shape,...  4.9 us
    all_to_all x2, waiting for transfers between devices, all_to_all(): return lax.all_to_all(x, 'dom', split_axis=0, concat_axis=0, tiled=True)  3.87 us
    pallas_call x1, Pallas kernels, collect(): pl.pallas_call(functools.partial(collect_kernel, n, slots, hubs), out_sha...  3.44 us
  transfers between devices with their start and end apart: 13, of which 6 were waited for; matrix products, arithmetic and copies ran while one was open for 0% of the time, Pallas kernels for 26%

profile of v4, /device:TPU:0, one launch (start us, length us, event | category | flops | bytes accessed | tf_op | source)
XLA Modules:
  0.0 66.8 jit_solution(8070364486056974781)
XLA Ops:
  0.6 3.0 %pack_rows.1 = bf16[32,48,128]{2,1,0:T(8,128)(2,1)} custom-call(s32[1,8,32]{2,1,0:T(8,128)} %bitcast.1, s32[1,32]{1,0:T(1,128)} %send_count_in.3, s32[4]{0:T(128)} %hub_rows_in.3, bf16[2048,512]{1,0:T(8,128)(2,1)} %feats_in.3), custom_call_target="tpu_custom_call" | custom-call | tf_op jit(solution)/shard_map/pack_rows/pallas_call | solution.py:129
  3.6 7.3 %all-to-all-start = ((bf16[32,48,128]{2,1,0:T(8,128)(2,1)}), bf16[32,48,128]{2,1,0:T(8,128)(2,1)S(1)}, u32[]{:S(2)}, u32[]{:S(2)}) async-start(bf16[32,48,128]{2,1,0:T(8,128)(2,1)} %pack_rows.1), calls=%async_computation | async-start | bytes 786432 | tf_op jit(solution)/shard_map/all_to_all | solution.py:586
  11.0 9.3 %near_forward.1 = (f32[2048,512]{1,0:T(8,128)}, s32[384]{0:T(512)}, bf16[2048,384]{1,0:T(8,128)(2,1)}) custom-call(s32[96]{0:T(128)} %tile_rows_in.5, s32[96]{0:T(128)} %tile_cols_in.3, s32[1,8,32]{2,1,0:T(8,128)} %bitcast.2, s32[1,32]{1,0:T(1,128)} %send_count_in.3, s32[4]{0:T(128)} %hub_rows_in.3, bf16[96,128,128]{2,1,0:T(8,128)(2,1)S(1)} %copy-done, ...), custom_call_target="tpu_custom_call" | custom-call | flops 4294967296 | bytes 8388608 | tf_op jit(solution)/shard_map/near_forward/pallas_call | solution.py:277
  20.3 3.9 %all-to-all-done.received = bf16[32,48,128]{2,1,0:T(8,128)(2,1)S(1)} async-done(((bf16[32,48,128]{2,1,0:T(8,128)(2,1)}), bf16[32,48,128]{2,1,0:T(8,128)(2,1)S(1)}, u32[]{:S(2)}, u32[]{:S(2)}) %all-to-all-start) | async-done | bytes 393248 | tf_op jit(solution)/shard_map/all_to_all | solution.py:586
  24.1 9.3 %forward.1 = (bf16[2048,512]{1,0:T(8,128)(2,1)}, bf16[2048,512]{1,0:T(8,128)(2,1)}, bf16[32,48,128]{2,1,0:T(8,128)(2,1)}, f32[256,512]{1,0:T(8,128)S(1)}, bf16[256,512]{1,0:T(8,128)(2,1)S(1)}) custom-call(s32[96]{0:T(128)} %tile_rows_in.5, s32[96]{0:T(128)} %tile_cols_in.3, s32[384]{0:T(512)} %get-tuple-element.24.plan_in, ...), custom_call_target="tpu_custom_call" | custom-call | flops 8589934592 | bytes 16777216 | tf_op jit(solution)/shard_map/forward/pallas_call | solution.py:444
  33.5 1.5 %collective-permute-done = bf16[256,512]{1,0:T(8,128)(2,1)S(1)} collective-permute-done((bf16[256,512]{1,0:T(8,128)(2,1)S(1)}, bf16[256,512]{1,0:T(8,128)(2,1)S(1)}, u32[]{:S(2)}, u32[]{:S(2)}) %collective-permute-start) | collective-permute-done | bytes 262176 | tf_op jit(solution)/shard_map/ppermute | solution.py:578
  35.0 0.1 add_convert_fusion
  35.1 2.7 %all-to-all-start.1 = ((bf16[32,48,128]{2,1,0:T(8,128)(2,1)}), bf16[32,48,128]{2,1,0:T(8,128)(2,1)S(1)}, u32[]{:S(2)}, u32[]{:S(2)}) async-start(bf16[32,48,128]{2,1,0:T(8,128)(2,1)} %get-tuple-element.38), calls=%async_computation.1 | async-start | bytes 786432 | tf_op jit(solution)/shard_map/all_to_all | solution.py:586
  37.8 1.8 %collective-permute-start.1 = (bf16[64,512]{1,0:T(8,128)(2,1)S(1)}, bf16[64,512]{1,0:T(8,128)(2,1)S(1)}, u32[]{:S(2)}, u32[]{:S(2)}) collective-permute-start(bf16[64,512]{1,0:T(8,128)(2,1)S(1)} %get-tuple-element.32), channel_id=1, source_target_pairs={{0,2},{1,3},{2,0},{3,1},{4,6},{5,7},{6,4},{7,5},{8,10},{9,11},{10,... | collective-permute-start | bytes 196616 | tf_op jit(solution)/shard_map/ppermute | solution.py:578
  39.6 1.5 %collective-permute-start.2 = (bf16[64,512]{1,0:T(8,128)(2,1)S(1)}, bf16[64,512]{1,0:T(8,128)(2,1)S(1)}, u32[]{:S(2)}, u32[]{:S(2)}) collective-permute-start(bf16[64,512]{1,0:T(8,128)(2,1)S(1)} %get-tuple-element.33), channel_id=1, source_target_pairs={{0,4},{1,5},{2,6},{3,7},{4,0},{5,1},{6,2},{7,3},{8,12},{9,13},{10,... | collective-permute-start | bytes 196616 | tf_op jit(solution)/shard_map/ppermute | solution.py:578
  41.1 0.3 collective-permute-start.3
  41.4 4.9 %near_backward.1.near = bf16[2048,512]{1,0:T(8,128)(2,1)S(1)} custom-call(s32[96]{0:T(128)} %tile_rows_in.5, s32[384]{0:T(512)} %get-tuple-element.24.plan_in, bf16[96,128,128]{2,1,0:T(8,128)(2,1)} %tiles_in.1, bf16[2048,512]{1,0:T(8,128)(2,1)} %get-tuple-element.35.grad_agg_in), custom_call_target="tpu_custom_call" | custom-call | tf_op jit(solution)/shard_map/near_backward/pallas_call | solution.py:496
  46.3 1.3 %collective-permute-done.3 = bf16[64,512]{1,0:T(8,128)(2,1)S(1)} collective-permute-done((bf16[64,512]{1,0:T(8,128)(2,1)S(1)}, bf16[64,512]{1,0:T(8,128)(2,1)S(1)}, u32[]{:S(2)}, u32[]{:S(2)}) %collective-permute-start.3) | collective-permute-done | bytes 65568 | tf_op jit(solution)/shard_map/ppermute | solution.py:578
  47.6 3.9 %collective-permute-start.6 = (bf16[64,512]{1,0:T(8,128)(2,1)S(1)}, bf16[64,512]{1,0:T(8,128)(2,1)S(1)}, u32[]{:S(2)}, u32[]{:S(2)}) collective-permute-start(bf16[64,512]{1,0:T(8,128)(2,1)S(1)} %add_convert_fusion.2), channel_id=1, source_target_pairs={{0,24},{1,25},{2,26},{3,27},{4,28},{5,29},{6,30},{7,31},{8,16},{9,... | collective-permute-start | bytes 196616 | tf_op jit(solution)/shard_map/ppermute | solution.py:578
  51.5 0.6 collective-permute-start.4
  52.2 2.3 %collective-permute-done.6 = bf16[64,512]{1,0:T(8,128)(2,1)S(1)} collective-permute-done((bf16[64,512]{1,0:T(8,128)(2,1)S(1)}, bf16[64,512]{1,0:T(8,128)(2,1)S(1)}, u32[]{:S(2)}, u32[]{:S(2)}) %collective-permute-start.6) | collective-permute-done | bytes 65568 | tf_op jit(solution)/shard_map/ppermute | solution.py:578
  54.4 2.6 %collective-permute-done.5 = bf16[64,512]{1,0:T(8,128)(2,1)S(1)} collective-permute-done((bf16[64,512]{1,0:T(8,128)(2,1)S(1)}, bf16[64,512]{1,0:T(8,128)(2,1)S(1)}, u32[]{:S(2)}, u32[]{:S(2)}) %collective-permute-start.5) | collective-permute-done | bytes 65568 | tf_op jit(solution)/shard_map/ppermute | solution.py:578
  57.1 1.0 %collective-permute-start.9 = (bf16[64,512]{1,0:T(8,128)(2,1)S(1)}, bf16[64,512]{1,0:T(8,128)(2,1)S(1)}, u32[]{:S(2)}, u32[]{:S(2)}) collective-permute-start(bf16[64,512]{1,0:T(8,128)(2,1)S(1)} %add_convert_fusion.1), channel_id=1, source_target_pairs={{0,6},{1,7},{2,4},{3,5},{4,2},{5,3},{6,0},{7,1},{8,14},{9,15},{10,... | collective-permute-start | bytes 196616 | tf_op jit(solution)/shard_map/ppermute | solution.py:578
  58.1 1.1 %collective-permute-start.8 = (bf16[64,512]{1,0:T(8,128)(2,1)S(1)}, bf16[64,512]{1,0:T(8,128)(2,1)S(1)}, u32[]{:S(2)}, u32[]{:S(2)}) collective-permute-start(bf16[64,512]{1,0:T(8,128)(2,1)S(1)} %add_convert_fusion.1), channel_id=1, source_target_pairs={{0,4},{1,5},{2,6},{3,7},{4,0},{5,1},{6,2},{7,3},{8,12},{9,13},{10,... | collective-permute-start | bytes 196616 | tf_op jit(solution)/shard_map/ppermute | solution.py:578
  59.3 1.4 %collective-permute-start.7 = (bf16[64,512]{1,0:T(8,128)(2,1)S(1)}, bf16[64,512]{1,0:T(8,128)(2,1)S(1)}, u32[]{:S(2)}, u32[]{:S(2)}) collective-permute-start(bf16[64,512]{1,0:T(8,128)(2,1)S(1)} %add_convert_fusion.1), channel_id=1, source_target_pairs={{0,2},{1,3},{2,0},{3,1},{4,6},{5,7},{6,4},{7,5},{8,10},{9,11},{10,... | collective-permute-start | bytes 196616 | tf_op jit(solution)/shard_map/ppermute | solution.py:578
  60.6 3.4 %collect.1 = bf16[2048,512]{1,0:T(8,128)(2,1)} custom-call(bf16[2048,512]{1,0:T(8,128)(2,1)S(1)} %near_backward.1.near, bf16[2048,384]{1,0:T(8,128)(2,1)} %get-tuple-element.41.spread_in, bf16[32,48,128]{2,1,0:T(8,128)(2,1)S(1)} %all-to-all-done.1.returned), custom_call_target="tpu_custom_call" | custom-call | flops 34359738368 | bytes 8388608 | tf_op jit(solution)/shard_map/collect/pallas_call | solution.py:549
  64.1 0.1 collective-permute-start.10
  64.2 1.5 %collective-permute-done.10.second = bf16[256,512]{1,0:T(8,128)(2,1)S(1)} collective-permute-done((bf16[256,512]{1,0:T(8,128)(2,1)S(1)}, bf16[256,512]{1,0:T(8,128)(2,1)S(1)}, u32[]{:S(2)}, u32[]{:S(2)}) %collective-permute-start.10) | collective-permute-done | bytes 262176 | tf_op jit(solution)/shard_map/ppermute | solution.py:578
  65.7 1.0 %order.1 = f32[512,512]{1,0:T(8,128)} custom-call(bf16[256,512]{1,0:T(8,128)(2,1)S(1)} %pad_maximum_fusion.first, bf16[256,512]{1,0:T(8,128)(2,1)S(1)} %collective-permute-done.10.second), custom_call_target="tpu_custom_call" | custom-call | tf_op jit(solution)/shard_map/order/pallas_call | solution.py:623
  (15 shorter events, 0.2 us)
Async XLA Ops:
  0.6 10.3 %copy-start = (bf16[96,128,128]{2,1,0:T(8,128)(2,1)S(1)}, bf16[96,128,128]{2,1,0:T(8,128)(2,1)}, u32[]{:S(2)}) copy-start(bf16[96,128,128]{2,1,0:T(8,128)(2,1)} %tiles_in.1) | copy-start | bytes 9437188
  3.6 20.5 %all-to-all-start = ((bf16[32,48,128]{2,1,0:T(8,128)(2,1)}), bf16[32,48,128]{2,1,0:T(8,128)(2,1)S(1)}, u32[]{:S(2)}, u32[]{:S(2)}) async-start(bf16[32,48,128]{2,1,0:T(8,128)(2,1)} %pack_rows.1), calls=%async_computation | async-start | bytes 786432 | tf_op jit(solution)/shard_map/all_to_all | solution.py:586
  33.4 1.6 %collective-permute-start = (bf16[256,512]{1,0:T(8,128)(2,1)S(1)}, bf16[256,512]{1,0:T(8,128)(2,1)S(1)}, u32[]{:S(2)}, u32[]{:S(2)}) collective-permute-start(bf16[256,512]{1,0:T(8,128)(2,1)S(1)} %get-tuple-element.28), channel_id=1, source_target_pairs={{0,1},{1,0},{2,3},{3,2},{4,5},{5,4},{6,7},{7,6},{8,9},{9,8},{10,11... | collective-permute-start | bytes 786440 | tf_op jit(solution)/shard_map/ppermute | solution.py:578
  35.1 21.9 %all-to-all-start.1 = ((bf16[32,48,128]{2,1,0:T(8,128)(2,1)}), bf16[32,48,128]{2,1,0:T(8,128)(2,1)S(1)}, u32[]{:S(2)}, u32[]{:S(2)}) async-start(bf16[32,48,128]{2,1,0:T(8,128)(2,1)} %get-tuple-element.38), calls=%async_computation.1 | async-start | bytes 786432 | tf_op jit(solution)/shard_map/all_to_all | solution.py:586
  37.8 8.5 %collective-permute-start.1 = (bf16[64,512]{1,0:T(8,128)(2,1)S(1)}, bf16[64,512]{1,0:T(8,128)(2,1)S(1)}, u32[]{:S(2)}, u32[]{:S(2)}) collective-permute-start(bf16[64,512]{1,0:T(8,128)(2,1)S(1)} %get-tuple-element.32), channel_id=1, source_target_pairs={{0,2},{1,3},{2,0},{3,1},{4,6},{5,7},{6,4},{7,5},{8,10},{9,11},{10,... | collective-permute-start | bytes 196616 | tf_op jit(solution)/shard_map/ppermute | solution.py:578
  39.6 6.6 %collective-permute-start.2 = (bf16[64,512]{1,0:T(8,128)(2,1)S(1)}, bf16[64,512]{1,0:T(8,128)(2,1)S(1)}, u32[]{:S(2)}, u32[]{:S(2)}) collective-permute-start(bf16[64,512]{1,0:T(8,128)(2,1)S(1)} %get-tuple-element.33), channel_id=1, source_target_pairs={{0,4},{1,5},{2,6},{3,7},{4,0},{5,1},{6,2},{7,3},{8,12},{9,13},{10,... | collective-permute-start | bytes 196616 | tf_op jit(solution)/shard_map/ppermute | solution.py:578
  41.1 6.5 %collective-permute-start.3 = (bf16[64,512]{1,0:T(8,128)(2,1)S(1)}, bf16[64,512]{1,0:T(8,128)(2,1)S(1)}, u32[]{:S(2)}, u32[]{:S(2)}) collective-permute-start(bf16[64,512]{1,0:T(8,128)(2,1)S(1)} %get-tuple-element.34), channel_id=1, source_target_pairs={{0,6},{1,7},{2,4},{3,5},{4,2},{5,3},{6,0},{7,1},{8,14},{9,15},{10,... | collective-permute-start | bytes 196616 | tf_op jit(solution)/shard_map/ppermute | solution.py:578
  47.6 6.8 %collective-permute-start.6 = (bf16[64,512]{1,0:T(8,128)(2,1)S(1)}, bf16[64,512]{1,0:T(8,128)(2,1)S(1)}, u32[]{:S(2)}, u32[]{:S(2)}) collective-permute-start(bf16[64,512]{1,0:T(8,128)(2,1)S(1)} %add_convert_fusion.2), channel_id=1, source_target_pairs={{0,24},{1,25},{2,26},{3,27},{4,28},{5,29},{6,30},{7,31},{8,16},{9,... | collective-permute-start | bytes 196616 | tf_op jit(solution)/shard_map/ppermute | solution.py:578
  51.5 5.5 %collective-permute-start.5 = (bf16[64,512]{1,0:T(8,128)(2,1)S(1)}, bf16[64,512]{1,0:T(8,128)(2,1)S(1)}, u32[]{:S(2)}, u32[]{:S(2)}) collective-permute-start(bf16[64,512]{1,0:T(8,128)(2,1)S(1)} %add_convert_fusion.2), channel_id=1, source_target_pairs={{0,16},{1,17},{2,18},{3,19},{4,20},{5,21},{6,22},{7,23},{8,24},{9,... | collective-permute-start | bytes 196616 | tf_op jit(solution)/shard_map/ppermute | solution.py:578
  51.5 5.5 %collective-permute-start.4 = (bf16[64,512]{1,0:T(8,128)(2,1)S(1)}, bf16[64,512]{1,0:T(8,128)(2,1)S(1)}, u32[]{:S(2)}, u32[]{:S(2)}) collective-permute-start(bf16[64,512]{1,0:T(8,128)(2,1)S(1)} %add_convert_fusion.2), channel_id=1, source_target_pairs={{0,8},{1,9},{2,10},{3,11},{4,12},{5,13},{6,14},{7,15},{8,0},{9,1},... | collective-permute-start | bytes 196616 | tf_op jit(solution)/shard_map/ppermute | solution.py:578
  57.1 7.0 %collective-permute-start.9 = (bf16[64,512]{1,0:T(8,128)(2,1)S(1)}, bf16[64,512]{1,0:T(8,128)(2,1)S(1)}, u32[]{:S(2)}, u32[]{:S(2)}) collective-permute-start(bf16[64,512]{1,0:T(8,128)(2,1)S(1)} %add_convert_fusion.1), channel_id=1, source_target_pairs={{0,6},{1,7},{2,4},{3,5},{4,2},{5,3},{6,0},{7,1},{8,14},{9,15},{10,... | collective-permute-start | bytes 196616 | tf_op jit(solution)/shard_map/ppermute | solution.py:578
  58.1 6.0 %collective-permute-start.8 = (bf16[64,512]{1,0:T(8,128)(2,1)S(1)}, bf16[64,512]{1,0:T(8,128)(2,1)S(1)}, u32[]{:S(2)}, u32[]{:S(2)}) collective-permute-start(bf16[64,512]{1,0:T(8,128)(2,1)S(1)} %add_convert_fusion.1), channel_id=1, source_target_pairs={{0,4},{1,5},{2,6},{3,7},{4,0},{5,1},{6,2},{7,3},{8,12},{9,13},{10,... | collective-permute-start | bytes 196616 | tf_op jit(solution)/shard_map/ppermute | solution.py:578
  59.3 4.8 %collective-permute-start.7 = (bf16[64,512]{1,0:T(8,128)(2,1)S(1)}, bf16[64,512]{1,0:T(8,128)(2,1)S(1)}, u32[]{:S(2)}, u32[]{:S(2)}) collective-permute-start(bf16[64,512]{1,0:T(8,128)(2,1)S(1)} %add_convert_fusion.1), channel_id=1, source_target_pairs={{0,2},{1,3},{2,0},{3,1},{4,6},{5,7},{6,4},{7,5},{8,10},{9,11},{10,... | collective-permute-start | bytes 196616 | tf_op jit(solution)/shard_map/ppermute | solution.py:578
  64.1 1.6 %collective-permute-start.10 = (bf16[256,512]{1,0:T(8,128)(2,1)S(1)}, bf16[256,512]{1,0:T(8,128)(2,1)S(1)}, u32[]{:S(2)}, u32[]{:S(2)}) collective-permute-start(bf16[256,512]{1,0:T(8,128)(2,1)S(1)} %pad_maximum_fusion.first), channel_id=1, source_target_pairs={{0,1},{1,0},{2,3},{3,2},{4,5},{5,4},{6,7},{7,6},{8,9},{9,8},{10,11... | collective-permute-start | bytes 786440 | tf_op jit(solution)/shard_map/ppermute | solution.py:578

commit v5 on v4

--- a/solution.py
+++ b/solution.py
@@ -243,7 +243,7 @@
 def near_forward_kernel(
     n, slots, hubs, tile_rows_in, tile_cols_in, send_rows_in, send_count_in, hub_rows_in, tiles, feats_in,
     near_out, plan_out, spread_out,
-    tile_rows, tile_cols, send_rows, send_count, hub_rows, feats, total, spread, plan, waiting, sems,
+    tile_rows, tile_cols, send_rows, send_count, hub_rows, feats, total, rounded, spread, plan, waiting, sems,
 ):
     rows, width = feats.shape
     blocks = rows // tiles.shape[1]
@@ -264,7 +264,8 @@
     for copy in copies[2:]:
         copy.wait()
     run_plan(NEAR_FWD, plan, tiles, lambda t: jnp.minimum(tile_cols[t], blocks - 1), feats, total, False)
-    sent.append(start(total, near_out, sems.at[1]))
+    rounded[...] = total[...].astype(BF16)
+    sent.append(start(rounded, near_out, sems.at[1]))
     make_spread(n, slots, hubs, width // LANES, send_rows, send_count, hub_rows, spread)
     sent.append(start(spread, spread_out, sems.at[2]))
     for copy in sent:
@@ -277,7 +278,7 @@
     return pl.pallas_call(
         functools.partial(near_forward_kernel, n, slots, hubs),
         out_shape=(
-            pltpu.HBM((rows, width), F32),
+            pltpu.HBM((rows, width), BF16),
             pltpu.HBM((PLAN,), I32),
             pltpu.HBM((rows, n * slots + LANES), BF16),
         ),
@@ -291,6 +292,7 @@
             pltpu.SMEM(hub_rows.shape, I32),
             pltpu.VMEM((rows, width), BF16),
             pltpu.VMEM((rows, width), F32),
+            pltpu.VMEM((rows, width), BF16),
             pltpu.VMEM((rows, n * slots + LANES), BF16),
             pltpu.SMEM((PLAN,), I32),
             pltpu.SMEM((4 * KEYS,), I32),
@@ -393,7 +395,7 @@
                 copy.wait()
 
     def first(at):
-        here = (total[at, :] + near[at, :]).astype(BF16)
+        here = (total[at, :] + near[at, :].astype(F32)).astype(BF16)
         agg[at, :] = here
         return jnp.dot(here, weight[...], preferred_element_type=F32)
 
@@ -460,7 +462,7 @@
             pltpu.VMEM((rows, width), F32),
             pltpu.VMEM((n * (slots + hubs), width), F32),
             pltpu.VMEM(packed, BF16),
-            pltpu.VMEM((rows, width), F32),
+            pltpu.VMEM((rows, width), BF16),
             pltpu.VMEM((width, width), BF16),
             pltpu.VMEM((rows, width), BF16),
             pltpu.VMEM((rows, width), BF16),

time: 67.2 us -> 66.6 us (level)
  transfers between devices with their start and end apart: 13 -> 13, of which waited for: 6 -> 6; matrix products, arithmetic and copies ran while one was open for 0% -> 0% of each run, Pallas kernels for 26% -> 27%
where the time goes in v5:
time: 66.6 us; the launch traced here: 66.3 us
  Pallas kernels  30.6 us (46%)
  starting transfers between devices  21.7 us (33%)
  waiting for transfers between devices  12.9 us (19%)
  between operations  0.8 us (1%)
    ppermute x11, starting transfers between devices, exchange(): return lax.ppermute(x, 'dom', [(i, i ^ mask) for i in range(n)])  11.8 us
    all_to_all x2, starting transfers between devices, all_to_all(): return lax.all_to_all(x, 'dom', split_axis=0, concat_axis=0, tiled=True)  9.95 us
    pallas_call x1, Pallas kernels, near_forward(): pl.pallas_call(functools.partial(near_forward_kernel, n, slots, hubs), ou...  9.45 us
    ppermute x11, waiting for transfers between devices, exchange(): return lax.ppermute(x, 'dom', [(i, i ^ mask) for i in range(n)])  9.22 us
    pallas_call x1, Pallas kernels, forward(): pl.pallas_call(functools.partial(forward_kernel, n, slots, hubs), out_sha...  8.78 us
    pallas_call x1, Pallas kernels, near_backward(): pl.pallas_call(near_backward_kernel, out_shape=pltpu.VMEM(grad_agg.shape,...  4.91 us
    all_to_all x2, waiting for transfers between devices, all_to_all(): return lax.all_to_all(x, 'dom', split_axis=0, concat_axis=0, tiled=True)  3.71 us
    pallas_call x1, Pallas kernels, collect(): pl.pallas_call(functools.partial(collect_kernel, n, slots, hubs), out_sha...  3.44 us
  transfers between devices with their start and end apart: 13, of which 6 were waited for; matrix products, arithmetic and copies ran while one was open for 0% of the time, Pallas kernels for 27%

profile of v5, /device:TPU:0, one launch (start us, length us, event | category | flops | bytes accessed | tf_op | source)
XLA Modules:
  0.0 66.3 jit_solution(15767355822038102427)
XLA Ops:
  0.6 3.0 %pack_rows.1 = bf16[32,48,128]{2,1,0:T(8,128)(2,1)} custom-call(s32[1,8,32]{2,1,0:T(8,128)} %bitcast.1, s32[1,32]{1,0:T(1,128)} %send_count_in.3, s32[4]{0:T(128)} %hub_rows_in.3, bf16[2048,512]{1,0:T(8,128)(2,1)} %feats_in.3), custom_call_target="tpu_custom_call" | custom-call | tf_op jit(solution)/shard_map/pack_rows/pallas_call | solution.py:129
  3.6 7.3 %all-to-all-start = ((bf16[32,48,128]{2,1,0:T(8,128)(2,1)}), bf16[32,48,128]{2,1,0:T(8,128)(2,1)S(1)}, u32[]{:S(2)}, u32[]{:S(2)}) async-start(bf16[32,48,128]{2,1,0:T(8,128)(2,1)} %pack_rows.1), calls=%async_computation | async-start | bytes 786432 | tf_op jit(solution)/shard_map/all_to_all | solution.py:588
  11.0 9.5 %near_forward.1 = (bf16[2048,512]{1,0:T(8,128)(2,1)}, s32[384]{0:T(512)}, bf16[2048,384]{1,0:T(8,128)(2,1)}) custom-call(s32[96]{0:T(128)} %tile_rows_in.5, s32[96]{0:T(128)} %tile_cols_in.3, s32[1,8,32]{2,1,0:T(8,128)} %bitcast.2, s32[1,32]{1,0:T(1,128)} %send_count_in.3, s32[4]{0:T(128)} %hub_rows_in.3, bf16[96,128,128]{2,1,0:T(8,128)(2,1)S(1)} %copy-done, ...), custom_call_target="tpu_custom_call" | custom-call | flops 4294967296 | bytes 8388608 | tf_op jit(solution)/shard_map/near_forward/pallas_call | solution.py:278
  20.4 3.7 %all-to-all-done.received = bf16[32,48,128]{2,1,0:T(8,128)(2,1)S(1)} async-done(((bf16[32,48,128]{2,1,0:T(8,128)(2,1)}), bf16[32,48,128]{2,1,0:T(8,128)(2,1)S(1)}, u32[]{:S(2)}, u32[]{:S(2)}) %all-to-all-start) | async-done | bytes 393248 | tf_op jit(solution)/shard_map/all_to_all | solution.py:588
  24.1 8.8 %forward.1 = (bf16[2048,512]{1,0:T(8,128)(2,1)}, bf16[2048,512]{1,0:T(8,128)(2,1)}, bf16[32,48,128]{2,1,0:T(8,128)(2,1)}, f32[256,512]{1,0:T(8,128)S(1)}, bf16[256,512]{1,0:T(8,128)(2,1)S(1)}) custom-call(s32[96]{0:T(128)} %tile_rows_in.5, s32[96]{0:T(128)} %tile_cols_in.3, s32[384]{0:T(512)} %get-tuple-element.24.plan_in, ...), custom_call_target="tpu_custom_call" | custom-call | flops 8589934592 | bytes 16777216 | tf_op jit(solution)/shard_map/forward/pallas_call | solution.py:446
  32.9 0.1 collective-permute-start
  33.0 1.5 %collective-permute-done = bf16[256,512]{1,0:T(8,128)(2,1)S(1)} collective-permute-done((bf16[256,512]{1,0:T(8,128)(2,1)S(1)}, bf16[256,512]{1,0:T(8,128)(2,1)S(1)}, u32[]{:S(2)}, u32[]{:S(2)}) %collective-permute-start) | collective-permute-done | bytes 262176 | tf_op jit(solution)/shard_map/ppermute | solution.py:580
  34.5 0.1 add_convert_fusion
  34.6 2.6 %all-to-all-start.1 = ((bf16[32,48,128]{2,1,0:T(8,128)(2,1)}), bf16[32,48,128]{2,1,0:T(8,128)(2,1)S(1)}, u32[]{:S(2)}, u32[]{:S(2)}) async-start(bf16[32,48,128]{2,1,0:T(8,128)(2,1)} %get-tuple-element.38), calls=%async_computation.1 | async-start | bytes 786432 | tf_op jit(solution)/shard_map/all_to_all | solution.py:588
  37.3 1.8 %collective-permute-start.1 = (bf16[64,512]{1,0:T(8,128)(2,1)S(1)}, bf16[64,512]{1,0:T(8,128)(2,1)S(1)}, u32[]{:S(2)}, u32[]{:S(2)}) collective-permute-start(bf16[64,512]{1,0:T(8,128)(2,1)S(1)} %get-tuple-element.32), channel_id=1, source_target_pairs={{0,2},{1,3},{2,0},{3,1},{4,6},{5,7},{6,4},{7,5},{8,10},{9,11},{10,... | collective-permute-start | bytes 196616 | tf_op jit(solution)/shard_map/ppermute | solution.py:580
  39.1 1.5 %collective-permute-start.2 = (bf16[64,512]{1,0:T(8,128)(2,1)S(1)}, bf16[64,512]{1,0:T(8,128)(2,1)S(1)}, u32[]{:S(2)}, u32[]{:S(2)}) collective-permute-start(bf16[64,512]{1,0:T(8,128)(2,1)S(1)} %get-tuple-element.33), channel_id=1, source_target_pairs={{0,4},{1,5},{2,6},{3,7},{4,0},{5,1},{6,2},{7,3},{8,12},{9,13},{10,... | collective-permute-start | bytes 196616 | tf_op jit(solution)/shard_map/ppermute | solution.py:580
  40.6 0.3 collective-permute-start.3
  40.8 4.9 %near_backward.1.near = bf16[2048,512]{1,0:T(8,128)(2,1)S(1)} custom-call(s32[96]{0:T(128)} %tile_rows_in.5, s32[384]{0:T(512)} %get-tuple-element.24.plan_in, bf16[96,128,128]{2,1,0:T(8,128)(2,1)} %tiles_in.1, bf16[2048,512]{1,0:T(8,128)(2,1)} %get-tuple-element.35.grad_agg_in), custom_call_target="tpu_custom_call" | custom-call | tf_op jit(solution)/shard_map/near_backward/pallas_call | solution.py:498
  45.8 1.3 %collective-permute-done.3 = bf16[64,512]{1,0:T(8,128)(2,1)S(1)} collective-permute-done((bf16[64,512]{1,0:T(8,128)(2,1)S(1)}, bf16[64,512]{1,0:T(8,128)(2,1)S(1)}, u32[]{:S(2)}, u32[]{:S(2)}) %collective-permute-start.3) | collective-permute-done | bytes 65568 | tf_op jit(solution)/shard_map/ppermute | solution.py:580
  47.1 3.9 %collective-permute-start.6 = (bf16[64,512]{1,0:T(8,128)(2,1)S(1)}, bf16[64,512]{1,0:T(8,128)(2,1)S(1)}, u32[]{:S(2)}, u32[]{:S(2)}) collective-permute-start(bf16[64,512]{1,0:T(8,128)(2,1)S(1)} %add_convert_fusion.2), channel_id=1, source_target_pairs={{0,24},{1,25},{2,26},{3,27},{4,28},{5,29},{6,30},{7,31},{8,16},{9,... | collective-permute-start | bytes 196616 | tf_op jit(solution)/shard_map/ppermute | solution.py:580
  51.0 0.6 collective-permute-start.4
  51.7 2.3 %collective-permute-done.6 = bf16[64,512]{1,0:T(8,128)(2,1)S(1)} collective-permute-done((bf16[64,512]{1,0:T(8,128)(2,1)S(1)}, bf16[64,512]{1,0:T(8,128)(2,1)S(1)}, u32[]{:S(2)}, u32[]{:S(2)}) %collective-permute-start.6) | collective-permute-done | bytes 65568 | tf_op jit(solution)/shard_map/ppermute | solution.py:580
  53.9 2.6 %collective-permute-done.5 = bf16[64,512]{1,0:T(8,128)(2,1)S(1)} collective-permute-done((bf16[64,512]{1,0:T(8,128)(2,1)S(1)}, bf16[64,512]{1,0:T(8,128)(2,1)S(1)}, u32[]{:S(2)}, u32[]{:S(2)}) %collective-permute-start.5) | collective-permute-done | bytes 65568 | tf_op jit(solution)/shard_map/ppermute | solution.py:580
  56.6 1.0 %collective-permute-start.9 = (bf16[64,512]{1,0:T(8,128)(2,1)S(1)}, bf16[64,512]{1,0:T(8,128)(2,1)S(1)}, u32[]{:S(2)}, u32[]{:S(2)}) collective-permute-start(bf16[64,512]{1,0:T(8,128)(2,1)S(1)} %add_convert_fusion.1), channel_id=1, source_target_pairs={{0,6},{1,7},{2,4},{3,5},{4,2},{5,3},{6,0},{7,1},{8,14},{9,15},{10,... | collective-permute-start | bytes 196616 | tf_op jit(solution)/shard_map/ppermute | solution.py:580
  57.6 1.1 %collective-permute-start.8 = (bf16[64,512]{1,0:T(8,128)(2,1)S(1)}, bf16[64,512]{1,0:T(8,128)(2,1)S(1)}, u32[]{:S(2)}, u32[]{:S(2)}) collective-permute-start(bf16[64,512]{1,0:T(8,128)(2,1)S(1)} %add_convert_fusion.1), channel_id=1, source_target_pairs={{0,4},{1,5},{2,6},{3,7},{4,0},{5,1},{6,2},{7,3},{8,12},{9,13},{10,... | collective-permute-start | bytes 196616 | tf_op jit(solution)/shard_map/ppermute | solution.py:580
  58.8 1.4 %collective-permute-start.7 = (bf16[64,512]{1,0:T(8,128)(2,1)S(1)}, bf16[64,512]{1,0:T(8,128)(2,1)S(1)}, u32[]{:S(2)}, u32[]{:S(2)}) collective-permute-start(bf16[64,512]{1,0:T(8,128)(2,1)S(1)} %add_convert_fusion.1), channel_id=1, source_target_pairs={{0,2},{1,3},{2,0},{3,1},{4,6},{5,7},{6,4},{7,5},{8,10},{9,11},{10,... | collective-permute-start | bytes 196616 | tf_op jit(solution)/shard_map/ppermute | solution.py:580
  60.1 3.4 %collect.1 = bf16[2048,512]{1,0:T(8,128)(2,1)} custom-call(bf16[2048,512]{1,0:T(8,128)(2,1)S(1)} %near_backward.1.near, bf16[2048,384]{1,0:T(8,128)(2,1)} %get-tuple-element.41.spread_in, bf16[32,48,128]{2,1,0:T(8,128)(2,1)S(1)} %all-to-all-done.1.returned), custom_call_target="tpu_custom_call" | custom-call | flops 34359738368 | bytes 8388608 | tf_op jit(solution)/shard_map/collect/pallas_call | solution.py:551
  63.7 1.5 %collective-permute-done.10.second = bf16[256,512]{1,0:T(8,128)(2,1)S(1)} collective-permute-done((bf16[256,512]{1,0:T(8,128)(2,1)S(1)}, bf16[256,512]{1,0:T(8,128)(2,1)S(1)}, u32[]{:S(2)}, u32[]{:S(2)}) %collective-permute-start.10) | collective-permute-done | bytes 262176 | tf_op jit(solution)/shard_map/ppermute | solution.py:580
  65.2 1.0 %order.1 = f32[512,512]{1,0:T(8,128)} custom-call(bf16[256,512]{1,0:T(8,128)(2,1)S(1)} %pad_maximum_fusion.first, bf16[256,512]{1,0:T(8,128)(2,1)S(1)} %collective-permute-done.10.second), custom_call_target="tpu_custom_call" | custom-call | tf_op jit(solution)/shard_map/order/pallas_call | solution.py:625
  (15 shorter events, 0.2 us)
Async XLA Ops:
  0.6 10.3 %copy-start = (bf16[96,128,128]{2,1,0:T(8,128)(2,1)S(1)}, bf16[96,128,128]{2,1,0:T(8,128)(2,1)}, u32[]{:S(2)}) copy-start(bf16[96,128,128]{2,1,0:T(8,128)(2,1)} %tiles_in.1) | copy-start | bytes 9437188
  3.6 20.5 %all-to-all-start = ((bf16[32,48,128]{2,1,0:T(8,128)(2,1)}), bf16[32,48,128]{2,1,0:T(8,128)(2,1)S(1)}, u32[]{:S(2)}, u32[]{:S(2)}) async-start(bf16[32,48,128]{2,1,0:T(8,128)(2,1)} %pack_rows.1), calls=%async_computation | async-start | bytes 786432 | tf_op jit(solution)/shard_map/all_to_all | solution.py:588
  32.9 1.6 %collective-permute-start = (bf16[256,512]{1,0:T(8,128)(2,1)S(1)}, bf16[256,512]{1,0:T(8,128)(2,1)S(1)}, u32[]{:S(2)}, u32[]{:S(2)}) collective-permute-start(bf16[256,512]{1,0:T(8,128)(2,1)S(1)} %get-tuple-element.28), channel_id=1, source_target_pairs={{0,1},{1,0},{2,3},{3,2},{4,5},{5,4},{6,7},{7,6},{8,9},{9,8},{10,11... | collective-permute-start | bytes 786440 | tf_op jit(solution)/shard_map/ppermute | solution.py:580
  34.6 21.9 %all-to-all-start.1 = ((bf16[32,48,128]{2,1,0:T(8,128)(2,1)}), bf16[32,48,128]{2,1,0:T(8,128)(2,1)S(1)}, u32[]{:S(2)}, u32[]{:S(2)}) async-start(bf16[32,48,128]{2,1,0:T(8,128)(2,1)} %get-tuple-element.38), calls=%async_computation.1 | async-start | bytes 786432 | tf_op jit(solution)/shard_map/all_to_all | solution.py:588
  37.3 8.5 %collective-permute-start.1 = (bf16[64,512]{1,0:T(8,128)(2,1)S(1)}, bf16[64,512]{1,0:T(8,128)(2,1)S(1)}, u32[]{:S(2)}, u32[]{:S(2)}) collective-permute-start(bf16[64,512]{1,0:T(8,128)(2,1)S(1)} %get-tuple-element.32), channel_id=1, source_target_pairs={{0,2},{1,3},{2,0},{3,1},{4,6},{5,7},{6,4},{7,5},{8,10},{9,11},{10,... | collective-permute-start | bytes 196616 | tf_op jit(solution)/shard_map/ppermute | solution.py:580
  39.1 6.6 %collective-permute-start.2 = (bf16[64,512]{1,0:T(8,128)(2,1)S(1)}, bf16[64,512]{1,0:T(8,128)(2,1)S(1)}, u32[]{:S(2)}, u32[]{:S(2)}) collective-permute-start(bf16[64,512]{1,0:T(8,128)(2,1)S(1)} %get-tuple-element.33), channel_id=1, source_target_pairs={{0,4},{1,5},{2,6},{3,7},{4,0},{5,1},{6,2},{7,3},{8,12},{9,13},{10,... | collective-permute-start | bytes 196616 | tf_op jit(solution)/shard_map/ppermute | solution.py:580
  40.6 6.5 %collective-permute-start.3 = (bf16[64,512]{1,0:T(8,128)(2,1)S(1)}, bf16[64,512]{1,0:T(8,128)(2,1)S(1)}, u32[]{:S(2)}, u32[]{:S(2)}) collective-permute-start(bf16[64,512]{1,0:T(8,128)(2,1)S(1)} %get-tuple-element.34), channel_id=1, source_target_pairs={{0,6},{1,7},{2,4},{3,5},{4,2},{5,3},{6,0},{7,1},{8,14},{9,15},{10,... | collective-permute-start | bytes 196616 | tf_op jit(solution)/shard_map/ppermute | solution.py:580
  47.1 6.8 %collective-permute-start.6 = (bf16[64,512]{1,0:T(8,128)(2,1)S(1)}, bf16[64,512]{1,0:T(8,128)(2,1)S(1)}, u32[]{:S(2)}, u32[]{:S(2)}) collective-permute-start(bf16[64,512]{1,0:T(8,128)(2,1)S(1)} %add_convert_fusion.2), channel_id=1, source_target_pairs={{0,24},{1,25},{2,26},{3,27},{4,28},{5,29},{6,30},{7,31},{8,16},{9,... | collective-permute-start | bytes 196616 | tf_op jit(solution)/shard_map/ppermute | solution.py:580
  51.0 5.5 %collective-permute-start.5 = (bf16[64,512]{1,0:T(8,128)(2,1)S(1)}, bf16[64,512]{1,0:T(8,128)(2,1)S(1)}, u32[]{:S(2)}, u32[]{:S(2)}) collective-permute-start(bf16[64,512]{1,0:T(8,128)(2,1)S(1)} %add_convert_fusion.2), channel_id=1, source_target_pairs={{0,16},{1,17},{2,18},{3,19},{4,20},{5,21},{6,22},{7,23},{8,24},{9,... | collective-permute-start | bytes 196616 | tf_op jit(solution)/shard_map/ppermute | solution.py:580
  51.0 5.5 %collective-permute-start.4 = (bf16[64,512]{1,0:T(8,128)(2,1)S(1)}, bf16[64,512]{1,0:T(8,128)(2,1)S(1)}, u32[]{:S(2)}, u32[]{:S(2)}) collective-permute-start(bf16[64,512]{1,0:T(8,128)(2,1)S(1)} %add_convert_fusion.2), channel_id=1, source_target_pairs={{0,8},{1,9},{2,10},{3,11},{4,12},{5,13},{6,14},{7,15},{8,0},{9,1},... | collective-permute-start | bytes 196616 | tf_op jit(solution)/shard_map/ppermute | solution.py:580
  56.6 7.0 %collective-permute-start.9 = (bf16[64,512]{1,0:T(8,128)(2,1)S(1)}, bf16[64,512]{1,0:T(8,128)(2,1)S(1)}, u32[]{:S(2)}, u32[]{:S(2)}) collective-permute-start(bf16[64,512]{1,0:T(8,128)(2,1)S(1)} %add_convert_fusion.1), channel_id=1, source_target_pairs={{0,6},{1,7},{2,4},{3,5},{4,2},{5,3},{6,0},{7,1},{8,14},{9,15},{10,... | collective-permute-start | bytes 196616 | tf_op jit(solution)/shard_map/ppermute | solution.py:580
  57.6 6.0 %collective-permute-start.8 = (bf16[64,512]{1,0:T(8,128)(2,1)S(1)}, bf16[64,512]{1,0:T(8,128)(2,1)S(1)}, u32[]{:S(2)}, u32[]{:S(2)}) collective-permute-start(bf16[64,512]{1,0:T(8,128)(2,1)S(1)} %add_convert_fusion.1), channel_id=1, source_target_pairs={{0,4},{1,5},{2,6},{3,7},{4,0},{5,1},{6,2},{7,3},{8,12},{9,13},{10,... | collective-permute-start | bytes 196616 | tf_op jit(solution)/shard_map/ppermute | solution.py:580
  58.8 4.8 %collective-permute-start.7 = (bf16[64,512]{1,0:T(8,128)(2,1)S(1)}, bf16[64,512]{1,0:T(8,128)(2,1)S(1)}, u32[]{:S(2)}, u32[]{:S(2)}) collective-permute-start(bf16[64,512]{1,0:T(8,128)(2,1)S(1)} %add_convert_fusion.1), channel_id=1, source_target_pairs={{0,2},{1,3},{2,0},{3,1},{4,6},{5,7},{6,4},{7,5},{8,10},{9,11},{10,... | collective-permute-start | bytes 196616 | tf_op jit(solution)/shard_map/ppermute | solution.py:580
  63.6 1.6 %collective-permute-start.10 = (bf16[256,512]{1,0:T(8,128)(2,1)S(1)}, bf16[256,512]{1,0:T(8,128)(2,1)S(1)}, u32[]{:S(2)}, u32[]{:S(2)}) collective-permute-start(bf16[256,512]{1,0:T(8,128)(2,1)S(1)} %pad_maximum_fusion.first), channel_id=1, source_target_pairs={{0,1},{1,0},{2,3},{3,2},{4,5},{5,4},{6,7},{7,6},{8,9},{9,8},{10,11... | collective-permute-start | bytes 786440 | tf_op jit(solution)/shard_map/ppermute | solution.py:580
